TPU v7x, 32 devices: a whole 2x2x4 slice. The times are simulated.
32 devices in a mesh: grp: 8 (over z, core), fsdp: 4 (over y, x).
Axes of the slice: x: 2, y: 2, z: 4, core: 2. Of those that a mesh axis runs over, the one named last changes fastest.
Arguments:
- tokens: bfloat16 [8192, 2048], P(('grp', 'fsdp')), may hold values from -6 to 6
- cotangent: bfloat16 [8192, 2048], P(('grp', 'fsdp')), may hold values from -6 to 6
- segment: int32 [8192], P(('grp', 'fsdp')), may hold values from 0 to 55, as said below
- ancestry: int32 [8192, 3], P(('grp', 'fsdp')), may hold values from 0 to 55, as said below
- position: int32 [8192], P(('grp', 'fsdp')), may hold values from 0 to 767, as said below
- routes: int32 [8192, 4], P(('grp', 'fsdp')), may hold values from 0 to 7, all different within a row; in each aligned block of 256 rows (0 to 255, 256 to 511, ...) at most 160 rows name the same one
- attn_gain: bfloat16 [2048], P('fsdp'), may hold values from 0.5 to 1.5
- w_query: bfloat16 [2048, 2048], P('fsdp'), may hold values from -0.125 to 0.125
- w_key: bfloat16 [2048, 2048], P('fsdp'), may hold values from -0.125 to 0.125
- w_value: bfloat16 [2048, 2048], P('fsdp'), may hold values from -0.125 to 0.125
- b_query: bfloat16 [2048], P('fsdp'), may hold values from -1.75 to 1.75
- b_key: bfloat16 [2048], P('fsdp'), may hold values from -1.75 to 1.75
- b_value: bfloat16 [2048], P('fsdp'), may hold values from -1.75 to 1.75
- w_output: bfloat16 [2048, 2048], P('fsdp'), may hold values from -1 to 1
- moe_gain: bfloat16 [2048], P('fsdp'), may hold values from 0.5 to 1.5
- w_router: bfloat16 [2048, 8], P('fsdp'), may hold values from -0.0625 to 0.0625
- shared_switch: bfloat16 [2048], P('fsdp'), may hold values from -0.125 to 0.125
- shared_gate: bfloat16 [2048, 5632], P(None, 'fsdp'), may hold values from -0.125 to 0.125
- shared_up: bfloat16 [2048, 5632], P(None, 'fsdp'), may hold values from -0.125 to 0.125
- shared_down: bfloat16 [5632, 2048], P('fsdp'), may hold values from -0.21875 to 0.21875
- expert_gate: bfloat16 [8, 2048, 1408], P('fsdp'), may hold values from -0.125 to 0.125
- routed_up_weight: bfloat16 [8, 2048, 1408], P('fsdp'), may hold values from -0.125 to 0.125
- expert_down: bfloat16 [8, 1408, 2048], P('fsdp'), may hold values from -0.625 to 0.625
Outputs:
- output: bfloat16 [8192, 2048], P(('grp', 'fsdp'))
- grad_tokens: float32 [8192, 2048], P(('grp', 'fsdp'))
- grad_attn_gain: float32 [2048], P(('fsdp', 'grp'))
- grad_w_query: float32 [2048, 2048], P('fsdp', 'grp')
- grad_w_key: float32 [2048, 2048], P('fsdp', 'grp')
- grad_w_value: float32 [2048, 2048], P('fsdp', 'grp')
- grad_b_query: float32 [2048], P(('fsdp', 'grp'))
- grad_b_key: float32 [2048], P(('fsdp', 'grp'))
- grad_b_value: float32 [2048], P(('fsdp', 'grp'))
- grad_w_output: float32 [2048, 2048], P('fsdp', 'grp')
- grad_moe_gain: float32 [2048], P(('fsdp', 'grp'))
- grad_w_router: float32 [2048, 8], P(('fsdp', 'grp'))
- grad_shared_switch: float32 [2048], P(('fsdp', 'grp'))
- grad_shared_gate: float32 [2048, 5632], P('grp', 'fsdp')
- grad_shared_up: float32 [2048, 5632], P('grp', 'fsdp')
- grad_shared_down: float32 [5632, 2048], P('fsdp', 'grp')
- grad_expert_gate: float32 [8, 2048, 1408], P('fsdp', 'grp')
- grad_expert_up: float32 [8, 2048, 1408], P('fsdp', 'grp')
- grad_expert_down: float32 [8, 1408, 2048], P('fsdp', None, 'grp')
Inputs may be any that keep to these rules, and one draw needn't show every extreme that they name: Tokens 1024 * k to 1024 * (k + 1) - 1 form tree k, of seven segments in this order: a trunk of 512 tokens, a first branch, its two leaves, a second branch, its two leaves; segment = 7 k + the segment's place in that order. ancestry(t) lists the trunk, the branch and the leaf on t's path; where t is in the trunk or a branch, its own segment stands in the deeper places. position counts the tokens before t on its path: trunk, then the branch, then the leaf; in every tree the path through the first leaf has exactly 768 tokens, and no path has more. `routes`: in the rows of one device no expert is named by more than 160 rows.
All inputs are finite; a program needn't handle non-finite values.
Results may differ from a plain program's by a relative error of at most 0.03.
Values may be sent and summed in bfloat16 or wider, within the bound.
A program may use at most 448 MiB of HBM per device.

v0:
```python
import jax
import jax.numpy as jnp
from jax import lax
from jax.sharding import PartitionSpec as P

HEADS = 16
HEAD_DIM = 128


EPSILON = 1e-06
ROPE_BASE = 1000000.0
MASK_FILL = -1e30
EXACT_MATMUL = lax.Precision.HIGHEST


def contract_rows(left, right):
    return lax.dot_general(
        left, right, (((0,), (0,)), ((), ())), preferred_element_type=jnp.float32
    )


def precise_rows(left, right):
    return lax.dot_general(
        left,
        right,
        (((0,), (0,)), ((), ())),
        precision=EXACT_MATMUL,
        preferred_element_type=jnp.float32,
    )


def times_transposed(left, right):
    return lax.dot_general(
        left, right, (((1,), (1,)), ((), ())), preferred_element_type=jnp.float32
    )


def precise_transposed(left, right):
    return lax.dot_general(
        left,
        right,
        (((1,), (1,)), ((), ())),
        precision=EXACT_MATMUL,
        preferred_element_type=jnp.float32,
    )


def normalize(values, gain):
    factor = lax.rsqrt(jnp.mean(values * values, axis=-1, keepdims=True) + EPSILON)
    return (values * factor * gain, factor)


def norm_back(values, factor, gain, grad):
    weighted = gain * grad
    back = factor * weighted - values * factor**3 * jnp.mean(
        weighted * values, axis=-1, keepdims=True
    )
    return (back, jnp.sum(grad * values * factor, axis=0))


def silu_pair(value):
    sigma = jax.nn.sigmoid(value)
    return (value * sigma, sigma * (1.0 + value * (1.0 - sigma)))


def angles(position):
    halfway = HEAD_DIM // 2
    freqs = ROPE_BASE ** (-(jnp.arange(halfway, dtype=jnp.float32) * 2.0 / HEAD_DIM))
    turns = position.astype(jnp.float32)[:, None] * freqs[None, :]
    return (jnp.cos(turns)[:, None, :], jnp.sin(turns)[:, None, :])


def rotate(field, cosine, sine_part):
    halfway = field.shape[-1] // 2
    leading = field[..., :halfway]
    second = field[..., halfway:]
    return jnp.concatenate(
        [leading * cosine - second * sine_part, second * cosine + leading * sine_part], axis=-1
    )


def unrotate(field, cosine, sine_part):
    halfway = field.shape[-1] // 2
    leading = field[..., :halfway]
    second = field[..., halfway:]
    return jnp.concatenate(
        [leading * cosine + second * sine_part, second * cosine - leading * sine_part], axis=-1
    )


def masked_scores(query, key_heads, key_segment, key_position, ancestry, position):
    scores = jnp.einsum(
        "qhd,khd->hqk", query, key_heads, preferred_element_type=jnp.float32
    ) * HEAD_DIM ** (-0.5)
    visible = (
        (key_segment[None, :] == ancestry[:, 0:1])
        | (key_segment[None, :] == ancestry[:, 1:2])
        | (key_segment[None, :] == ancestry[:, 2:3])
    ) & (key_position[None, :] <= position[:, None])
    return jnp.where(visible[None, :, :], scores, MASK_FILL)


def on_device(
    tokens,
    cotangent,
    segment,
    ancestry,
    position,
    routes,
    attn_gain,
    w_query,
    w_key,
    w_value,
    b_query,
    b_key,
    b_value,
    w_output,
    moe_gain,
    w_router,
    shared_switch,
    shared_gate,
    shared_up,
    shared_down,
    expert_gate,
    routed_up_weight,
    expert_down,
):
    rows_dev = tokens.shape[0]
    features = tokens.shape[1]
    experts = w_router.shape[1]
    choose = routes.shape[1]
    capacity = 5 * rows_dev // 8
    inv_root = HEAD_DIM ** (-0.5)
    (
        gain_one,
        query_w,
        key_w,
        value_w,
        bias_q,
        bias_k,
        bias_v,
        output_w,
        gain_two,
        router_w,
        switch_w,
    ) = (
        lax.all_gather(attn_gain, "fsdp", axis=0, tiled=True),
        lax.all_gather(w_query, "fsdp", axis=0, tiled=True),
        lax.all_gather(w_key, "fsdp", axis=0, tiled=True),
        lax.all_gather(w_value, "fsdp", axis=0, tiled=True),
        lax.all_gather(b_query, "fsdp", axis=0, tiled=True),
        lax.all_gather(b_key, "fsdp", axis=0, tiled=True),
        lax.all_gather(b_value, "fsdp", axis=0, tiled=True),
        lax.all_gather(w_output, "fsdp", axis=0, tiled=True),
        lax.all_gather(moe_gain, "fsdp", axis=0, tiled=True),
        lax.all_gather(w_router, "fsdp", axis=0, tiled=True),
        lax.all_gather(shared_switch, "fsdp", axis=0, tiled=True),
    )
    tokens_f = tokens.astype(jnp.float32)
    normed_f, factor_one = normalize(tokens_f, gain_one.astype(jnp.float32))
    normed = normed_f.astype(jnp.bfloat16)
    cosine, sine_part = angles(position)
    query_pre = jnp.dot(normed, query_w, preferred_element_type=jnp.float32) + bias_q.astype(
        jnp.float32
    )
    key_pre = jnp.dot(normed, key_w, preferred_element_type=jnp.float32) + bias_k.astype(
        jnp.float32
    )
    value_pre = jnp.dot(normed, value_w, preferred_element_type=jnp.float32) + bias_v.astype(
        jnp.float32
    )
    query = rotate(query_pre.reshape(rows_dev, HEADS, HEAD_DIM), cosine, sine_part).astype(
        jnp.bfloat16
    )
    keys = rotate(key_pre.reshape(rows_dev, HEADS, HEAD_DIM), cosine, sine_part).astype(
        jnp.bfloat16
    )
    keys = keys.reshape(rows_dev, features)
    values = value_pre.astype(jnp.bfloat16)
    key_all, value_all, seg_all, pos_all = (
        lax.all_gather(keys, "fsdp", axis=0, tiled=True),
        lax.all_gather(values, "fsdp", axis=0, tiled=True),
        lax.all_gather(segment, "fsdp", axis=0, tiled=True),
        lax.all_gather(position, "fsdp", axis=0, tiled=True),
    )
    key_count = key_all.shape[0]
    masked = masked_scores(
        query, key_all.reshape(key_count, HEADS, HEAD_DIM), seg_all, pos_all, ancestry, position
    )
    peak = jnp.max(masked, axis=-1, keepdims=True)
    expo = jnp.exp(masked - peak)
    total = jnp.sum(expo, axis=-1, keepdims=True)
    log_total = peak + jnp.log(total)
    attn_weights = (expo / total).astype(jnp.bfloat16)
    attended = (
        jnp.einsum(
            "hqk,khd->qhd",
            attn_weights,
            value_all.reshape(key_count, HEADS, HEAD_DIM),
            preferred_element_type=jnp.float32,
        )
        .reshape(rows_dev, features)
        .astype(jnp.bfloat16)
    )
    branch = jnp.dot(attended, output_w, preferred_element_type=jnp.float32)
    mixed = tokens_f + branch
    normed_two, factor_two = normalize(mixed, gain_two.astype(jnp.float32))
    moe_in = normed_two.astype(jnp.bfloat16)
    moe_f = moe_in.astype(jnp.float32)
    shared_rows = lax.all_gather(moe_in, "fsdp", axis=0, tiled=True)
    gate_pre = jnp.dot(shared_rows, shared_gate, preferred_element_type=jnp.float32)
    up_pre = jnp.dot(shared_rows, shared_up, preferred_element_type=jnp.float32)
    gate_act, gate_slope = silu_pair(gate_pre)
    shared_hidden = (gate_act * up_pre).astype(jnp.bfloat16)
    shared_out = lax.psum_scatter(
        jnp.dot(shared_hidden, shared_down, preferred_element_type=jnp.float32).astype(
            jnp.bfloat16
        ),
        "fsdp",
        scatter_dimension=0,
        tiled=True,
    ).astype(jnp.float32)
    opener = jax.nn.sigmoid(jnp.dot(moe_in, switch_w, preferred_element_type=jnp.float32))
    logits = jnp.dot(moe_in, router_w, preferred_element_type=jnp.float32)
    router_probs = jax.nn.softmax(logits, axis=-1)
    chooser = routes[:, :, None] == jnp.arange(experts, dtype=jnp.int32)[None, None, :]
    gates = jnp.sum(jnp.where(chooser, router_probs[:, None, :], 0.0), axis=-1)
    flat_hot = chooser.reshape(rows_dev * choose, experts).astype(jnp.int32)
    slots = jnp.sum((jnp.cumsum(flat_hot, axis=0) - 1) * flat_hot, axis=1)
    target = routes.reshape(-1) * capacity + slots
    entries = rows_dev * choose
    source = (
        jnp.full((experts * capacity,), entries, jnp.int32)
        .at[target]
        .set(jnp.arange(entries, dtype=jnp.int32))
    )
    token_of = source // choose
    padded_in = jnp.concatenate([moe_in, jnp.zeros((1, features), jnp.bfloat16)], axis=0)
    send = padded_in[token_of].reshape(experts, capacity, features)
    incoming_rows = lax.all_to_all(send, "fsdp", split_axis=0, concat_axis=1, tiled=True)
    expert_gate_rows = jnp.einsum(
        "htl,hlz->htz", incoming_rows, expert_gate, preferred_element_type=jnp.float32
    )
    expert_up_rows = jnp.einsum(
        "htl,hlz->htz", incoming_rows, routed_up_weight, preferred_element_type=jnp.float32
    )
    expert_activation, expert_silu_slope = silu_pair(expert_gate_rows)
    expert_hidden_rows = (expert_activation * expert_up_rows).astype(jnp.bfloat16)
    eout = jnp.einsum(
        "ecf,efd->ecd", expert_hidden_rows, expert_down, preferred_element_type=jnp.float32
    ).astype(jnp.bfloat16)
    returned = lax.all_to_all(eout, "fsdp", split_axis=1, concat_axis=0, tiled=True)
    picked = (
        returned.reshape(experts * capacity, features)[target]
        .reshape(rows_dev, choose, features)
        .astype(jnp.float32)
    )
    mixture = jnp.sum(gates[:, :, None] * picked, axis=1)
    output = (mixed + mixture + opener[:, None] * shared_out).astype(jnp.bfloat16)
    grad_out = cotangent.astype(jnp.float32)
    kept = (
        query_w,
        key_w,
        value_w,
        output_w,
        gain_one,
        gain_two,
        router_w,
        switch_w,
        key_all,
        value_all,
        seg_all,
        pos_all,
    )
    (
        query_w,
        key_w,
        value_w,
        output_w,
        gain_one,
        gain_two,
        router_w,
        switch_w,
        key_all,
        value_all,
        seg_all,
        pos_all,
    ) = kept
    gate_sens = jnp.sum(grad_out * shared_out, axis=-1) * opener * (1.0 - opener)
    shared_grad = (opener[:, None] * grad_out).astype(jnp.bfloat16)
    grad_rows = lax.all_gather(shared_grad, "fsdp", axis=0, tiled=True)
    grad_sdown = contract_rows(shared_hidden, grad_rows)
    grad_shidden = times_transposed(grad_rows, shared_down)
    grad_sgate_pre = (grad_shidden * up_pre * gate_slope).astype(jnp.bfloat16)
    grad_sup_pre = (grad_shidden * gate_act).astype(jnp.bfloat16)
    grad_sgate = contract_rows(shared_rows, grad_sgate_pre)
    grad_sup = contract_rows(shared_rows, grad_sup_pre)
    moe_shared = lax.psum_scatter(
        times_transposed(grad_sgate_pre, shared_gate) + times_transposed(grad_sup_pre, shared_up),
        "fsdp",
        scatter_dimension=0,
        tiled=True,
    )
    gate_flat = jnp.concatenate([gates.reshape(-1), jnp.zeros((1,), jnp.float32)], axis=0)
    grad_pad = jnp.concatenate([grad_out, jnp.zeros((1, features), jnp.float32)], axis=0)
    slot_grad = (gate_flat[source][:, None] * grad_pad[token_of]).astype(jnp.bfloat16)
    grad_recv = lax.all_to_all(
        slot_grad.reshape(experts, capacity, features),
        "fsdp",
        split_axis=0,
        concat_axis=1,
        tiled=True,
    )
    grad_expert_hidden = jnp.einsum(
        "ecd,efd->ecf", grad_recv, expert_down, preferred_element_type=jnp.float32
    )
    grad_edown = jnp.einsum(
        "ecf,ecd->efd", expert_hidden_rows, grad_recv, preferred_element_type=jnp.float32
    )
    grad_expert_gate_logits = (grad_expert_hidden * expert_up_rows * expert_silu_slope).astype(
        jnp.bfloat16
    )
    grad_expert_up_logits = (grad_expert_hidden * expert_activation).astype(jnp.bfloat16)
    grad_egate = jnp.einsum(
        "zmt,zmj->ztj", incoming_rows, grad_expert_gate_logits, preferred_element_type=jnp.float32
    )
    grad_expert_up_rows = jnp.einsum(
        "zmt,zmj->ztj", incoming_rows, grad_expert_up_logits, preferred_element_type=jnp.float32
    )
    grad_ein = jnp.einsum(
        "ksq,knq->ksn", grad_expert_gate_logits, expert_gate, preferred_element_type=jnp.float32
    ) + jnp.einsum(
        "ksq,knq->ksn", grad_expert_up_logits, routed_up_weight, preferred_element_type=jnp.float32
    )
    grad_back = lax.all_to_all(grad_ein, "fsdp", split_axis=1, concat_axis=0, tiled=True)
    moe_expert = jnp.sum(
        grad_back.reshape(experts * capacity, features)[target].reshape(rows_dev, choose, features),
        axis=1,
    )
    gate_grad = jnp.sum(grad_out[:, None, :] * picked, axis=-1)
    prob_grad = jnp.sum(jnp.where(chooser, gate_grad[:, :, None], 0.0), axis=1)
    logit_grad = router_probs * (
        prob_grad - jnp.sum(prob_grad * router_probs, axis=-1, keepdims=True)
    )
    grad_router = precise_rows(moe_f, logit_grad)
    switch_f = switch_w.astype(jnp.float32)
    grad_switch = jnp.dot(gate_sens, moe_f, precision=EXACT_MATMUL)
    grad_moe = (
        moe_shared
        + moe_expert
        + precise_transposed(logit_grad, router_w.astype(jnp.float32))
        + gate_sens[:, None] * switch_f[None, :]
    )
    back_mixed, grad_gain_two = norm_back(mixed, factor_two, gain_two.astype(jnp.float32), grad_moe)
    grad_mixed = grad_out + back_mixed
    branch_grad = grad_mixed.astype(jnp.bfloat16)
    grad_attended = (
        times_transposed(branch_grad, output_w)
        .astype(jnp.bfloat16)
        .reshape(rows_dev, HEADS, HEAD_DIM)
    )
    key_heads = key_all.reshape(key_count, HEADS, HEAD_DIM)
    value_heads = value_all.reshape(key_count, HEADS, HEAD_DIM)
    again_masked = masked_scores(query, key_heads, seg_all, pos_all, ancestry, position)
    probs = jnp.exp(again_masked - log_total)
    probs_low = probs.astype(jnp.bfloat16)
    weight_grad = jnp.einsum(
        "qhd,khd->hqk", grad_attended, value_heads, preferred_element_type=jnp.float32
    )
    diagonal = jnp.sum(probs * weight_grad, axis=-1, keepdims=True)
    score_grad = (probs * (weight_grad - diagonal)).astype(jnp.bfloat16)
    grad_query = (
        jnp.einsum("hqk,khd->qhd", score_grad, key_heads, preferred_element_type=jnp.float32)
        * inv_root
    )
    grad_keys = (
        jnp.einsum("hqk,qhd->khd", score_grad, query, preferred_element_type=jnp.float32) * inv_root
    )
    grad_values = jnp.einsum(
        "hqk,qhd->khd", probs_low, grad_attended, preferred_element_type=jnp.float32
    )
    key_value_grad = lax.psum_scatter(
        jnp.concatenate(
            [
                grad_keys.reshape(rows_dev * lax.axis_size("fsdp"), features),
                grad_values.reshape(rows_dev * lax.axis_size("fsdp"), features),
            ],
            axis=1,
        ).astype(jnp.bfloat16),
        "fsdp",
        scatter_dimension=0,
        tiled=True,
    ).astype(jnp.float32)
    grad_qpre = (
        unrotate(grad_query, cosine, sine_part).reshape(rows_dev, features).astype(jnp.bfloat16)
    )
    grad_kpre = (
        unrotate(key_value_grad[:, :features].reshape(rows_dev, HEADS, HEAD_DIM), cosine, sine_part)
        .reshape(rows_dev, features)
        .astype(jnp.bfloat16)
    )
    grad_vpre = key_value_grad[:, features:].astype(jnp.bfloat16)
    grad_bias_q = jnp.sum(grad_qpre.astype(jnp.float32), axis=0)
    grad_bias_k = jnp.sum(grad_kpre.astype(jnp.float32), axis=0)
    grad_bias_v = jnp.sum(grad_vpre.astype(jnp.float32), axis=0)
    grad_normed = (
        times_transposed(grad_qpre, query_w)
        + times_transposed(grad_kpre, key_w)
        + times_transposed(grad_vpre, value_w)
    )
    back_tokens, grad_gain_one = norm_back(
        tokens_f, factor_one, gain_one.astype(jnp.float32), grad_normed
    )
    grad_tokens = grad_mixed + back_tokens
    normed_all, attended_all, qpre_all, kpre_all, vpre_all, branch_all = (
        lax.all_gather(normed, "fsdp", axis=0, tiled=True),
        lax.all_gather(attended, "fsdp", axis=0, tiled=True),
        lax.all_gather(grad_qpre, "fsdp", axis=0, tiled=True),
        lax.all_gather(grad_kpre, "fsdp", axis=0, tiled=True),
        lax.all_gather(grad_vpre, "fsdp", axis=0, tiled=True),
        lax.all_gather(branch_grad, "fsdp", axis=0, tiled=True),
    )
    width = features // lax.axis_size("fsdp")
    offset = lax.axis_index("fsdp") * width
    normed_cols = lax.dynamic_slice_in_dim(normed_all, offset, width, 1)
    attended_cols = lax.dynamic_slice_in_dim(attended_all, offset, width, 1)
    sum_query = contract_rows(normed_cols, qpre_all)
    sum_key = contract_rows(normed_cols, kpre_all)
    sum_value = contract_rows(normed_cols, vpre_all)
    sum_output = contract_rows(attended_cols, branch_all)
    sum_gain_one, sum_bias_q, sum_bias_k, sum_bias_v, sum_gain_two, sum_router, sum_switch = (
        lax.psum_scatter(
            grad_gain_one.astype(jnp.bfloat16), "fsdp", scatter_dimension=0, tiled=True
        ).astype(jnp.float32),
        lax.psum_scatter(
            grad_bias_q.astype(jnp.bfloat16), "fsdp", scatter_dimension=0, tiled=True
        ).astype(jnp.float32),
        lax.psum_scatter(
            grad_bias_k.astype(jnp.bfloat16), "fsdp", scatter_dimension=0, tiled=True
        ).astype(jnp.float32),
        lax.psum_scatter(
            grad_bias_v.astype(jnp.bfloat16), "fsdp", scatter_dimension=0, tiled=True
        ).astype(jnp.float32),
        lax.psum_scatter(
            grad_gain_two.astype(jnp.bfloat16), "fsdp", scatter_dimension=0, tiled=True
        ).astype(jnp.float32),
        lax.psum_scatter(
            grad_router.astype(jnp.bfloat16), "fsdp", scatter_dimension=0, tiled=True
        ).astype(jnp.float32),
        lax.psum_scatter(
            grad_switch.astype(jnp.bfloat16), "fsdp", scatter_dimension=0, tiled=True
        ).astype(jnp.float32),
    )
    (
        final_gain_one,
        final_query,
        final_key,
        final_value,
        final_bias_q,
        final_bias_k,
        final_bias_v,
        final_output,
        final_gain_two,
        final_router,
        final_switch,
        final_sgate,
        final_sup,
        final_sdown,
        final_egate,
        final_expert_up,
        final_edown,
    ) = (
        lax.psum_scatter(
            sum_gain_one.astype(jnp.bfloat16), "grp", scatter_dimension=0, tiled=True
        ).astype(jnp.float32),
        lax.psum_scatter(
            sum_query.astype(jnp.bfloat16), "grp", scatter_dimension=1, tiled=True
        ).astype(jnp.float32),
        lax.psum_scatter(
            sum_key.astype(jnp.bfloat16), "grp", scatter_dimension=1, tiled=True
        ).astype(jnp.float32),
        lax.psum_scatter(
            sum_value.astype(jnp.bfloat16), "grp", scatter_dimension=1, tiled=True
        ).astype(jnp.float32),
        lax.psum_scatter(
            sum_bias_q.astype(jnp.bfloat16), "grp", scatter_dimension=0, tiled=True
        ).astype(jnp.float32),
        lax.psum_scatter(
            sum_bias_k.astype(jnp.bfloat16), "grp", scatter_dimension=0, tiled=True
        ).astype(jnp.float32),
        lax.psum_scatter(
            sum_bias_v.astype(jnp.bfloat16), "grp", scatter_dimension=0, tiled=True
        ).astype(jnp.float32),
        lax.psum_scatter(
            sum_output.astype(jnp.bfloat16), "grp", scatter_dimension=1, tiled=True
        ).astype(jnp.float32),
        lax.psum_scatter(
            sum_gain_two.astype(jnp.bfloat16), "grp", scatter_dimension=0, tiled=True
        ).astype(jnp.float32),
        lax.psum_scatter(
            sum_router.astype(jnp.bfloat16), "grp", scatter_dimension=0, tiled=True
        ).astype(jnp.float32),
        lax.psum_scatter(
            sum_switch.astype(jnp.bfloat16), "grp", scatter_dimension=0, tiled=True
        ).astype(jnp.float32),
        lax.psum_scatter(
            grad_sgate.astype(jnp.bfloat16), "grp", scatter_dimension=0, tiled=True
        ).astype(jnp.float32),
        lax.psum_scatter(
            grad_sup.astype(jnp.bfloat16), "grp", scatter_dimension=0, tiled=True
        ).astype(jnp.float32),
        lax.psum_scatter(
            grad_sdown.astype(jnp.bfloat16), "grp", scatter_dimension=1, tiled=True
        ).astype(jnp.float32),
        lax.psum_scatter(
            grad_egate.astype(jnp.bfloat16), "grp", scatter_dimension=1, tiled=True
        ).astype(jnp.float32),
        lax.psum_scatter(
            grad_expert_up_rows.astype(jnp.bfloat16), "grp", scatter_dimension=1, tiled=True
        ).astype(jnp.float32),
        lax.psum_scatter(
            grad_edown.astype(jnp.bfloat16), "grp", scatter_dimension=2, tiled=True
        ).astype(jnp.float32),
    )
    return (
        output,
        grad_tokens,
        final_gain_one,
        final_query,
        final_key,
        final_value,
        final_bias_q,
        final_bias_k,
        final_bias_v,
        final_output,
        final_gain_two,
        final_router,
        final_switch,
        final_sgate,
        final_sup,
        final_sdown,
        final_egate,
        final_expert_up,
        final_edown,
    )


def solution(mesh):
    return jax.shard_map(
        on_device,
        mesh=mesh,
        in_specs=(
            P(("grp", "fsdp"), None),
            P(("grp", "fsdp"), None),
            P(("grp", "fsdp")),
            P(("grp", "fsdp"), None),
            P(("grp", "fsdp")),
            P(("grp", "fsdp"), None),
            P("fsdp"),
            P("fsdp", None),
            P("fsdp", None),
            P("fsdp", None),
            P("fsdp"),
            P("fsdp"),
            P("fsdp"),
            P("fsdp", None),
            P("fsdp"),
            P("fsdp", None),
            P("fsdp"),
            P(None, "fsdp"),
            P(None, "fsdp"),
            P("fsdp", None),
            P("fsdp", None, None),
            P("fsdp", None, None),
            P("fsdp", None, None),
        ),
        out_specs=(
            P(("grp", "fsdp"), None),
            P(("grp", "fsdp"), None),
            P(("fsdp", "grp")),
            P("fsdp", "grp"),
            P("fsdp", "grp"),
            P("fsdp", "grp"),
            P(("fsdp", "grp")),
            P(("fsdp", "grp")),
            P(("fsdp", "grp")),
            P("fsdp", "grp"),
            P(("fsdp", "grp")),
            P(("fsdp", "grp"), None),
            P(("fsdp", "grp")),
            P("grp", "fsdp"),
            P("grp", "fsdp"),
            P("fsdp", "grp"),
            P("fsdp", "grp", None),
            P("fsdp", "grp", None),
            P("fsdp", None, "grp"),
        ),
        check_vma=False,
    )
```

profile of v0, /device:TPU:0, one launch (start us, length us, event | category | flops | bytes accessed | tf_op | source)
XLA Modules:
  0.0 2382.4 jit_solution(15781833688969058597)
XLA Ops:
  36.1 64.3 %all-gather.27.cloned.1.call-done = bf16[2048,2048]{1,0:T(8,128)(2,1)} async-done(((bf16[512,2048]{1,0:T(8,128)(2,1)}), bf16[2048,2048]{1,0:T(8,128)(2,1)}) %all-gather.27.cloned.1.call-update) | async-done | bytes 8388624 | tf_op jit(solution)/shard_map/all_gather | solution.py:148
  106.5 83.4 %all-gather.29.cloned.1.call-done = bf16[2048,2048]{1,0:T(8,128)(2,1)} async-done(((bf16[512,2048]{1,0:T(8,128)(2,1)}), bf16[2048,2048]{1,0:T(8,128)(2,1)}) %all-gather.29.cloned.1.call-update) | async-done | bytes 8388624 | tf_op jit(solution)/shard_map/all_gather | solution.py:149
  212.8 66.6 %all-gather.23.cloned.1.call-done = bf16[2048,2048]{1,0:T(8,128)(2,1)} async-done(((bf16[512,2048]{1,0:T(8,128)(2,1)}), bf16[2048,2048]{1,0:T(8,128)(2,1)}) %all-gather.23.cloned.1.call-update) | async-done | bytes 8388624 | tf_op jit(solution)/shard_map/all_gather | solution.py:150
  310.7 23.6 all-gather.31.cloned.1.call-done
  350.2 39.1 %all-gather.25.cloned.1.call-done = bf16[1024,2048]{1,0:T(8,128)(2,1)} async-done(((bf16[256,2048]{1,0:T(8,128)(2,1)}), bf16[1024,2048]{1,0:T(8,128)(2,1)}) %all-gather.25.cloned.1.call-update) | async-done | bytes 4194320 | tf_op jit(solution)/shard_map/all_gather | solution.py:182
  399.2 79.4 %all-gather.33.cloned.1.call-done = bf16[2048,2048]{1,0:T(8,128)(2,1)} async-done(((bf16[512,2048]{1,0:T(8,128)(2,1)}), bf16[2048,2048]{1,0:T(8,128)(2,1)}) %all-gather.33.cloned.1.call-update) | async-done | bytes 8388624 | tf_op jit(solution)/shard_map/all_gather | solution.py:154
  487.8 52.1 %all-gather.35.cloned.1.call-done = bf16[1024,2048]{1,0:T(8,128)(2,1)} async-done(((bf16[256,2048]{1,0:T(8,128)(2,1)}), bf16[1024,2048]{1,0:T(8,128)(2,1)}) %all-gather.35.cloned.1.call-update) | async-done | bytes 4194320 | tf_op jit(solution)/shard_map/all_gather | solution.py:210
  539.9 11.1 fusion.68
  551.1 12.9 multiply_convert_fusion.8
  625.4 56.4 %all-to-all-done.2 = bf16[8,160,2048]{2,1,0:T(8,128)(2,1)} async-done(((bf16[8,160,2048]{2,1,0:T(8,128)(2,1)}), bf16[8,160,2048]{2,1,0:T(8,128)(2,1)}, u32[]{:S(2)}, u32[]{:S(2)}) %all-to-all-start.2) | async-done | bytes 5242912 | tf_op jit(solution)/shard_map/all_to_all | solution.py:307
  687.1 61.6 %all-gather.7 = bf16[4,1,512]{2,1,0:T(2,128)(2,1)S(1)} all-gather(bf16[1,1,512]{2,1,0:T(2,128)(2,1)S(1)} %reshape.476), channel_id=1, replica_groups=mesh['grp'=8,'fsdp'=4] {'fsdp'}, dimensions={0}, use_global_device_ids=true | all-gather | bytes 5120 | tf_op jit(solution)/shard_map/all_gather | solution.py:157
  762.4 14.9 fusion.65
  787.6 18.2 all-gather.37.cloned.1.call-done
  805.8 14.6 multiply_convert_fusion.6
  838.1 18.7 multiply_convert_fusion.3
  856.7 15.5 convolution_convert_fusion.6
  887.9 14.8 fusion.70
  902.7 18.8 convolution_add_fusion
  921.6 18.7 copy.164
  940.3 26.7 %all-to-all-done.1 = bf16[2,640,2048]{2,0,1:T(2,128)(2,1)} async-done(((bf16[2,640,2048]{2,0,1:T(2,128)(2,1)}), bf16[2,640,2048]{2,0,1:T(2,128)(2,1)}, u32[]{:S(2)}, u32[]{:S(2)}) %all-to-all-start.1) | async-done | bytes 5242912 | tf_op jit(solution)/shard_map/all_to_all | solution.py:252
  980.5 12.2 gather_fusion.1
  1001.2 11.1 multiply_reduce_fusion.1
  1012.4 75.0 %all-to-all-done.3 = f32[2,640,2048]{2,0,1:T(2,128)} async-done(((f32[2,640,2048]{2,0,1:T(2,128)}), f32[2,640,2048]{2,0,1:T(2,128)}, u32[]{:S(2)}, u32[]{:S(2)}) %all-to-all-start.3) | async-done | bytes 10485792 | tf_op jit(solution)/shard_map/all_to_all | solution.py:335
  1087.4 13.9 copy.165
  1101.3 12.9 gather_fusion.4
  1158.0 13.0 multiply_reduce_fusion
  1171.0 12.3 multiply_convert_fusion
  1208.0 74.3 %reduce-scatter.22.cloned.1.call-done = bf16[256,4096]{0,1:T(8,128)(2,1)} async-done(((bf16[1024,4096]{0,1:T(8,128)(2,1)}), bf16[256,4096]{0,1:T(8,128)(2,1)}) %reduce-scatter.22.cloned.1.call-update) | async-done | bytes 2097168 | tf_op jit(solution)/shard_map/reduce_scatter | solution.py:382
  1310.8 14.7 convolution_convert_fusion
  1326.1 15.2 convolution_convert_fusion.2
  1341.3 15.4 convolution_convert_fusion.1
  1389.7 29.0 %all-gather.49.cloned.1.call-done = bf16[1024,2048]{1,0:T(8,128)(2,1)} async-done(((bf16[256,2048]{1,0:T(8,128)(2,1)}), bf16[1024,2048]{1,0:T(8,128)(2,1)}) %all-gather.49.cloned.1.call-update) | async-done | bytes 4194320 | tf_op jit(solution)/shard_map/all_gather | solution.py:421
  1425.1 48.6 %all-gather.39.cloned.1.call-done = bf16[1024,2048]{1,0:T(8,128)(2,1)} async-done(((bf16[256,2048]{1,0:T(8,128)(2,1)}), bf16[1024,2048]{1,0:T(8,128)(2,1)}) %all-gather.39.cloned.1.call-update) | async-done | bytes 4194320 | tf_op jit(solution)/shard_map/all_gather | solution.py:416
  1473.7 54.3 %all-gather.43.cloned.1.call-done = bf16[1024,2048]{0,1:T(8,128)(2,1)} async-done(((bf16[256,2048]{0,1:T(8,128)(2,1)}), bf16[1024,2048]{0,1:T(8,128)(2,1)}) %all-gather.43.cloned.1.call-update) | async-done | bytes 4194320 | tf_op jit(solution)/shard_map/all_gather | solution.py:419
  1534.3 48.0 %all-gather.41.cloned.1.call-done = bf16[1024,2048]{0,1:T(8,128)(2,1)} async-done(((bf16[256,2048]{0,1:T(8,128)(2,1)}), bf16[1024,2048]{0,1:T(8,128)(2,1)}) %all-gather.41.cloned.1.call-update) | async-done | bytes 4194320 | tf_op jit(solution)/shard_map/all_gather | solution.py:418
  1588.8 48.3 %all-gather.45.cloned.1.call-done = bf16[1024,2048]{0,1:T(8,128)(2,1)} async-done(((bf16[256,2048]{0,1:T(8,128)(2,1)}), bf16[1024,2048]{0,1:T(8,128)(2,1)}) %all-gather.45.cloned.1.call-update) | async-done | bytes 4194320 | tf_op jit(solution)/shard_map/all_gather | solution.py:420
  1645.8 24.2 %reduce-scatter.46.cloned.1.call-done = bf16[64,8]{1,0:T(8,128)(2,1)} async-done(((bf16[512,8]{1,0:T(8,128)(2,1)}), bf16[64,8]{1,0:T(8,128)(2,1)}) %reduce-scatter.46.cloned.1.call-update) | async-done | bytes 1040
  1672.0 117.9 %reduce-scatter.44.cloned.1.call-done = bf16[2,1408,256]{2,1,0:T(8,128)(2,1)} async-done(((bf16[2,1408,2048]{2,1,0:T(8,128)(2,1)}), bf16[2,1408,256]{2,1,0:T(8,128)(2,1)}) %reduce-scatter.44.cloned.1.call-update) | async-done | bytes 1441808 | tf_op jit(solution)/shard_map/reduce_scatter | solution.py:521
  1793.0 117.0 %reduce-scatter.40.cloned.1.call-done = bf16[2,256,1408]{2,1,0:T(8,128)(2,1)} async-done(((bf16[2,2048,1408]{2,1,0:T(8,128)(2,1)}), bf16[2,256,1408]{2,1,0:T(8,128)(2,1)}) %reduce-scatter.40.cloned.1.call-update) | async-done | bytes 1441808 | tf_op jit(solution)/shard_map/reduce_scatter | solution.py:515
  1913.1 117.0 %reduce-scatter.42.cloned.1.call-done = bf16[2,256,1408]{2,1,0:T(8,128)(2,1)} async-done(((bf16[2,2048,1408]{2,1,0:T(8,128)(2,1)}), bf16[2,256,1408]{2,1,0:T(8,128)(2,1)}) %reduce-scatter.42.cloned.1.call-update) | async-done | bytes 1441808 | tf_op jit(solution)/shard_map/reduce_scatter | solution.py:518
  2033.2 62.5 %reduce-scatter.34.cloned.1.call-done = bf16[256,1408]{1,0:T(8,128)(2,1)} async-done(((bf16[2048,1408]{1,0:T(8,128)(2,1)}), bf16[256,1408]{1,0:T(8,128)(2,1)}) %reduce-scatter.34.cloned.1.call-update) | async-done | bytes 720912 | tf_op jit(solution)/shard_map/reduce_scatter | solution.py:506
  2098.0 63.2 %reduce-scatter.36.cloned.1.call-done = bf16[256,1408]{1,0:T(8,128)(2,1)} async-done(((bf16[2048,1408]{1,0:T(8,128)(2,1)}), bf16[256,1408]{1,0:T(8,128)(2,1)}) %reduce-scatter.36.cloned.1.call-update) | async-done | bytes 720912 | tf_op jit(solution)/shard_map/reduce_scatter | solution.py:509
  2163.5 63.4 %reduce-scatter.38.cloned.1.call-done = bf16[1408,256]{1,0:T(8,128)(2,1)} async-done(((bf16[1408,2048]{1,0:T(8,128)(2,1)}), bf16[1408,256]{1,0:T(8,128)(2,1)}) %reduce-scatter.38.cloned.1.call-update) | async-done | bytes 720912 | tf_op jit(solution)/shard_map/reduce_scatter | solution.py:512
  2229.2 34.1 %reduce-scatter.30.cloned.1.call-done = bf16[512,256]{1,0:T(8,128)(2,1)} async-done(((bf16[512,2048]{1,0:T(8,128)(2,1)}), bf16[512,256]{1,0:T(8,128)(2,1)}) %reduce-scatter.30.cloned.1.call-update) | async-done | bytes 262160 | tf_op jit(solution)/shard_map/reduce_scatter | solution.py:494
  2281.3 16.1 all-reduce.15
  2297.9 13.9 all-reduce.14
  2320.6 16.5 reduce-scatter.24.cloned.1.call-done
  2338.8 34.9 %reduce-scatter.28.cloned.1.call-done = bf16[512,256]{1,0:T(8,128)(2,1)} async-done(((bf16[512,2048]{1,0:T(8,128)(2,1)}), bf16[512,256]{1,0:T(8,128)(2,1)}) %reduce-scatter.28.cloned.1.call-update) | async-done | bytes 262160 | tf_op jit(solution)/shard_map/reduce_scatter | solution.py:482
  (417 shorter events, 474.8 us)
Async XLA Ops:
  7.2 93.1 %all-gather.27.cloned.1.call-start = ((), (), s32[]{:S(2)}) async-start(), calls=%async_computation.21 | async-start | bytes 10485760 | tf_op jit(solution)/shard_map/all_gather | solution.py:148
  8.0 181.9 %all-gather.29.cloned.1.call-start = ((), (), s32[]{:S(2)}) async-start(), calls=%async_computation.22 | async-start | bytes 10485760 | tf_op jit(solution)/shard_map/all_gather | solution.py:149
  8.7 270.7 %all-gather.23.cloned.1.call-start = ((), (), s32[]{:S(2)}) async-start(), calls=%async_computation.19 | async-start | bytes 10485760 | tf_op jit(solution)/shard_map/all_gather | solution.py:150
  9.5 324.9 %all-gather.31.cloned.1.call-start = ((), (), s32[]{:S(2)}) async-start(), calls=%async_computation.23 | async-start | bytes 5242880 | tf_op jit(solution)/shard_map/all_gather | solution.py:181
  19.1 81.3 %copy-start.42 = (f32[4,1,512]{2,1,0:T(1,128)}, f32[4,1,512]{2,1,0:T(1,128)S(1)}, u32[]{:S(2)}) copy-start(f32[4,1,512]{2,1,0:T(1,128)S(1)} %convert_element_type.324) | copy-start | bytes 24580
  35.2 65.2 %copy-start.57 = (f32[256]{0:T(256)}, f32[256]{0:T(256)S(1)}, u32[]{:S(2)}) copy-start(f32[256]{0:T(256)S(1)} %get-tuple-element.80) | copy-start | bytes 3076
  35.7 161.9 %copy-start.26 = (f32[256,64]{1,0:T(8,128)}, f32[256,64]{1,0:T(8,128)S(1)}, u32[]{:S(2)}) copy-start(f32[256,64]{1,0:T(8,128)S(1)} %get-tuple-element.77) | copy-start | bytes 196612
  35.7 161.9 %copy-start.28 = (f32[256,64]{1,0:T(8,128)}, f32[256,64]{1,0:T(8,128)S(1)}, u32[]{:S(2)}) copy-start(f32[256,64]{1,0:T(8,128)S(1)} %get-tuple-element.78) | copy-start | bytes 196612
  36.1 64.3 %copy-start.24 = (bf16[256,2048]{1,0:T(8,128)(2,1)}, bf16[256,2048]{1,0:T(8,128)(2,1)S(1)}, u32[]{:S(2)}) copy-start(bf16[256,2048]{1,0:T(8,128)(2,1)S(1)} %fusion.23) | copy-start | bytes 3145732
  200.4 133.9 %copy-start.11 = (bf16[256,16,64]{2,0,1:T(8,128)(2,1)}, bf16[256,16,64]{2,0,1:T(8,128)(2,1)S(1)}, u32[]{:S(2)}) copy-start(bf16[256,16,64]{2,0,1:T(8,128)(2,1)S(1)} %get-tuple-element.52) | copy-start | bytes 1572868
  200.4 133.9 %copy-start.13 = (bf16[256,16,64]{2,0,1:T(8,128)(2,1)}, bf16[256,16,64]{2,0,1:T(8,128)(2,1)S(1)}, u32[]{:S(2)}) copy-start(bf16[256,16,64]{2,0,1:T(8,128)(2,1)S(1)} %get-tuple-element.53) | copy-start | bytes 1572868
  204.5 184.8 %all-gather.25.cloned.1.call-start = ((), (), s32[]{:S(2)}) async-start(), calls=%async_computation.20 | async-start | bytes 5242880 | tf_op jit(solution)/shard_map/all_gather | solution.py:182
  286.5 192.2 %all-gather.33.cloned.1.call-start = ((), (), s32[]{:S(2)}) async-start(), calls=%async_computation.24 | async-start | bytes 10485760 | tf_op jit(solution)/shard_map/all_gather | solution.py:154
  287.1 252.9 %all-gather.35.cloned.1.call-start = ((), (), s32[]{:S(2)}) async-start(), calls=%async_computation.25 | async-start | bytes 5242880 | tf_op jit(solution)/shard_map/all_gather | solution.py:210
  295.2 189.9 %copy-start.36 = (f32[4,1,512]{2,1,0:T(1,128)}, f32[4,1,512]{2,1,0:T(1,128)S(1)}, u32[]{:S(2)}) copy-start(f32[4,1,512]{2,1,0:T(1,128)S(1)} %convert_element_type.328) | copy-start | bytes 24580
  399.2 85.3 %copy-start.17 = (bf16[16,128,256]{2,1,0:T(8,128)(2,1)}, bf16[16,128,256]{2,1,0:T(8,128)(2,1)S(1)}, u32[]{:S(2)}) copy-start(bf16[16,128,256]{2,1,0:T(8,128)(2,1)S(1)} %fusion.32) | copy-start | bytes 3145732
  485.1 66.0 %copy-start.51 = (f32[256]{0:T(256)}, f32[256]{0:T(256)S(1)}, u32[]{:S(2)}) copy-start(f32[256]{0:T(256)S(1)} %get-tuple-element.82) | copy-start | bytes 3076
  487.1 261.9 %reduce-scatter.18.cloned.1.call-start = ((), (), s32[]{:S(2)}) async-start(), calls=%async_computation.26 | async-start | bytes 5242880 | tf_op jit(solution)/shard_map/reduce_scatter | solution.py:215
  614.1 67.7 %all-to-all-start.2 = ((bf16[8,160,2048]{2,1,0:T(8,128)(2,1)}), bf16[8,160,2048]{2,1,0:T(8,128)(2,1)}, u32[]{:S(2)}, u32[]{:S(2)}) async-start(bf16[8,160,2048]{2,1,0:T(8,128)(2,1)} %multiply_convert_fusion.1), calls=%async_computation.4 | async-start | bytes 10485760 | tf_op jit(solution)/shard_map/all_to_all | solution.py:307
  681.8 67.3 %copy-start.7 = (bf16[256,2048]{1,0:T(8,128)(2,1)S(1)}, bf16[256,2048]{1,0:T(8,128)(2,1)}, u32[]{:S(2)}) copy-start(bf16[256,2048]{1,0:T(8,128)(2,1)} %param.24) | copy-start | bytes 3145732
  681.8 76.9 %all-to-all-start = ((bf16[8,160,2048]{2,1,0:T(8,128)(2,1)}), bf16[8,160,2048]{2,1,0:T(8,128)(2,1)}, u32[]{:S(2)}, u32[]{:S(2)}) async-start(bf16[8,160,2048]{2,1,0:T(8,128)(2,1)} %bitcast.170), calls=%async_computation | async-start | bytes 10485760 | tf_op jit(solution)/shard_map/all_to_all | solution.py:240
  687.0 118.8 %all-gather.37.cloned.1.call-start = ((), (), s32[]{:S(2)}) async-start(), calls=%async_computation.27 | async-start | bytes 5242880 | tf_op jit(solution)/shard_map/all_gather | solution.py:291
  753.0 381.5 %reduce-scatter.20.cloned.1.call-start = ((), (), s32[]{:S(2)}) async-start(), calls=%async_computation.28 | async-start | bytes 10485760 | tf_op jit(solution)/shard_map/reduce_scatter | solution.py:298
  882.7 84.4 %all-to-all-start.1 = ((bf16[2,640,2048]{2,0,1:T(2,128)(2,1)}), bf16[2,640,2048]{2,0,1:T(2,128)(2,1)}, u32[]{:S(2)}, u32[]{:S(2)}) async-start(bf16[2,640,2048]{2,0,1:T(2,128)(2,1)} %copy.160), calls=%async_computation.1 | async-start | bytes 10485760 | tf_op jit(solution)/shard_map/all_to_all | solution.py:252
  967.0 120.4 %all-to-all-start.3 = ((f32[2,640,2048]{2,0,1:T(2,128)}), f32[2,640,2048]{2,0,1:T(2,128)}, u32[]{:S(2)}, u32[]{:S(2)}) async-start(f32[2,640,2048]{2,0,1:T(2,128)} %copy.164), calls=%async_computation.5 | async-start | bytes 20971520 | tf_op jit(solution)/shard_map/all_to_all | solution.py:335
  973.0 309.3 %reduce-scatter.22.cloned.1.call-start = ((), (), s32[]{:S(2)}) async-start(), calls=%async_computation.29 | async-start | bytes 10485760 | tf_op jit(solution)/shard_map/reduce_scatter | solution.py:382
  1195.8 113.5 %reduce-scatter.32.cloned.1.call-start = ((), (), s32[]{:S(2)}) async-start(), calls=%async_computation.40 | async-start | bytes 40960 | tf_op jit(solution)/shard_map/reduce_scatter | solution.py:447
  1198.1 191.5 %all-gather.47.cloned.1.call-start = ((), (), s32[]{:S(2)}) async-start(), calls=%async_computation.37 | async-start | bytes 5242880 | tf_op jit(solution)/shard_map/all_gather | solution.py:417
  1198.9 219.8 %all-gather.49.cloned.1.call-start = ((), (), s32[]{:S(2)}) async-start(), calls=%async_computation.38 | async-start | bytes 5242880 | tf_op jit(solution)/shard_map/all_gather | solution.py:421
  1199.5 274.2 %all-gather.39.cloned.1.call-start = ((), (), s32[]{:S(2)}) async-start(), calls=%async_computation.30 | async-start | bytes 5242880 | tf_op jit(solution)/shard_map/all_gather | solution.py:416
  1200.0 327.9 %all-gather.43.cloned.1.call-start = ((), (), s32[]{:S(2)}) async-start(), calls=%async_computation.33 | async-start | bytes 5242880 | tf_op jit(solution)/shard_map/all_gather | solution.py:419
  1301.4 280.9 %all-gather.41.cloned.1.call-start = ((), (), s32[]{:S(2)}) async-start(), calls=%async_computation.31 | async-start | bytes 5242880 | tf_op jit(solution)/shard_map/all_gather | solution.py:418
  1305.4 331.7 %all-gather.45.cloned.1.call-start = ((), (), s32[]{:S(2)}) async-start(), calls=%async_computation.35 | async-start | bytes 5242880 | tf_op jit(solution)/shard_map/all_gather | solution.py:420
  1306.0 364.1 %reduce-scatter.46.cloned.1.call-start = ((), (), s32[]{:S(2)}) async-start(), calls=%async_computation.47 | async-start | bytes 147456
  1310.8 479.1 %reduce-scatter.44.cloned.1.call-start = ((), (), s32[]{:S(2)}) async-start(), calls=%async_computation.46 | async-start | bytes 12976128 | tf_op jit(solution)/shard_map/reduce_scatter | solution.py:521
  1325.5 584.4 %reduce-scatter.40.cloned.1.call-start = ((), (), s32[]{:S(2)}) async-start(), calls=%async_computation.44 | async-start | bytes 12976128 | tf_op jit(solution)/shard_map/reduce_scatter | solution.py:515
  1341.3 688.8 %reduce-scatter.42.cloned.1.call-start = ((), (), s32[]{:S(2)}) async-start(), calls=%async_computation.45 | async-start | bytes 12976128 | tf_op jit(solution)/shard_map/reduce_scatter | solution.py:518
  1356.8 739.0 %reduce-scatter.34.cloned.1.call-start = ((), (), s32[]{:S(2)}) async-start(), calls=%async_computation.41 | async-start | bytes 6488064 | tf_op jit(solution)/shard_map/reduce_scatter | solution.py:506
  1368.0 793.3 %reduce-scatter.36.cloned.1.call-start = ((), (), s32[]{:S(2)}) async-start(), calls=%async_computation.42 | async-start | bytes 6488064 | tf_op jit(solution)/shard_map/reduce_scatter | solution.py:509
  1379.0 847.9 %reduce-scatter.38.cloned.1.call-start = ((), (), s32[]{:S(2)}) async-start(), calls=%async_computation.43 | async-start | bytes 6488064 | tf_op jit(solution)/shard_map/reduce_scatter | solution.py:512
  1389.6 873.8 %reduce-scatter.30.cloned.1.call-start = ((), (), s32[]{:S(2)}) async-start(), calls=%async_computation.39 | async-start | bytes 2359296 | tf_op jit(solution)/shard_map/reduce_scatter | solution.py:494
  1425.0 893.8 %reduce-scatter.26.cloned.1.call-start = ((), (), s32[]{:S(2)}) async-start(), calls=%async_computation.34 | async-start | bytes 2359296 | tf_op jit(solution)/shard_map/reduce_scatter | solution.py:479
  1534.2 802.8 %reduce-scatter.24.cloned.1.call-start = ((), (), s32[]{:S(2)}) async-start(), calls=%async_computation.32 | async-start | bytes 2359296 | tf_op jit(solution)/shard_map/reduce_scatter | solution.py:476
  1588.5 54.8 %copy-start.79 = (u32[32]{0:T(128)S(1)}, u32[32]{0:T(128)}, u32[]{:S(2)}) copy-start(u32[32]{0:T(128)} %constant.90) | copy-start | bytes 388
  1588.5 55.4 %copy-start.78 = (u32[32]{0:T(128)S(1)}, u32[32]{0:T(128)}, u32[]{:S(2)}) copy-start(u32[32]{0:T(128)} %constant.94) | copy-start | bytes 388
  1588.6 82.9 %copy-start.60 = (f32[256]{0:T(256)S(1)}, f32[256]{0:T(256)}, u32[]{:S(2)}) copy-start(f32[256]{0:T(256)} %get-tuple-element.43) | copy-start | bytes 3076
  1588.6 785.1 %reduce-scatter.28.cloned.1.call-start = ((), (), s32[]{:S(2)}) async-start(), calls=%async_computation.36 | async-start | bytes 2359296 | tf_op jit(solution)/shard_map/reduce_scatter | solution.py:482
  2033.2 231.9 %copy-start.23 = (bf16[256,16,128]{0,2,1:T(8,128)(2,1)S(1)}, bf16[256,16,128]{0,2,1:T(8,128)(2,1)}, u32[]{:S(2)}) copy-start(bf16[256,16,128]{0,2,1:T(8,128)(2,1)} %copy.170) | copy-start | bytes 3145732
  (79 other events, 1016.1 us)
Sparse Core Ops, SparseCore 0:
  9.9 90.3 all-gather.26
  102.2 87.5 all-gather.28
  191.7 87.6 all-gather.22
  281.7 52.6 all-gather.30
  336.6 52.6 all-gather.24
  391.0 87.5 all-gather.32
  487.2 52.6 all-gather.34
  574.0 85.5 reduce-scatter.17
  753.1 52.6 all-gather.36
  838.2 133.6 reduce-scatter.19
  1195.9 86.3 reduce-scatter.21
  1285.6 23.5 reduce-scatter.31
  1311.1 52.5 all-gather.46
  1365.9 52.7 all-gather.48
  1420.9 52.6 all-gather.38
  1475.4 52.5 all-gather.42
  1529.6 52.5 all-gather.40
  1584.5 52.5 all-gather.44
  1639.9 30.1 reduce-scatter.45
  1672.3 117.4 reduce-scatter.43
  1792.2 117.6 reduce-scatter.39
  1912.4 117.6 reduce-scatter.41
  2032.5 63.2 reduce-scatter.33
  2098.0 63.1 reduce-scatter.35
  2163.6 63.2 reduce-scatter.37
  2229.1 34.1 reduce-scatter.29
  2265.6 34.5 reduce-scatter.25
  2302.5 34.4 reduce-scatter.23
  2339.4 34.2 reduce-scatter.27
where the time goes:
time: 2390 us; the launch traced here: 2380 us
  waiting for transfers between devices  1550 us (65%)
  matrix products  364 us (15%)
  local copies, waits for them, and re-layouts  164 us (7%)
  blocking collectives  156 us (7%)
  other arithmetic  111 us (5%)
  starting transfers between devices  24.1 us (1%)
    reduce_scatter x1, waiting for transfers between devices, on_device(): lax.psum_scatter(grad_edown.astype(jnp.bfloat16), 'grp', scatter_dimensio...  118 us
    reduce_scatter x1, waiting for transfers between devices, on_device(): lax.psum_scatter(grad_expert_up_rows.astype(jnp.bfloat16), 'grp', scatter...  117 us
    reduce_scatter x1, waiting for transfers between devices, on_device(): lax.psum_scatter(grad_egate.astype(jnp.bfloat16), 'grp', scatter_dimensio...  117 us
    all_gather x1, waiting for transfers between devices, on_device(): lax.all_gather(w_key, 'fsdp', axis=0, tiled=True)  83.4 us
    all_gather x1, waiting for transfers between devices, on_device(): lax.all_gather(w_output, 'fsdp', axis=0, tiled=True)  79.4 us
    all_to_all x1, waiting for transfers between devices, on_device(): lax.all_to_all(grad_ein, 'fsdp', split_axis=1, concat_axis=0, tiled=True)  75 us
    reduce_scatter x1, waiting for transfers between devices, on_device(): lax.psum_scatter(jnp.concatenate([grad_keys.reshape(rows_dev * lax.axis_s...  74.3 us
    all_gather x1, waiting for transfers between devices, on_device(): lax.all_gather(w_value, 'fsdp', axis=0, tiled=True)  66.6 us
  transfers between devices with their start and end apart: 33, of which 28 were waited for; matrix products, arithmetic and copies ran while one was open for 21% of the time, Pallas kernels for 0%

commit v1 on v0

v1 whole, which is shorter than its diff:
```python
import functools

import jax
import jax.numpy as jnp
from jax import lax
from jax.experimental import pallas as pl
from jax.experimental.pallas import tpu as pltpu
from jax.sharding import PartitionSpec as P

HEADS = 16
HEAD_DIM = 128
EPSILON = 1e-06
ROPE_BASE = 1000000.0
MASK_FILL = -1e30

F32 = jnp.float32
BF16 = jnp.bfloat16
MESH = pl.DeviceIdType.MESH
ANY = pl.BlockSpec(memory_space=pl.ANY)
VMEM = pl.BlockSpec(memory_space=pltpu.VMEM)


def line_kernel(
    parts, stack, out, sib, recv, own_v, sib_v, in_v, more_v, send_v, out_v,
    load_sems, out_sem, sib_send, sib_recv, send_sems, recv_sems,
):
    matrices = stack.shape[0]
    rows = stack.shape[3] // parts
    chunks = matrices * parts
    slots = send_v.shape[0]
    g = lax.axis_index("grp")
    z, core = g // 2, lax.rem(g, 2)
    is_end = (z == 0) | (z == 3)
    is_mid = (z == 1) | (z == 2)

    def at(zz, cc):
        return {"grp": 2 * zz + cc}

    barrier = pltpu.get_barrier_semaphore()
    pl.semaphore_signal(barrier, inc=1, device_id=at(z, 1 - core), device_id_type=MESH)

    @pl.when(z > 0)
    def _():
        pl.semaphore_signal(barrier, inc=1, device_id=at(z - 1, core), device_id_type=MESH)

    @pl.when(z < 3)
    def _():
        pl.semaphore_signal(barrier, inc=1, device_id=at(z + 1, core), device_id_type=MESH)

    @pl.when(is_end)
    def _():
        pl.semaphore_wait(barrier, 2)

    @pl.when(is_mid)
    def _():
        pl.semaphore_wait(barrier, 3)

    def span(q):
        return lax.div(q, parts), pl.ds(pl.multiple_of(lax.rem(q, parts) * rows, rows), rows)

    def swap(q):
        m, r = span(q)
        return pltpu.make_async_remote_copy(
            src_ref=stack.at[m, :, 1 - core, r],
            dst_ref=sib.at[m, :, r],
            send_sem=sib_send.at[q],
            recv_sem=sib_recv.at[q],
            device_id=at(z, 1 - core),
            device_id_type=MESH,
        )

    def begin(q, carry):
        swap(q).start()
        return carry

    lax.fori_loop(0, chunks, begin, 0)

    def out_copy(q):
        m, r = span(q)
        return pltpu.make_async_copy(out_v, out.at[m, r], out_sem)

    def hop(q, slot, p, target, place):
        m, r = span(q)
        return pltpu.make_async_remote_copy(
            src_ref=send_v.at[slot],
            dst_ref=recv.at[m, place, r],
            send_sem=send_sems.at[slot],
            recv_sem=recv_sems.at[q, place],
            device_id=at(target, core),
            device_id_type=MESH,
        )

    def arrived(q, place):
        m, r = span(q)
        hop(q, 0, 0, z, place).wait_recv()

    def base_loads(q, p):
        m, r = span(q)
        return (
            pltpu.make_async_copy(stack.at[m, p, core, r], own_v, load_sems.at[0]),
            pltpu.make_async_copy(sib.at[m, p, r], sib_v, load_sems.at[1]),
        )

    def extra_load(q, place, buf, k):
        m, r = span(q)
        return pltpu.make_async_copy(recv.at[m, place, r], buf, load_sems.at[k])

    def send(t, j, q, p, target, place, more):
        slot = lax.rem(t, slots // 3) * 3 + j

        @pl.when(t >= slots // 3 + (q_first(j)))
        def _():
            hop(q, slot, p, target, place).wait_send()

        loads = base_loads(q, p)
        if more:
            arrived(q, p)
            loads = loads + (extra_load(q, p, in_v, 2),)
        for c in loads:
            c.start()
        for c in loads:
            c.wait()
        total = own_v[...].astype(F32) + sib_v[...].astype(F32)
        if more:
            total = total + in_v[...].astype(F32)
        send_v[slot] = total.astype(BF16)
        hop(q, slot, p, target, place).start()

    def q_first(j):
        return jnp.where(is_end, 0, 1 if j < 2 else 2)

    def turn(t, carry):
        @pl.when(t < chunks)
        def _():
            swap(t).wait_recv()

        @pl.when(is_end & (t < chunks))
        def _():
            for j in range(3):
                p = jnp.where(z == 0, 3 - j, j)
                target = jnp.where(z == 0, 1, 2)
                place = jnp.where((z == 3) & (p == 2), 4, p)
                send(t, j, t, p, target, place, False)

        @pl.when(is_mid & (t >= 1) & (t < chunks + 1))
        def _():
            for j in range(2):
                p = jnp.where(z == 1, 3 - j, j)
                target = jnp.where(z == 1, 2, 1)
                place = jnp.where((z == 2) & (p == 1), 4, p)
                send(t, j, t - 1, p, target, place, True)

        @pl.when(is_mid & (t >= 2) & (t < chunks + 2))
        def _():
            p = jnp.where(z == 2, 3, 0)
            target = p
            place = jnp.where(z == 1, 4, p)
            send(t, 2, t - 2, p, target, place, True)

        @pl.when(t >= 3)
        def _():
            q = t - 3
            loads = base_loads(q, z)
            for c in loads:
                c.start()

            @pl.when(z > 0)
            def _():
                arrived(q, z)
                c = extra_load(q, z, in_v, 2)
                c.start()
                c.wait()

            @pl.when(z < 3)
            def _():
                arrived(q, 4)
                c = extra_load(q, 4, more_v, 3)
                c.start()
                c.wait()

            for c in loads:
                c.wait()

            @pl.when(q >= 1)
            def _():
                out_copy(q - 1).wait()

            total = own_v[...].astype(F32) + sib_v[...].astype(F32)

            @pl.when(z == 0)
            def _():
                out_v[...] = total + more_v[...].astype(F32)

            @pl.when(z == 3)
            def _():
                out_v[...] = total + in_v[...].astype(F32)

            @pl.when(is_mid)
            def _():
                out_v[...] = total + (in_v[...].astype(F32) + more_v[...].astype(F32))

            out_copy(q).start()

        return carry

    lax.fori_loop(0, chunks + 3, turn, 0)
    out_copy(chunks - 1).wait()

    def finish(q, carry):
        swap(q).wait_send()
        return carry

    lax.fori_loop(0, chunks, finish, 0)
    for slot in range(slots):
        hop(0, slot, 0, z, 0).wait_send()


def line_sum(stack, parts, collective_id):
    m, _, _, rows, cols = stack.shape
    r = rows // parts
    chunks = m * parts
    slots = 3 * min(3, chunks)
    buf = (r, cols)
    out, _, _ = pl.pallas_call(
        functools.partial(line_kernel, parts),
        out_shape=(
            jax.ShapeDtypeStruct((m, rows, cols), F32),
            jax.ShapeDtypeStruct((m, 4, rows, cols), BF16),
            jax.ShapeDtypeStruct((m, 5, rows, cols), BF16),
        ),
        in_specs=[ANY],
        out_specs=(ANY, ANY, ANY),
        scratch_shapes=[pltpu.VMEM(buf, BF16)] * 4
        + [
            pltpu.VMEM((slots,) + buf, BF16),
            pltpu.VMEM(buf, F32),
            pltpu.SemaphoreType.DMA((4,)),
            pltpu.SemaphoreType.DMA,
            pltpu.SemaphoreType.DMA((chunks,)),
            pltpu.SemaphoreType.DMA((chunks,)),
            pltpu.SemaphoreType.DMA((slots,)),
            pltpu.SemaphoreType.DMA((chunks, 5)),
        ],
        compiler_params=pltpu.CompilerParams(
            collective_id=collective_id, has_side_effects=True, vmem_limit_bytes=48 * 2**20
        ),
    )(stack)
    return out


def plane_neighbours():
    f = lax.axis_index("fsdp")
    by_x = f + 1 - 2 * lax.rem(f, 2)
    by_y = f + 2 - 4 * (f // 2)
    return {"fsdp": by_x}, {"fsdp": by_y}


def plane_barrier(by_x, by_y):
    barrier = pltpu.get_barrier_semaphore()
    for other in (by_x, by_y):
        pl.semaphore_signal(barrier, inc=1, device_id=other, device_id_type=MESH)
    pl.semaphore_wait(barrier, 2)


def mid_kernel(middle, chunks, gathers, n_in, n_out, *refs):
    partial, ins = refs[0], refs[1 : 1 + n_in]
    refs = refs[1 + n_in :]
    outs, refs = refs[:n_out], refs[n_out:]
    gathered = None
    if gathers:
        gathered, refs = refs[0], refs[1:]
    relay_x, relay_y, got_x, got_y, sum_x, sum_y, own, send_sems, recv_sems, local_sems = refs
    rows = partial.shape[1]
    r = rows // chunks
    h = r // 2
    by_x, by_y = plane_neighbours()
    plane_barrier(by_x, by_y)

    def copy(i, kind, src, dst, target):
        return pltpu.make_async_remote_copy(
            src_ref=src, dst_ref=dst, send_sem=send_sems.at[i, kind], recv_sem=recv_sems.at[i, kind],
            device_id=target, device_id_type=MESH,
        )

    def sends(i):
        lo, hi = pl.ds(i * r, h), pl.ds(i * r + h, h)
        half = pl.ds(i * h, h)
        made = {
            0: lambda: copy(i, 0, partial.at[3, lo], relay_x.at[half], by_x),
            1: lambda: copy(i, 1, partial.at[3, hi], relay_y.at[half], by_y),
            2: lambda: copy(i, 2, partial.at[1, lo], got_x.at[lo], by_x),
            3: lambda: copy(i, 3, partial.at[2, hi], got_y.at[hi], by_y),
            4: lambda: copy(i, 4, sum_y.at[half], got_y.at[lo], by_y),
            5: lambda: copy(i, 5, sum_x.at[half], got_x.at[hi], by_x),
        }
        if gathers:
            made |= {
                6: lambda: copy(i, 6, own.at[lo], gathered.at[1, lo], by_x),
                7: lambda: copy(i, 7, own.at[hi], gathered.at[2, hi], by_y),
                8: lambda: copy(i, 8, own.at[hi], gathered.at[1, hi], by_x),
                9: lambda: copy(i, 9, own.at[lo], gathered.at[2, lo], by_y),
                10: lambda: copy(i, 10, gathered.at[1, lo], gathered.at[3, lo], by_y),
                11: lambda: copy(i, 11, gathered.at[2, hi], gathered.at[3, hi], by_x),
            }
        return made

    def keep(i):
        span = pl.ds(i * r, r)
        return pltpu.make_async_copy(own.at[span], gathered.at[0, span], local_sems.at[i])

    def stage(n, i):
        s = sends(i)
        lo, hi = pl.ds(i * r, h), pl.ds(i * r + h, h)
        half, span = pl.ds(i * h, h), pl.ds(i * r, r)
        if n == 0:
            for kind in (0, 1, 2, 3):
                s[kind]().start()
        elif n == 1:
            s[0]().wait_recv()
            sum_y[half] = (partial[2, lo].astype(F32) + relay_x[half].astype(F32)).astype(BF16)
            s[4]().start()
            s[1]().wait_recv()
            sum_x[half] = (partial[1, hi].astype(F32) + relay_y[half].astype(F32)).astype(BF16)
            s[5]().start()
        elif n == 2:
            for kind in (2, 3, 4, 5):
                s[kind]().wait_recv()
            total = partial[0, span].astype(F32) + (got_x[span].astype(F32) + got_y[span].astype(F32))
            given = middle(total, span, ins, outs)
            if gathers:
                own[span] = given
                for kind in (6, 7, 8, 9):
                    s[kind]().start()
                keep(i).start()
        elif n == 3 and gathers:
            s[6]().wait_recv()
            s[10]().start()
            s[7]().wait_recv()
            s[11]().start()
        elif n == 4:
            if gathers:
                for kind in (8, 9, 10, 11):
                    s[kind]().wait_recv()
                keep(i).wait()
            for kind in s:
                s[kind]().wait_send()

    for t in range(chunks + 4):
        for n in range(5):
            if 0 <= t - n < chunks:
                stage(n, t - n)


def mid_call(middle, partial, ins, out_shapes, gathers, collective_id, chunks=4):
    _, rows, cols = partial.shape
    outs = tuple(out_shapes)
    specs = (VMEM,) * len(outs)
    if gathers:
        outs += (jax.ShapeDtypeStruct((4, rows, cols), BF16),)
        specs += (ANY,)
    return pl.pallas_call(
        functools.partial(mid_kernel, middle, chunks, gathers, len(ins), len(out_shapes)),
        out_shape=outs,
        in_specs=[VMEM] * (1 + len(ins)),
        out_specs=specs,
        scratch_shapes=[
            pltpu.VMEM((rows // 2, cols), BF16),
            pltpu.VMEM((rows // 2, cols), BF16),
            pltpu.VMEM((rows, cols), BF16),
            pltpu.VMEM((rows, cols), BF16),
            pltpu.VMEM((rows // 2, cols), BF16),
            pltpu.VMEM((rows // 2, cols), BF16),
            pltpu.VMEM((rows, cols), BF16),
            pltpu.SemaphoreType.DMA((chunks, 12)),
            pltpu.SemaphoreType.DMA((chunks, 12)),
            pltpu.SemaphoreType.DMA((chunks,)),
        ],
        compiler_params=pltpu.CompilerParams(
            collective_id=collective_id, has_side_effects=True, vmem_limit_bytes=48 * 2**20
        ),
    )(partial, *ins)


def start_kernel(
    tokens, small, marks, w_q, w_k, w_v,
    tokens_all, small_all, marks_all, w_cols, relay,
    send_sems, recv_sems, local_sems,
):
    f = lax.axis_index("fsdp")
    g = lax.axis_index("grp")
    core = lax.rem(g, 2)
    rows = tokens.shape[0]
    depth = w_q.shape[0]
    width = w_q.shape[1] // 4
    by_x, by_y = plane_neighbours()
    fx, fy = by_x["fsdp"], by_y["fsdp"]
    fd = fx + 2 - 4 * (fx // 2)
    by_d, sibling = {"fsdp": fd}, {"grp": g + 1 - 2 * core}
    barrier = pltpu.get_barrier_semaphore()
    for other in (by_x, by_y, by_d, sibling):
        pl.semaphore_signal(barrier, inc=1, device_id=other, device_id_type=MESH)
    pl.semaphore_wait(barrier, 4)

    def copy(n, src, dst, target):
        return pltpu.make_async_remote_copy(
            src_ref=src, dst_ref=dst, send_sem=send_sems.at[n], recv_sem=recv_sems.at[n],
            device_id=target, device_id_type=MESH,
        )

    def columns(j):
        return pl.ds(pl.multiple_of(j * width, width), width)

    def block_rows(owner, c):
        return pl.ds(pl.multiple_of(owner * depth + c * (depth // 2), depth // 2), depth // 2)

    half = depth // 2
    mine = pl.ds(pl.multiple_of(core * half, half), half)
    all_sends = []

    def go(c):
        c.start()
        all_sends.append(c)
        return c

    waits = []
    n = 0
    for k, target in ((1, by_x), (2, by_y), (3, by_d)):
        waits.append(go(copy(n, small, small_all.at[k], target)))
        waits.append(go(copy(n + 1, marks, marks_all.at[k], target)))
        n += 2
    locals_ = [
        pltpu.make_async_copy(small, small_all.at[0], local_sems.at[0]),
        pltpu.make_async_copy(marks, marks_all.at[0], local_sems.at[1]),
        pltpu.make_async_copy(tokens, tokens_all.at[0], local_sems.at[2]),
    ]
    for j, w in enumerate((w_q, w_k, w_v)):
        locals_.append(
            pltpu.make_async_copy(
                w.at[:, columns(f)],
                w_cols.at[pl.ds(pl.multiple_of(f * depth, depth), depth), pl.ds(j * width, width)],
                local_sems.at[3 + j],
            )
        )
    for c in locals_:
        c.start()

    quarter = half // 2
    first = pl.ds(pl.multiple_of(core * half, quarter), quarter)
    second = pl.ds(pl.multiple_of(core * half + quarter, quarter), quarter)
    relays_x, relays_y, direct_x, direct_y = [], [], [], []
    for j, w in enumerate((w_q, w_k, w_v)):
        relays_x.append(go(copy(n, w.at[first, columns(fd)], relay.at[0, j], by_x)))
        relays_y.append(go(copy(n + 1, w.at[second, columns(fd)], relay.at[1, j], by_y)))
        n += 2
    for j, w in enumerate((w_q, w_k, w_v)):
        place = w_cols.at[block_rows(f, core), pl.ds(j * width, width)]
        direct_x.append(go(copy(n, w.at[mine, columns(fx)], place, by_x)))
        direct_y.append(go(copy(n + 1, w.at[mine, columns(fy)], place, by_y)))
        n += 2
    low, high = pl.ds(0, rows // 2), pl.ds(rows // 2, rows // 2)
    t_x0 = go(copy(n, tokens.at[low], tokens_all.at[1, low], by_x))
    t_y1 = go(copy(n + 1, tokens.at[high], tokens_all.at[2, high], by_y))
    t_x1 = go(copy(n + 2, tokens.at[high], tokens_all.at[1, high], by_x))
    t_y0 = go(copy(n + 3, tokens.at[low], tokens_all.at[2, low], by_y))
    n += 4
    forwarded = []
    for j in range(3):
        relays_x[j].wait_recv()
        forwarded.append(
            go(copy(
                n, relay.at[0, j],
                w_cols.at[pl.ds(pl.multiple_of(fx * depth + core * half, quarter), quarter), pl.ds(j * width, width)],
                by_y,
            ))
        )
        relays_y[j].wait_recv()
        forwarded.append(
            go(copy(
                n + 1, relay.at[1, j],
                w_cols.at[pl.ds(pl.multiple_of(fy * depth + core * half + quarter, quarter), quarter), pl.ds(j * width, width)],
                by_x,
            ))
        )
        n += 2
    shares = []

    def share(owner):
        nonlocal n
        place = w_cols.at[block_rows(owner, core)]
        shares.append(go(copy(n, place, place, sibling)))
        n += 1

    for c in direct_x:
        c.wait_recv()
    share(fx)
    for c in direct_y:
        c.wait_recv()
    share(fy)
    t_x0.wait_recv()
    t_d0 = go(copy(n, tokens_all.at[1, low], tokens_all.at[3, low], by_y))
    t_y1.wait_recv()
    t_d1 = go(copy(n + 1, tokens_all.at[2, high], tokens_all.at[3, high], by_x))
    n += 2
    for c in forwarded:
        c.wait_recv()
    share(fd)
    for c in waits + shares + [t_x1, t_y0, t_d0, t_d1]:
        c.wait_recv()
    for c in locals_:
        c.wait()
    for c in all_sends:
        c.wait_send()


def start_call(tokens, small, marks, w_q, w_k, w_v, collective_id):
    depth, features = w_q.shape
    width = features // 4
    n = 6 + 6 + 6 + 4 + 6 + 2 + 3
    return pl.pallas_call(
        start_kernel,
        out_shape=(
            jax.ShapeDtypeStruct((4,) + tokens.shape, tokens.dtype),
            jax.ShapeDtypeStruct((4,) + small.shape, small.dtype),
            jax.ShapeDtypeStruct((4,) + marks.shape, marks.dtype),
            jax.ShapeDtypeStruct((4 * depth, 3 * width), BF16),
            jax.ShapeDtypeStruct((2, 3, depth // 4, width), BF16),
        ),
        in_specs=[ANY] * 6,
        out_specs=(ANY,) * 5,
        scratch_shapes=[
            pltpu.SemaphoreType.DMA((n,)),
            pltpu.SemaphoreType.DMA((n,)),
            pltpu.SemaphoreType.DMA((6,)),
        ],
        compiler_params=pltpu.CompilerParams(
            collective_id=collective_id, has_side_effects=True, vmem_limit_bytes=16 * 2**20
        ),
    )(tokens, small, marks, w_q, w_k, w_v)[:4]


def dot(left, right, dims, out=F32):
    return lax.dot_general(left, right, (dims, ((), ())), preferred_element_type=out)


def rows_dot(left, right):
    return dot(left, right, ((0,), (0,)))


def plain_dot(left, right):
    return dot(left, right, ((1,), (0,)))


def trans_dot(left, right):
    return dot(left, right, ((1,), (1,)))


def silu_pair(value):
    sigma = jax.nn.sigmoid(value)
    return value * sigma, sigma * (1.0 + value * (1.0 - sigma))


def angles(position):
    halfway = HEAD_DIM // 2
    freqs = ROPE_BASE ** (-(jnp.arange(halfway, dtype=F32) * 2.0 / HEAD_DIM))
    turns = position.astype(F32)[:, None] * freqs[None, :]
    return jnp.cos(turns)[:, None, :], jnp.sin(turns)[:, None, :]


def rotate(field, cosine, sine):
    halfway = field.shape[-1] // 2
    first, second = field[..., :halfway], field[..., halfway:]
    return jnp.concatenate(
        [first * cosine - second * sine, second * cosine + first * sine], axis=-1
    )


def two_parts(value):
    high = value.astype(BF16)
    return high, (value - high.astype(F32)).astype(BF16)


class Load:
    def __init__(self, value):
        self.value = value

    def __getitem__(self, place):
        return self.value[place]


class Store:
    def __init__(self, shape):
        self.value = jnp.zeros(shape.shape, shape.dtype)

    def __getitem__(self, place):
        return self.value[place]

    def __setitem__(self, place, value):
        self.value = value.astype(self.value.dtype)


def first_middle(total, span, ins, outs):
    tokens, gain = ins
    mixed = tokens[span].astype(F32) + total
    factor = lax.rsqrt(jnp.mean(mixed * mixed, axis=-1, keepdims=True) + EPSILON)
    outs[0][span] = mixed
    return (mixed * factor * gain[...]).astype(BF16)


def norm_back(values, gain, grad):
    factor = lax.rsqrt(jnp.mean(values * values, axis=-1, keepdims=True) + EPSILON)
    weighted = gain * grad
    back = factor * weighted - values * (factor * factor * factor) * jnp.mean(
        weighted * values, axis=-1, keepdims=True
    )
    return back, jnp.sum(grad * values * factor, axis=0, keepdims=True)


def back_middle(total, span, ins, outs):
    values, gain, base = ins
    back, grad_gain = norm_back(values[span].astype(F32), gain[...], total)
    grad = base[span].astype(F32) + back
    outs[0][span] = grad
    outs[1][span if span == slice(None) else pl.ds(span.start // span.size, 1)] = grad_gain
    return grad.astype(BF16)


class Wires:
    def __init__(self, mesh):
        self.nf = mesh.shape["fsdp"]
        self.ng = mesh.shape["grp"]
        self.nz = self.ng // 2
        self.fast = self.nf == 4 and self.ng == 8
        self.chunks = 4 if self.fast else 1

    def xor(self, value, k):
        return lax.ppermute(value, "fsdp", [(i, i ^ k) for i in range(self.nf)])

    def gather_list(self, value):
        return [value] + [self.xor(value, k) for k in range(1, self.nf)]

    def gather(self, value):
        return jnp.concatenate(self.gather_list(value), axis=0)

    def scatter_sum(self, value):
        rows = value.shape[0] // self.nf
        total = value[:rows]
        for k in range(1, self.nf):
            part = value[k * rows : (k + 1) * rows].astype(BF16)
            total = total + self.xor(part, k).astype(F32)
        return total

    def core_swap(self, value):
        return lax.ppermute(value, "grp", [(i, i ^ 1) for i in range(self.ng)])

    def core_sum(self, partial):
        core = lax.rem(lax.axis_index("grp"), 2)
        mine = lax.dynamic_index_in_dim(partial, core, 1, keepdims=False)
        other = lax.dynamic_index_in_dim(partial, 1 - core, 1, keepdims=False)
        got = self.core_swap(other)
        return (mine.astype(F32) + got.astype(F32)).astype(BF16)

    def line_sum(self, pieces):
        nz = self.nz
        z = lax.axis_index("grp") // 2

        def move(value, up, step):
            pairs = []
            for a in range(nz):
                b = a + 1 if up else a - 1
                sends = a < step if up else a > nz - 1 - step
                if sends and 0 <= b < nz:
                    pairs += [(2 * a + c, 2 * b + c) for c in (0, 1)]
            return lax.ppermute(value, "grp", pairs)

        ups = downs = None
        for step in range(1, nz):
            up_own = pieces(jnp.clip(z + nz - step, 0, nz - 1))
            down_own = pieces(jnp.clip(z - nz + step, 0, nz - 1))
            up_send = up_own if ups is None else (up_own.astype(F32) + ups.astype(F32)).astype(BF16)
            down_send = (
                down_own if downs is None else (down_own.astype(F32) + downs.astype(F32)).astype(BF16)
            )
            ups = move(up_send, True, step)
            downs = move(down_send, False, step)
        return pieces(z).astype(F32) + ups.astype(F32) + downs.astype(F32)

    def reduce_background(self, partial):
        return lax.psum_scatter(
            partial.astype(BF16), "grp", scatter_dimension=0, tiled=True
        ).astype(F32)

    def line_stack(self, stack, parts, number):
        if self.fast:
            return line_sum(stack, parts, number)
        m, nz, _, rows, cols = stack.shape
        flat = stack.reshape(m, nz * 2 * rows, cols)
        return lax.psum_scatter(flat, "grp", scatter_dimension=1, tiled=True).astype(F32)

    def gather_start(self, tokens, small, marks, weights):
        if self.fast:
            return start_call(tokens, small, marks, *weights, 1)
        width = tokens.shape[1] // self.nf
        cols = jnp.concatenate(
            [lax.all_to_all(w, "fsdp", split_axis=1, concat_axis=0, tiled=True) for w in weights],
            axis=1,
        )
        assert cols.shape[1] == 3 * width
        return tuple(jnp.stack(self.gather_list(v)) for v in (tokens, small, marks)) + (cols,)

    def middle(self, body, partial, ins, out_shapes, gathers, number):
        nf = self.nf
        rows, cols = partial.shape[0] // nf, partial.shape[1]
        if self.fast:
            return mid_call(
                body, partial.astype(BF16).reshape(nf, rows, cols), ins, out_shapes, gathers, number
            )
        total = self.scatter_sum(partial)
        outs = [Store(s) for s in out_shapes]
        given = body(total, slice(None), [Load(v) for v in ins], outs)
        results = tuple(o.value for o in outs)
        if gathers:
            results += (jnp.stack(self.gather_list(given)),)
        return results

    def reduce_rows(self, partial):
        rows = partial.shape[0] // self.ng
        partial = partial.astype(BF16).reshape((self.nz, 2, rows) + partial.shape[1:])
        acc = self.core_sum(partial)
        return self.line_sum(lambda i: lax.dynamic_index_in_dim(acc, i, 0, keepdims=False))


def on_device(
    wires,
    tokens,
    cotangent,
    segment,
    ancestry,
    position,
    routes,
    attn_gain,
    w_query,
    w_key,
    w_value,
    b_query,
    b_key,
    b_value,
    w_output,
    moe_gain,
    w_router,
    shared_switch,
    shared_gate,
    shared_up,
    shared_down,
    expert_gate,
    routed_up_weight,
    expert_down,
):
    nf, ng, nz = wires.nf, wires.ng, wires.nz
    me = lax.axis_index("fsdp")
    rows_dev, features = tokens.shape
    count = rows_dev * nf
    width = features // nf
    heads = width // HEAD_DIM
    experts = w_router.shape[1]
    local_experts = experts // nf
    capacity = 5 * rows_dev // 8
    inv_root = HEAD_DIM ** (-0.5)

    small = jnp.concatenate([attn_gain[None], moe_gain[None], w_router.T, shared_switch[None]], axis=0)
    small = jnp.pad(small, ((0, -small.shape[0] % 16), (0, 0)))
    marks = jnp.concatenate([segment[None], ancestry.T, position[None], routes.T], axis=0)
    marks = jnp.pad(marks, ((0, -marks.shape[0] % 16), (0, 0)))
    tokens_all, small_blocks, marks_all, w_cols = wires.gather_start(
        tokens, small, marks, (w_query, w_key, w_value)
    )
    tokens_all = tokens_all.reshape(count, features)
    small_all = jnp.concatenate(
        [lax.dynamic_index_in_dim(small_blocks, me ^ i, 0, keepdims=False) for i in range(nf)], axis=1
    )
    gain_one = small_all[0:1].astype(F32)
    gain_two = small_all[1:2].astype(F32)
    heads_w = small_all[2 : experts + 3].T
    marks_all = jnp.concatenate([marks_all[k] for k in range(nf)], axis=1)
    seg_all, anc_all, pos_all = marks_all[0], marks_all[1:4].T, marks_all[4]
    routes_all = marks_all[5 : 5 + routes.shape[1]].T

    tokens_all, cotangent = lax.optimization_barrier((tokens_all, cotangent))
    cot_all = wires.gather(cotangent)

    tokens_all_f = tokens_all.astype(F32)
    factor_all = lax.rsqrt(jnp.mean(tokens_all_f * tokens_all_f, axis=-1, keepdims=True) + EPSILON)
    normed = (tokens_all_f * factor_all * gain_one).astype(BF16)
    bias = jnp.concatenate([b_query, b_key, b_value]).astype(F32)
    three = plain_dot(normed, w_cols) + bias
    cosine, sine = angles(pos_all)

    def heads_of(x):
        return x.reshape(count, heads, HEAD_DIM)

    query = rotate(heads_of(three[:, :width]), cosine, sine).astype(BF16)
    keys = rotate(heads_of(three[:, width : 2 * width]), cosine, sine).astype(BF16)
    values = heads_of(three[:, 2 * width :]).astype(BF16)
    visible = (
        (seg_all[None, :] == anc_all[:, 0:1])
        | (seg_all[None, :] == anc_all[:, 1:2])
        | (seg_all[None, :] == anc_all[:, 2:3])
    ) & (pos_all[None, :] <= pos_all[:, None])
    scores = jnp.einsum("qhd,khd->hqk", query, keys, preferred_element_type=F32) * inv_root
    masked = jnp.where(visible[None], scores, MASK_FILL)
    peak = jnp.max(masked, axis=-1, keepdims=True)
    expo = jnp.exp(masked - peak)
    total = jnp.sum(expo, axis=-1, keepdims=True)
    log_total = peak + jnp.log(total)
    weights = (expo / total).astype(BF16)
    attended = (
        jnp.einsum("hqk,khd->qhd", weights, values, preferred_element_type=F32)
        .reshape(count, width)
        .astype(BF16)
    )
    mixed, moe_in = wires.middle(
        first_middle,
        plain_dot(attended, w_output),
        (tokens, gain_two),
        (jax.ShapeDtypeStruct((rows_dev, features), F32),),
        True,
        2,
    )
    moe_in = moe_in.reshape(count, features)

    head_pre = plain_dot(moe_in, heads_w)
    router_probs = jax.nn.softmax(head_pre[:, :experts], axis=-1)
    opener = jax.nn.sigmoid(head_pre[:, experts:])
    cot_f = cot_all.astype(F32)

    gate_pre = plain_dot(moe_in, shared_gate)
    up_pre = plain_dot(moe_in, shared_up)
    gate_act, gate_slope = silu_pair(gate_pre)
    shared_hidden = (gate_act * up_pre).astype(BF16)
    shared_grad = (opener * cot_f).astype(BF16)
    grad_shidden = trans_dot(shared_grad, shared_down)
    part_sdown = rows_dot(shared_grad, shared_hidden).astype(BF16)
    grad_sgate_pre = (grad_shidden * up_pre * gate_slope).astype(BF16)
    grad_sup_pre = (grad_shidden * gate_act).astype(BF16)
    part_sgate = rows_dot(moe_in, grad_sgate_pre).astype(BF16)
    part_sup = rows_dot(moe_in, grad_sup_pre).astype(BF16)
    gate_sens = (1.0 - opener) * jnp.sum(
        grad_shidden * shared_hidden.astype(F32), axis=-1, keepdims=True
    )
    out_part = opener * plain_dot(shared_hidden, shared_down)
    moe_part = trans_dot(grad_sgate_pre, shared_gate) + trans_dot(grad_sup_pre, shared_up)

    out_part, part_sdown, part_sgate, part_sup = lax.optimization_barrier(
        (out_part, part_sdown, part_sgate, part_sup)
    )
    final_sdown = wires.reduce_background(part_sdown)
    final_sgate = wires.reduce_background(part_sgate)
    final_sup = wires.reduce_background(part_sup)

    moe_blocks = moe_in.reshape(nf, rows_dev, features)
    cot_blocks = cot_all.reshape(nf, rows_dev, features)
    earlier = (
        jnp.arange(rows_dev)[None, :] < jnp.arange(rows_dev)[:, None]
    ).astype(BF16)
    lanes = jnp.arange(experts, dtype=jnp.int32)[None, :]
    prob_grad = jnp.zeros((count, experts), F32)
    parts = []
    for i in range(local_experts):
        number = me * local_experts + i
        named = jnp.any(routes_all == number, axis=1)
        named_blocks = named.reshape(nf, rows_dev)
        slot = jnp.einsum(
            "ts,bs->bt", earlier, named_blocks.astype(BF16), preferred_element_type=F32
        ).astype(jnp.int32)
        pick = (
            jnp.arange(capacity, dtype=jnp.int32)[None, :, None] == slot[:, None, :]
        ) & named_blocks[:, None, :]
        pick_b = pick.astype(BF16)

        def dispatch(x):
            return (
                jnp.einsum("bst,btd->bsd", pick_b, x, preferred_element_type=F32)
                .astype(BF16)
                .reshape(nf * capacity, features)
            )

        def collect(x):
            return jnp.einsum(
                "bst,bsd->btd", pick_b, x.reshape(nf, capacity, -1), preferred_element_type=F32
            ).reshape(count, -1)

        here = lanes == number
        prob_here = jnp.sum(jnp.where(here, router_probs, 0.0), axis=1)
        gate = jnp.sum(
            jnp.where(pick, prob_here.reshape(nf, 1, rows_dev), 0.0), axis=2
        ).reshape(nf * capacity, 1)
        rows_in = dispatch(moe_blocks)
        cot_rows = dispatch(cot_blocks)
        deout = (gate * cot_rows.astype(F32)).astype(BF16)
        egate = plain_dot(rows_in, expert_gate[i])
        eup = plain_dot(rows_in, routed_up_weight[i])
        act, slope = silu_pair(egate)
        hidden = (act * eup).astype(BF16)
        plain_hidden = trans_dot(cot_rows, expert_down[i])
        grad_hidden = gate * plain_hidden
        part_down = rows_dot(deout, hidden).astype(BF16)
        grad_gate_pre = (grad_hidden * eup * slope).astype(BF16)
        grad_up_pre = (grad_hidden * act).astype(BF16)
        part_gate = rows_dot(rows_in, grad_gate_pre).astype(BF16)
        part_up = rows_dot(rows_in, grad_up_pre).astype(BF16)
        parts += [part_gate, part_up, part_down]
        eout = plain_dot(hidden, expert_down[i]).astype(BF16)
        out_part = out_part + collect((gate * eout.astype(F32)).astype(BF16))
        grad_in = trans_dot(grad_gate_pre, expert_gate[i]) + trans_dot(
            grad_up_pre, routed_up_weight[i]
        )
        moe_part = moe_part + collect(grad_in.astype(BF16))
        gate_grad = jnp.sum(plain_hidden * hidden.astype(F32), axis=-1)
        gate_grad = jnp.sum(
            jnp.where(pick, gate_grad.reshape(nf, capacity, 1), 0.0), axis=1
        ).reshape(count, 1)
        prob_grad = prob_grad + jnp.where(here, gate_grad, 0.0)

    logit_grad = router_probs * (
        prob_grad - jnp.sum(prob_grad * router_probs, axis=-1, keepdims=True)
    )
    high, lower = two_parts(jnp.concatenate([logit_grad, gate_sens], axis=1))
    sens = jnp.concatenate([high, lower], axis=1)
    moe_part = moe_part + trans_dot(sens, jnp.concatenate([heads_w, heads_w], axis=1))
    grad_heads = rows_dot(moe_in, sens)
    grad_heads = grad_heads[:, : experts + 1] + grad_heads[:, experts + 1 :]

    grad_mixed, grad_gain_two, branch_grad = wires.middle(
        back_middle,
        moe_part,
        (mixed, gain_two, cotangent),
        (
            jax.ShapeDtypeStruct((rows_dev, features), F32),
            jax.ShapeDtypeStruct((wires.chunks, features), F32),
        ),
        True,
        3,
    )
    grad_gain_two = jnp.sum(grad_gain_two, axis=0)
    branch_grad = branch_grad.reshape(count, features)

    grad_attended = heads_of(trans_dot(branch_grad, w_output).astype(BF16))
    probs = jnp.exp(masked - log_total)
    weight_grad = jnp.einsum("qhd,khd->hqk", grad_attended, values, preferred_element_type=F32)
    diagonal = jnp.sum(probs * weight_grad, axis=-1, keepdims=True)
    score_grad = (probs * (weight_grad - diagonal)).astype(BF16)
    grad_query = jnp.einsum("hqk,khd->qhd", score_grad, keys, preferred_element_type=F32) * inv_root
    grad_keys = jnp.einsum("hqk,qhd->khd", score_grad, query, preferred_element_type=F32) * inv_root
    grad_values = jnp.einsum("hqk,qhd->khd", weights, grad_attended, preferred_element_type=F32)
    grad_qpre = rotate(grad_query, cosine, -sine).reshape(count, width).astype(BF16)
    grad_kpre = rotate(grad_keys, cosine, -sine).reshape(count, width).astype(BF16)
    grad_vpre = grad_values.reshape(count, width).astype(BF16)
    grad_three = jnp.concatenate([grad_qpre, grad_kpre, grad_vpre], axis=1)
    grad_bias = jnp.sum(grad_three.astype(F32), axis=0)

    grad_tokens, grad_gain_one = wires.middle(
        back_middle,
        trans_dot(grad_three, w_cols),
        (tokens, gain_one, grad_mixed),
        (
            jax.ShapeDtypeStruct((rows_dev, features), F32),
            jax.ShapeDtypeStruct((wires.chunks, features), F32),
        ),
        False,
        4,
    )
    grad_gain_one = jnp.sum(grad_gain_one, axis=0)

    part_output = rows_dot(branch_grad, attended).astype(BF16)
    part_three = rows_dot(grad_three, normed).astype(BF16).reshape(3 * width, nf, width)
    owned = []
    for k in range(nf):
        part = lax.dynamic_index_in_dim(part_three, me ^ k, 1, keepdims=False)
        owned.append(wires.xor(part, k) if k else part)
    out_total = wires.scatter_sum(out_part)

    ngz = (nz, 2, features // ng)
    stack = jnp.stack(parts, axis=0).reshape((3 * local_experts,) + ngz + (-1,))
    stack, final_sdown, final_sgate, final_sup, grad_tokens = lax.optimization_barrier(
        (stack, final_sdown, final_sgate, final_sup, grad_tokens)
    )
    sums = wires.line_stack(stack, 2, 5).reshape((local_experts, 3) + (features // ng, -1))
    output = (mixed + out_total).astype(BF16)
    owned = jnp.stack(owned, axis=0).reshape((nf, 3, 2, width // 2, width))
    owned = jnp.stack(
        [lax.dynamic_index_in_dim(owned, me ^ i, 0, keepdims=False) for i in range(nf)], axis=1
    )
    small_stack = jnp.concatenate(
        [owned, part_output.reshape((1,) + ngz + (width,))], axis=0
    )
    small_stack, sums = lax.optimization_barrier((small_stack, sums))
    attn = wires.line_stack(small_stack, 1, 6).transpose(0, 2, 1)

    vectors = jnp.concatenate(
        [grad_gain_one[:, None], grad_gain_two[:, None], grad_heads], axis=1
    )
    vectors = lax.psum_scatter(vectors, "fsdp", scatter_dimension=0, tiled=True)
    vectors = jnp.concatenate([vectors, grad_bias.reshape(3, width).T], axis=1)
    vectors = lax.psum_scatter(vectors, "grp", scatter_dimension=0, tiled=True)
    return (
        output,
        grad_tokens,
        vectors[:, 0],
        attn[0],
        attn[1],
        attn[2],
        vectors[:, experts + 3],
        vectors[:, experts + 4],
        vectors[:, experts + 5],
        attn[3],
        vectors[:, 1],
        vectors[:, 2 : experts + 2],
        vectors[:, experts + 2],
        final_sgate,
        final_sup,
        final_sdown.T,
        sums[:, 0],
        sums[:, 1],
        sums[:, 2].transpose(0, 2, 1),
    )


def solution(mesh):
    wires = Wires(mesh)

    def step(*args):
        return on_device(wires, *args)

    rows = P(("grp", "fsdp"))
    shard = P("fsdp")
    small = P(("fsdp", "grp"))
    return jax.shard_map(
        step,
        mesh=mesh,
        in_specs=(rows,) * 6
        + (shard,) * 11
        + (P(None, "fsdp"), P(None, "fsdp"), shard, shard, shard, shard),
        out_specs=(
            rows,
            rows,
            small,
            P("fsdp", "grp"),
            P("fsdp", "grp"),
            P("fsdp", "grp"),
            small,
            small,
            small,
            P("fsdp", "grp"),
            small,
            small,
            small,
            P("grp", "fsdp"),
            P("grp", "fsdp"),
            P("fsdp", "grp"),
            P("fsdp", "grp", None),
            P("fsdp", "grp", None),
            P("fsdp", None, "grp"),
        ),
        check_vma=False,
    )
```

time: 2390 us -> 1340 us (0.56)
  waiting for transfers between devices: 1550 us -> 62.5 us
  Pallas kernels: 0 us -> 638 us
  blocking collectives: 156 us -> 0 us
    all_gather x14 -> x0, waiting for transfers between devices: 655 us -> none  [the longest x1 83.4 us: on_device(): lax.all_gather(w_key, 'fsdp', axis=0, tiled=True)]
    reduce_scatter x14 -> x4, waiting for transfers between devices: 704 us -> 54.2 us  [the longest x3 32.2 us: reduce_background(): lax.psum_scatter(partial.astype(BF16), 'grp', scatter_dimension=0, tiled=...]
    pallas_call x0 -> x6, Pallas kernels: none -> 638 us  [the longest x2 384 us: line_sum(): pl.pallas_call(functools.partial(line_kernel, parts), out_shape=(jax.Shap...]
    all_to_all x4 -> x0, waiting for transfers between devices: 158 us -> none  [the longest x1 75 us: on_device(): lax.all_to_all(grad_ein, 'fsdp', split_axis=1, concat_axis=0, tiled=True)]
    all_gather x9 -> x0, blocking collectives: 126 us -> none  [the longest x1 61.6 us: on_device(): lax.all_gather(shared_switch, 'fsdp', axis=0, tiled=True)]
    gather x5 -> x0, local copies, waits for them, and re-layouts: 45.4 us -> none  [the longest x1 12.9 us: on_device(): grad_back.reshape(experts * capacity, features)[target]]
    unnamed x210 -> x260, local copies, waits for them, and re-layouts: 24.1 us -> 68.3 us
    all_to_all x4 -> x0, local copies, waits for them, and re-layouts: 30.3 us -> none  [the longest x1 13.9 us: on_device(): lax.all_to_all(grad_ein, 'fsdp', split_axis=1, concat_axis=0, tiled=True)]
  transfers between devices with their start and end apart: 33 -> 14, of which waited for: 28 -> 3; matrix products, arithmetic and copies ran while one was open for 21% -> 23% of each run, Pallas kernels for 0% -> 5%
where the time goes in v1:
time: 1340 us; the launch traced here: 1320 us
  Pallas kernels  638 us (48%)
  matrix products  359 us (27%)
  local copies, waits for them, and re-layouts  148 us (11%)
  other arithmetic  89.7 us (7%)
  waiting for transfers between devices  62.5 us (5%)
  between operations  15.6 us (1%)
    pallas_call x2, Pallas kernels, line_sum(): pl.pallas_call(functools.partial(line_kernel, parts), out_shape=(jax.Shap...  384 us
    dot_general x36, matrix products, dot(): lax.dot_general(left, right, (dims, ((), ())), preferred_element_type=out)  293 us
    pallas_call x3, Pallas kernels, mid_call(): pl.pallas_call(functools.partial(mid_kernel, middle, chunks, gathers, len...  179 us
    pallas_call x1, Pallas kernels, start_call(): pl.pallas_call(start_kernel, out_shape=(jax.ShapeDtypeStruct((4,) + token...  74.4 us
    unnamed x260, local copies, waits for them, and re-layouts  68.3 us
    reduce_scatter x3, waiting for transfers between devices, reduce_background(): lax.psum_scatter(partial.astype(BF16), 'grp', scatter_dimension=0, tiled=...  32.2 us
  transfers between devices with their start and end apart: 14, of which 3 were waited for; matrix products, arithmetic and copies ran while one was open for 23% of the time, Pallas kernels for 5%

profile of v1, /device:TPU:0, one launch (start us, length us, event | category | flops | bytes accessed | tf_op | source)
XLA Modules:
  0.0 1323.1 jit_solution(1153679800481045273)
XLA Ops:
  16.9 74.4 %shard_map.366 = (bf16[4,256,2048]{2,1,0:T(8,128)(2,1)S(1)}, bf16[4,16,512]{2,1,0:T(8,128)(2,1)S(1)}, s32[4,16,256]{2,1,0:T(8,128)S(1)}, bf16[2048,1536]{1,0:T(8,128)(2,1)S(1)}, bf16[2,3,128,512]{3,2,1,0:T(8,128)(2,1)}) custom-call(bf16[256,2048]{1,0:T(8,128)(2,1)S(1)} %copy-done.2, bf16[16,512]{1,0:T(8,128)(2,1)S(1)} %fusion.120.small, ...), custom_call_target="tpu_custom_call" | custom-call | tf_op jit(solution)/shard_map/pallas_call | solution.py:519
  102.7 10.1 convolution_add_fusion
  122.7 6.0 fusion.135
  134.2 8.5 fusion.139
  142.7 8.0 fusion
  150.7 7.2 divide_convert_fusion
  165.5 5.7 convolution_convert_fusion.11
  171.2 71.6 %shard_map.367 = (f32[256,2048]{1,0:T(8,128)S(1)}, bf16[4,256,2048]{2,1,0:T(8,128)(2,1)}) custom-call(bf16[4,256,2048]{2,1,0:T(8,128)(2,1)} %bitcast.313, bf16[256,2048]{1,0:T(8,128)(2,1)S(1)} %copy-done.3, f32[1,2048]{1,0:T(1,128)S(1)} %get-tuple-element.182.refs_2_), custom_call_target="tpu_custom_call" | custom-call | tf_op jit(solution)/shard_map/pallas_call | solution.py:361
  246.7 9.7 fusion.24
  256.4 6.1 fusion.28
  265.9 10.0 fusion.12
  276.0 6.1 fusion.16
  283.4 8.5 fusion.140
  291.9 8.6 fusion.141
  312.3 9.7 multiply_reduce_fusion.3
  322.3 12.3 multiply_reduce_fusion.2
  335.1 16.8 %multiply_reduce_fusion.1 = (f32[1024]{0:T(1024)S(1)}, bf16[1024,1408]{1,0:T(8,128)(2,1)}, bf16[1024,1408]{1,0:T(8,128)(2,1)}, bf16[1024,1408]{1,0:T(8,128)(2,1)}) fusion(f32[1024,1408]{1,0:T(8,128)} %fusion.141, f32[1024,1408]{1,0:T(8,128)} %fusion.140, bf16[1408,2048]{1,0:T(8,128)(2,1)} %param.42, bf16[1024,2048]{1,0:T(8,128)(2,1)} %copy-done.22, ...), kind=kOutput, calls=%fused_computation.56 | convolution fusion | flops 5937822720 | bytes 30154752 | tf_op jit(solution)/shard_map/dot_general | solution.py:542
  357.6 10.2 fusion.22
  367.9 6.3 add_convert_fusion.1
  379.1 5.3 multiply_convert_fusion.9
  384.5 10.2 fusion.10
  394.7 6.4 add_convert_fusion
  406.2 10.9 fusion.142
  417.1 9.1 fusion.143
  426.2 13.9 %fusion.5 = bf16[1024,2048]{1,0:T(8,128)(2,1)} fusion(f32[4,256,2048]{2,1,0:T(8,128)} %fusion.82, f32[4,256,2048]{2,1,0:T(8,128)} %fusion.75, f32[1024,2048]{1,0:T(8,128)} %fusion.142, f32[1024,2048]{1,0:T(8,128)} %fusion.143, bf16[2048,9]{0,1:T(8,128)(2,1)S(1)} %fusion.122, bf16[1024,9]{0,1:T(8,128)(2,1)S(1)} %fusion.110, bf16[1024,9]{0,1:T(8,128)(2,1)S(1)} %fusion.109), kind=kOutput, calls=%fused_computation.15 | convolution fusion | flops 86204416 | bytes 37822464 | tf_op jit(solution)/shard_map/dot_general | solution.py:542
  440.1 70.8 %shard_map.368 = (f32[256,2048]{1,0:T(8,128)S(1)}, f32[4,2048]{1,0:T(4,128)S(1)}, bf16[4,256,2048]{2,1,0:T(8,128)(2,1)}) custom-call(bf16[4,256,2048]{2,1,0:T(8,128)(2,1)} %bitcast.281, f32[256,2048]{1,0:T(8,128)S(1)} %copy-done.6, f32[1,2048]{1,0:T(1,128)S(1)} %get-tuple-element.182.refs_2_, bf16[256,2048]{1,0:T(8,128)(2,1)S(1)} %copy-done.9), custom_call_target="tpu_custom_call" | custom-call | tf_op jit(solution)/shard_map/pallas_call | solution.py:361
  510.9 5.3 convolution_convert_fusion.18
  516.3 11.5 multiply_reduce_fusion
  527.9 12.6 multiply_convert_fusion
  552.8 8.6 convolution_convert_fusion.7
  561.5 11.3 convolution_convert_fusion.8
  582.5 11.3 convolution_convert_fusion.9
  593.9 11.5 convolution_convert_fusion.10
  605.4 37.1 %shard_map.369 = (f32[256,2048]{1,0:T(8,128)S(1)}, f32[4,2048]{1,0:T(4,128)S(1)}) custom-call(bf16[4,256,2048]{2,1,0:T(8,128)(2,1)} %bitcast.320, bf16[256,2048]{1,0:T(8,128)(2,1)S(1)} %copy-done.4, f32[1,2048]{1,0:T(1,128)S(1)} %copy-done.17, f32[256,2048]{1,0:T(8,128)S(1)} %copy-done.15), custom_call_target="tpu_custom_call" | custom-call | tf_op jit(solution)/shard_map/pallas_call | solution.py:361
  646.8 22.0 %reduce-scatter.14.cloned.1.call-done = f32[512,11]{0,1:T(8,128)} async-done(((f32[2048,11]{0,1:T(8,128)}), f32[512,11]{0,1:T(8,128)}) %reduce-scatter.14.cloned.1.call-update) | async-done | bytes 22544 | tf_op jit(solution)/shard_map/reduce_scatter | solution.py:1001
  670.5 10.8 convolution_multiply_fusion
  683.2 13.7 %convolution_convert_fusion = bf16[1536,2048]{1,0:T(8,128)(2,1)} fusion(bf16[1024,2048]{1,0:T(8,128)(2,1)} %bitcast.265, f32[2048]{0:T(1024)S(1)} %bitcast.268, f32[1024]{0:T(1024)S(1)} %copy-done.76, bf16[1024,512]{0,1:T(8,128)(2,1)S(1)} %bitcast.312, bf16[1024,512]{0,1:T(8,128)(2,1)S(1)} %bitcast.319, bf16[1024,512]{0,1:T(8,128)(2,1)S(1)} %bitcast.316), kind=kOutput, calls=%fused_computation.20 | convolution fusion | flops 6463422464 | bytes 13643776 | tf_op jit(solution)/shard_map/dot_general | solution.py:542
  696.8 11.2 reshape.464
  708.1 20.1 %constant_dynamic-slice_fusion.3 = (bf16[1536,1,512]{2,1,0:T(2,128)(2,1)S(1)}, bf16[1536,1,512]{2,1,0:T(2,128)(2,1)S(1)}, bf16[1536,1,512]{2,1,0:T(2,128)(2,1)S(1)}, bf16[1536,1,512]{2,1,0:T(2,128)(2,1)S(1)}) fusion(bf16[1536,4,512]{2,1,0:T(4,128)(2,1)} %reshape.464, s32[]{:T(128)S(6)} %select_n.55, s32[]{:T(128)S(6)} %select_n.57, s32[]{:T(128)S(6)} %select_n.56, ...), kind=kLoop, calls=%fused_computation.259 | loop fusion | bytes 12582928 | tf_op jit(solution)/shard_map/jit(dynamic_index_in_dim)/dynamic_slice | solution.py:977
  755.3 13.9 %fusion.132 = (bf16[1024,2048]{1,0:T(8,128)(2,1)S(1)}, f32[1024,2048]{1,0:T(8,128)}) fusion(f32[4,256,2048]{2,1,0:T(8,128)} %fusion.85, f32[1024,2048]{1,0:T(8,128)} %convolution_multiply_fusion, f32[4,256,2048]{2,1,0:T(8,128)} %fusion.78), kind=kLoop, calls=%fused_computation.269 | loop fusion | flops 6291456 | bytes 37748736 | tf_op jit(solution)/shard_map/convert.6
  790.7 5.7 convolution_convert_fusion.4
  818.6 5.7 convolution_convert_fusion.1
  840.9 7.7 collective-permute-done.5
  866.0 32.2 %reduce-scatter.12.cloned.1.call-done = bf16[256,1408]{1,0:T(8,128)(2,1)} async-done(((bf16[2048,1408]{1,0:T(8,128)(2,1)}), bf16[256,1408]{1,0:T(8,128)(2,1)}) %reduce-scatter.12.cloned.1.call-update) | async-done | bytes 720912 | tf_op jit(solution)/shard_map/reduce_scatter | solution.py:688
  900.5 299.6 %shard_map.370 = (f32[6,256,1408]{2,1,0:T(8,128)}, bf16[6,4,256,1408]{3,2,1,0:T(8,128)(2,1)}, bf16[6,5,256,1408]{3,2,1,0:T(8,128)(2,1)}) custom-call(bf16[6,4,2,256,1408]{4,3,2,1,0:T(8,128)(2,1)} %constant_dynamic-update-slice_fusion.4.stack), custom_call_target="tpu_custom_call" | custom-call | tf_op jit(solution)/shard_map/pallas_call | solution.py:224
  1200.2 9.1 copy.117
  1209.3 5.6 slice_bitcast_fusion.1
  1214.9 84.5 %shard_map.371 = (f32[4,256,512]{2,1,0:T(8,128)S(1)}, bf16[4,4,256,512]{3,2,1,0:T(8,128)(2,1)}, bf16[4,5,256,512]{3,2,1,0:T(8,128)(2,1)}) custom-call(bf16[4,4,2,256,512]{4,3,2,1,0:T(8,128)(2,1)} %pad_maximum_fusion.stack), custom_call_target="tpu_custom_call" | custom-call | tf_op jit(solution)/shard_map/pallas_call | solution.py:224
  (397 shorter events, 234.0 us)
Async XLA Ops:
  7.2 158.2 %copy-start = (bf16[512,2048]{1,0:T(8,128)(2,1)S(1)}, bf16[512,2048]{1,0:T(8,128)(2,1)}, u32[]{:S(2)}) copy-start(bf16[512,2048]{1,0:T(8,128)(2,1)} %param.36) | copy-start | bytes 6291460
  7.2 661.6 %reduce-scatter.14.cloned.1.call-start = ((), (), s32[]{:S(2)}) async-start(), calls=%async_computation.8 | async-start | bytes 163840 | tf_op jit(solution)/shard_map/reduce_scatter | solution.py:1001
  16.9 79.0 %copy-start.9 = (bf16[256,2048]{1,0:T(8,128)(2,1)S(1)}, bf16[256,2048]{1,0:T(8,128)(2,1)}, u32[]{:S(2)}) copy-start(bf16[256,2048]{1,0:T(8,128)(2,1)} %refs_3_) | copy-start | bytes 3145732
  16.9 85.7 %copy-start.79 = (bf16[512]{0:T(512)(128)(2,1)S(1)}, bf16[512]{0:T(512)(128)(2,1)}, u32[]{:S(2)}) copy-start(bf16[512]{0:T(512)(128)(2,1)} %param.35) | copy-start | bytes 3076
  16.9 85.7 %copy-start.80 = (bf16[512]{0:T(512)(128)(2,1)S(1)}, bf16[512]{0:T(512)(128)(2,1)}, u32[]{:S(2)}) copy-start(bf16[512]{0:T(512)(128)(2,1)} %param.34) | copy-start | bytes 3076
  16.9 85.7 %copy-start.81 = (bf16[512]{0:T(512)(128)(2,1)S(1)}, bf16[512]{0:T(512)(128)(2,1)}, u32[]{:S(2)}) copy-start(bf16[512]{0:T(512)(128)(2,1)} %param.33) | copy-start | bytes 3076
  96.0 205.4 %collective-permute-start = (bf16[256,2048]{1,0:T(8,128)(2,1)S(1)}, bf16[256,2048]{1,0:T(8,128)(2,1)}, u32[]{:S(2)}, u32[]{:S(2)}) collective-permute-start(bf16[256,2048]{1,0:T(8,128)(2,1)S(1)} %copy-done.9), channel_id=1, source_target_pairs={{0,1},{1,0},{2,3},{3,2},{4,5},{5,4},{6,7},{7,6},{8,9},{9,8},{10,11... | collective-permute-start | bytes 3145736 | tf_op jit(solution)/shard_map/ppermute | solution.py:636
  97.4 205.3 %collective-permute-start.1 = (bf16[256,2048]{1,0:T(8,128)(2,1)S(1)}, bf16[256,2048]{1,0:T(8,128)(2,1)}, u32[]{:S(2)}, u32[]{:S(2)}) collective-permute-start(bf16[256,2048]{1,0:T(8,128)(2,1)S(1)} %copy-done.9), channel_id=1, source_target_pairs={{0,2},{1,3},{2,0},{3,1},{4,6},{5,7},{6,4},{7,5},{8,10},{9,11},{10,... | collective-permute-start | bytes 3145736 | tf_op jit(solution)/shard_map/ppermute | solution.py:636
  98.0 206.0 %collective-permute-start.2 = (bf16[256,2048]{1,0:T(8,128)(2,1)S(1)}, bf16[256,2048]{1,0:T(8,128)(2,1)}, u32[]{:S(2)}, u32[]{:S(2)}) collective-permute-start(bf16[256,2048]{1,0:T(8,128)(2,1)S(1)} %copy-done.9), channel_id=1, source_target_pairs={{0,3},{1,2},{2,1},{3,0},{4,7},{5,6},{6,5},{7,4},{8,11},{9,10},{10,... | collective-permute-start | bytes 3145736 | tf_op jit(solution)/shard_map/ppermute | solution.py:636
  165.2 208.9 %copy-start.67 = (pred[4,256]{1,0:T(4,128)(4,1)}, pred[4,256]{1,0:T(4,128)(4,1)S(1)}, u32[]{:S(2)}) copy-start(pred[4,256]{1,0:T(4,128)(4,1)S(1)} %reshape.444) | copy-start | bytes 3076
  165.4 208.7 %copy-start.55 = (s32[4,256]{1,0:T(4,128)}, s32[4,256]{1,0:T(4,128)S(1)}, u32[]{:S(2)}) copy-start(s32[4,256]{1,0:T(4,128)S(1)} %convolution_convert_fusion.21) | copy-start | bytes 12292
  242.8 13.6 %slice-start.4 = ((s8[11534336]{0:T(1024)(128)(4,1)}), s8[4194304]{0:T(1024)(128)(4,1)S(1)}, s32[]{:S(2)}) async-start(s8[11534336]{0:T(1024)(128)(4,1)} %bitcast.354), calls=%async_computation.14 | async-start | bytes 8388608
  262.5 138.7 %copy-start.69 = (pred[4,256]{1,0:T(4,128)(4,1)}, pred[4,256]{1,0:T(4,128)(4,1)S(1)}, u32[]{:S(2)}) copy-start(pred[4,256]{1,0:T(4,128)(4,1)S(1)} %reshape.448) | copy-start | bytes 3076
  262.7 138.5 %copy-start.57 = (s32[4,256]{1,0:T(4,128)}, s32[4,256]{1,0:T(4,128)S(1)}, u32[]{:S(2)}) copy-start(s32[4,256]{1,0:T(4,128)S(1)} %convolution_convert_fusion.20) | copy-start | bytes 12292
  262.7 13.3 %slice-start.7 = ((s8[11534336]{0:T(1024)(128)(4,1)}), s8[4194304]{0:T(1024)(128)(4,1)S(1)}, s32[]{:S(2)}) async-start(s8[11534336]{0:T(1024)(128)(4,1)} %bitcast.356), calls=%async_computation.17 | async-start | bytes 8388608
  265.9 17.4 %slice-start.19 = ((s8[5767168]{0:T(1024)(128)(4,1)}), s8[4194304]{0:T(1024)(128)(4,1)S(1)}, s32[]{:S(2)}) async-start(s8[5767168]{0:T(1024)(128)(4,1)} %bitcast.364), calls=%async_computation.29 | async-start | bytes 8388608
  301.2 33.8 %copy-start.77 = (f32[1024,1]{0,1:T(1,128)}, f32[1024,1]{0,1:T(1,128)S(1)}, u32[]{:S(2)}) copy-start(f32[1024,1]{0,1:T(1,128)S(1)} %fusion.125) | copy-start | bytes 12292
  352.2 15.6 %slice-start.10 = ((s8[11534336]{0:T(1024)(128)(4,1)}), s8[4194304]{0:T(1024)(128)(4,1)S(1)}, s32[]{:S(2)}) async-start(s8[11534336]{0:T(1024)(128)(4,1)} %bitcast.358), calls=%async_computation.20 | async-start | bytes 8388608
  352.3 15.6 %slice-start.11 = ((s8[11534336]{0:T(1024)(128)(4,1)}), s8[4194304]{0:T(1024)(128)(4,1)S(1)}, s32[]{:S(2)}) async-start(s8[11534336]{0:T(1024)(128)(4,1)} %bitcast.358), calls=%async_computation.21 | async-start | bytes 8388608
  379.1 15.5 %slice-start.13 = ((s8[11534336]{0:T(1024)(128)(4,1)}), s8[4194304]{0:T(1024)(128)(4,1)S(1)}, s32[]{:S(2)}) async-start(s8[11534336]{0:T(1024)(128)(4,1)} %bitcast.360), calls=%async_computation.23 | async-start | bytes 8388608
  379.1 15.5 %slice-start.14 = ((s8[11534336]{0:T(1024)(128)(4,1)}), s8[4194304]{0:T(1024)(128)(4,1)S(1)}, s32[]{:S(2)}) async-start(s8[11534336]{0:T(1024)(128)(4,1)} %bitcast.360), calls=%async_computation.24 | async-start | bytes 8388608
  401.2 15.9 %slice-start.23 = ((s8[5767168]{0:T(1024)(128)(4,1)}), s8[4194304]{0:T(1024)(128)(4,1)S(1)}, s32[]{:S(2)}) async-start(s8[5767168]{0:T(1024)(128)(4,1)} %bitcast.368), calls=%async_computation.33 | async-start | bytes 8388608
  406.2 10.9 slice-start.24
  406.2 10.9 copy-start.89
  426.2 13.9 %copy-start.6 = (f32[256,2048]{1,0:T(8,128)S(1)}, f32[256,2048]{1,0:T(8,128)}, u32[]{:S(2)}) copy-start(f32[256,2048]{1,0:T(8,128)} %copy-done.5) | copy-start | bytes 6291460
  440.1 76.2 %slice-start.2 = ((s8[6291456]{0:T(1024)(128)(4,1)}), s8[2097152]{0:T(1024)(128)(4,1)S(1)}, s32[]{:S(2)}) async-start(s8[6291456]{0:T(1024)(128)(4,1)} %bitcast.282), calls=%async_computation.12 | async-start | bytes 4194304
  516.3 32.6 %slice-start = ((s8[8388608]{0:T(1024)(128)(4,1)}), s8[4194304]{0:T(1024)(128)(4,1)S(1)}, s32[]{:S(2)}) async-start(s8[8388608]{0:T(1024)(128)(4,1)} %bitcast.275), calls=%async_computation.10 | async-start | bytes 8388608
  527.9 12.6 copy-start.61
  527.9 12.6 copy-start.63
  527.9 21.0 %slice-start.1 = ((s8[8388608]{0:T(1024)(128)(4,1)}), s8[4194304]{0:T(1024)(128)(4,1)S(1)}, s32[]{:S(2)}) async-start(s8[8388608]{0:T(1024)(128)(4,1)} %bitcast.275), calls=%async_computation.11 | async-start | bytes 8388608
  593.8 11.5 copy-start.4
  593.8 11.5 copy-start.15
  593.9 11.5 copy-start.17
  643.7 26.7 %copy-start.83 = (bf16[1024,1408]{1,0:T(8,128)(2,1)S(1)}, bf16[1024,1408]{1,0:T(8,128)(2,1)}, u32[]{:S(2)}) copy-start(bf16[1024,1408]{1,0:T(8,128)(2,1)} %get-tuple-element.134) | copy-start | bytes 8650756
  644.5 190.2 %reduce-scatter.16.cloned.1.call-start = ((), (), s32[]{:S(2)}) async-start(), calls=%async_computation.9 | async-start | bytes 294912
  670.4 191.0 %reduce-scatter.8.cloned.1.call-start = ((), (), s32[]{:S(2)}) async-start(), calls=%async_computation.5 | async-start | bytes 6488064 | tf_op jit(solution)/shard_map/reduce_scatter | solution.py:688
  681.3 182.4 %reduce-scatter.10.cloned.1.call-start = ((), (), s32[]{:S(2)}) async-start(), calls=%async_computation.6 | async-start | bytes 6488064 | tf_op jit(solution)/shard_map/reduce_scatter | solution.py:688
  681.9 216.3 %reduce-scatter.12.cloned.1.call-start = ((), (), s32[]{:S(2)}) async-start(), calls=%async_computation.7 | async-start | bytes 6488064 | tf_op jit(solution)/shard_map/reduce_scatter | solution.py:688
  708.0 28.4 %slice-start.16 = ((s8[11534336]{0:T(1024)(128)(4,1)}), s8[4194304]{0:T(1024)(128)(4,1)S(1)}, s32[]{:S(2)}) async-start(s8[11534336]{0:T(1024)(128)(4,1)} %bitcast.362), calls=%async_computation.26 | async-start | bytes 8388608
  708.0 28.4 %slice-start.17 = ((s8[11534336]{0:T(1024)(128)(4,1)}), s8[4194304]{0:T(1024)(128)(4,1)S(1)}, s32[]{:S(2)}) async-start(s8[11534336]{0:T(1024)(128)(4,1)} %bitcast.362), calls=%async_computation.27 | async-start | bytes 8388608
  729.7 122.8 %collective-permute-start.6 = (bf16[1536,512]{1,0:T(8,128)(2,1)}, bf16[1536,512]{1,0:T(8,128)(2,1)}, u32[]{:S(2)}, u32[]{:S(2)}) collective-permute-start(bf16[1536,512]{1,0:T(8,128)(2,1)} %bitcast.262), channel_id=1, source_target_pairs={{0,1},{1,0},{2,3},{3,2},{4,5},{5,4},{6,7},{7,6},{8,9},{9,8},{10,11... | collective-permute-start | bytes 4718600 | tf_op jit(solution)/shard_map/ppermute | solution.py:636
  732.7 119.8 %collective-permute-start.7 = (bf16[1536,512]{1,0:T(8,128)(2,1)}, bf16[1536,512]{1,0:T(8,128)(2,1)}, u32[]{:S(2)}, u32[]{:S(2)}) collective-permute-start(bf16[1536,512]{1,0:T(8,128)(2,1)} %bitcast.261), channel_id=1, source_target_pairs={{0,2},{1,3},{2,0},{3,1},{4,6},{5,7},{6,4},{7,5},{8,10},{9,11},{10,... | collective-permute-start | bytes 4718600 | tf_op jit(solution)/shard_map/ppermute | solution.py:636
  734.9 117.6 %collective-permute-start.8 = (bf16[1536,512]{1,0:T(8,128)(2,1)}, bf16[1536,512]{1,0:T(8,128)(2,1)}, u32[]{:S(2)}, u32[]{:S(2)}) collective-permute-start(bf16[1536,512]{1,0:T(8,128)(2,1)} %bitcast.260), channel_id=1, source_target_pairs={{0,3},{1,2},{2,1},{3,0},{4,7},{5,6},{6,5},{7,4},{8,11},{9,10},{10,... | collective-permute-start | bytes 4718600 | tf_op jit(solution)/shard_map/ppermute | solution.py:636
  770.8 53.6 %collective-permute-start.3 = (bf16[256,2048]{1,0:T(8,128)(2,1)S(1)}, bf16[256,2048]{1,0:T(8,128)(2,1)S(1)}, u32[]{:S(2)}, u32[]{:S(2)}) collective-permute-start(bf16[256,2048]{1,0:T(8,128)(2,1)S(1)} %get-tuple-element.163), channel_id=1, source_target_pairs={{0,1},{1,0},{2,3},{3,2},{4,5},{5,4},{6,7},{7,6},{8,9},{9,8},{10,11... | collective-permute-start | bytes 3145736 | tf_op jit(solution)/shard_map/ppermute | solution.py:636
  772.2 68.7 %collective-permute-start.4 = (bf16[256,2048]{1,0:T(8,128)(2,1)}, bf16[256,2048]{1,0:T(8,128)(2,1)}, u32[]{:S(2)}, u32[]{:S(2)}) collective-permute-start(bf16[256,2048]{1,0:T(8,128)(2,1)} %get-tuple-element.165), channel_id=1, source_target_pairs={{0,2},{1,3},{2,0},{3,1},{4,6},{5,7},{6,4},{7,5},{8,10},{9,11},{10,... | collective-permute-start | bytes 3145736 | tf_op jit(solution)/shard_map/ppermute | solution.py:636
  824.4 24.3 %collective-permute-start.5 = (bf16[256,2048]{1,0:T(8,128)(2,1)}, bf16[256,2048]{1,0:T(8,128)(2,1)}, u32[]{:S(2)}, u32[]{:S(2)}) collective-permute-start(bf16[256,2048]{1,0:T(8,128)(2,1)} %get-tuple-element.164), channel_id=1, source_target_pairs={{0,3},{1,2},{2,1},{3,0},{4,7},{5,6},{6,5},{7,4},{8,11},{9,10},{10,... | collective-permute-start | bytes 3145736 | tf_op jit(solution)/shard_map/ppermute | solution.py:636
  830.9 17.8 %copy-start.7 = (f32[256,2048]{1,0:T(8,128)S(1)}, f32[256,2048]{1,0:T(8,128)}, u32[]{:S(2)}) copy-start(f32[256,2048]{1,0:T(8,128)} %copy-done.5) | copy-start | bytes 6291460
  830.9 17.8 %copy-start.65 = (bf16[256,2048]{1,0:T(8,128)(2,1)S(1)}, bf16[256,2048]{1,0:T(8,128)(2,1)}, u32[]{:S(2)}) copy-start(bf16[256,2048]{1,0:T(8,128)(2,1)} %copy-done.64) | copy-start | bytes 3145732
  (82 other events, 428.1 us)
Sparse Core Ops, SparseCore 0:
  644.6 24.0 reduce-scatter.13
  671.7 30.3 reduce-scatter.15
  704.4 63.0 reduce-scatter.7
  769.6 63.2 reduce-scatter.9
  835.0 63.1 reduce-scatter.11

commit v2 on v1

v2 whole, which is shorter than its diff:
```python
import functools

import jax
import jax.numpy as jnp
from jax import lax
from jax.experimental import pallas as pl
from jax.experimental.pallas import tpu as pltpu
from jax.sharding import PartitionSpec as P

HEADS = 16
HEAD_DIM = 128
EPSILON = 1e-06
ROPE_BASE = 1000000.0
MASK_FILL = -1e30

F32 = jnp.float32
BF16 = jnp.bfloat16
MESH = pl.DeviceIdType.MESH
ANY = pl.BlockSpec(memory_space=pl.ANY)
VMEM = pl.BlockSpec(memory_space=pltpu.VMEM)
MIB = 2**20


def dot(left, right, dims, out=F32):
    return lax.dot_general(left, right, (dims, ((), ())), preferred_element_type=out)


def plain_dot(left, right):
    return dot(left, right, ((1,), (0,)))


def trans_dot(left, right):
    return dot(left, right, ((1,), (1,)))


def rows_dot(left, right):
    return dot(left, right, ((0,), (0,)))


def pieces(total, size):
    return [(a, min(size, total - a)) for a in range(0, total, size)]


def hidden_part(x, g, gate, w_gate, w_up, w_down, hidden, d_gate, d_up):
    units = w_gate.shape[1]
    sens = None
    for a, n in pieces(units, 256):
        s = pl.ds(a, n)
        pre = plain_dot(x, w_gate[:, s])
        up = plain_dot(x, w_up[:, s])
        plain = trans_dot(g, w_down[s, :])
        sigma = 1.0 / (1.0 + jnp.exp(-pre))
        act = pre * sigma
        slope = sigma * (1.0 + pre * (1.0 - sigma))
        h = (act * up).astype(BF16)
        hidden[:, s] = h
        grad = gate * plain
        d_gate[:, s] = (grad * up * slope).astype(BF16)
        d_up[:, s] = (grad * act).astype(BF16)
        part = jnp.sum(plain * h.astype(F32), axis=-1, keepdims=True)
        sens = part if sens is None else sens + part
    return sens


def expert_kernel(x_ref, g_ref, gate_ref, wg, wu, wd, hidden, d_gate, d_up, d_out, y_ref, dx_ref, sens_ref):
    blocks, _, slots, features = x_ref.shape
    rows = blocks * slots
    x = x_ref[...].reshape(rows, features)
    g = g_ref[...].reshape(rows, features)
    gate = gate_ref[...].reshape(rows, 1)
    wg, wu, wd = wg.at[0], wu.at[0], wd.at[0]
    hid, dg, du = hidden.at[0], d_gate.at[0], d_up.at[0]
    d_out[...] = (gate * g.astype(F32)).astype(BF16).reshape(d_out.shape)
    sens = hidden_part(x, g, gate, wg, wu, wd, hid, dg, du)
    sens_ref[...] = sens.reshape(sens_ref.shape)
    for a, n in pieces(features, 512):
        s = pl.ds(a, n)
        y = plain_dot(hid[...], wd[:, s]).astype(BF16)
        y_ref[:, :, :, s] = (gate * y.astype(F32)).astype(BF16).reshape(blocks, 1, slots, n)
        dx = trans_dot(dg[...], wg[s, :]) + trans_dot(du[...], wu[s, :])
        dx_ref[:, :, :, s] = dx.astype(BF16).reshape(blocks, 1, slots, n)


def expert_call(rows_in, rows_cot, gate, w_gate, w_up, w_down, tile):
    blocks, experts, slots, features = rows_in.shape
    units = w_gate.shape[2]
    steps = blocks // tile
    rows = tile * slots

    def slot_spec(cols):
        return pl.BlockSpec((tile, 1, slots, cols), lambda i, t: (t, i, 0, 0))

    def unit_spec():
        return pl.BlockSpec((1, rows, units), lambda i, t: (i, t, 0))

    def weight_spec(a, b):
        return pl.BlockSpec((1, a, b), lambda i, t: (i, 0, 0))

    units_shape = jax.ShapeDtypeStruct((experts, blocks * slots, units), BF16)
    slots_shape = jax.ShapeDtypeStruct((blocks, experts, slots, features), BF16)
    return pl.pallas_call(
        expert_kernel,
        grid=(experts, steps),
        in_specs=[
            slot_spec(features),
            slot_spec(features),
            slot_spec(1),
            weight_spec(features, units),
            weight_spec(features, units),
            weight_spec(units, features),
        ],
        out_specs=[unit_spec()] * 3 + [slot_spec(features)] * 3 + [slot_spec(1)],
        out_shape=[units_shape] * 3
        + [slots_shape] * 3
        + [jax.ShapeDtypeStruct((blocks, experts, slots, 1), F32)],
        compiler_params=pltpu.CompilerParams(vmem_limit_bytes=62 * MIB),
    )(rows_in, rows_cot, gate, w_gate, w_up, w_down)


def shared_kernel(
    x_ref, g_ref, head_ref, pick_ref, y_in, dx_in, lane_ref, heads_w, switch_row, wg, wu, wd,
    hidden, d_gate, d_up, d_out, y_ref, dx_ref, sens_ref,
):
    features = x_ref.shape[1]
    x = x_ref[...]
    g = g_ref[...]
    opener = head_ref[...]
    d_out[...] = (opener * g.astype(F32)).astype(BF16)
    sens = hidden_part(x, d_out[...], 1.0, wg, wu, wd, hidden, d_gate, d_up)
    sens = (1.0 - opener) * sens
    sens_ref[...] = sens
    pick = pick_ref[0]
    lanes = lane_ref[...]
    for a, n in pieces(features, 512):
        s = pl.ds(a, n)
        y = opener * plain_dot(hidden[...], wd[:, s]) + rows_dot(pick, y_in[0, :, s])
        y_ref[:, s] = y.astype(BF16)
        dx = trans_dot(d_gate[...], wg[s, :]) + trans_dot(d_up[...], wu[s, :])
        dx = dx + rows_dot(pick, dx_in[0, :, s])
        dx = dx + plain_dot(lanes, heads_w[:, s]) + sens * switch_row[:, s]
        dx_ref[:, s] = dx.astype(BF16)


def shared_call(x, g, opener, pick, y_in, dx_in, lanes, heads_w, switch_row, w_gate, w_up, w_down):
    count, features = x.shape
    units = w_gate.shape[1]
    blocks, taken, tile = pick.shape
    width = lanes.shape[1]

    def rows_spec(cols):
        return pl.BlockSpec((tile, cols), lambda b: (b, 0))

    def block_spec(cols):
        return pl.BlockSpec((1, taken, cols), lambda b: (b, 0, 0))

    def whole(a, b):
        return pl.BlockSpec((a, b), lambda b_: (0, 0), pipeline_mode=pl.Buffered(1))

    def shape(cols, dtype=BF16):
        return jax.ShapeDtypeStruct((count, cols), dtype)

    return pl.pallas_call(
        shared_kernel,
        grid=(blocks,),
        in_specs=[
            rows_spec(features),
            rows_spec(features),
            rows_spec(1),
            block_spec(tile),
            block_spec(features),
            block_spec(features),
            rows_spec(width),
            whole(width, features),
            whole(1, features),
            whole(features, units),
            whole(features, units),
            whole(units, features),
        ],
        out_specs=[rows_spec(units)] * 3 + [rows_spec(features)] * 3 + [rows_spec(1)],
        out_shape=[shape(units)] * 3 + [shape(features)] * 3 + [shape(1, F32)],
        compiler_params=pltpu.CompilerParams(vmem_limit_bytes=62 * MIB),
    )(x, g, opener, pick, y_in, dx_in, lanes, heads_w, switch_row, w_gate, w_up, w_down)


def other_kernel(x_ref, g_ref, heads, wg, wu, wd, hidden, d_gate, d_up, d_out):
    x = x_ref[...]
    pre = trans_dot(x, heads[...])
    opener = 1.0 / (1.0 + jnp.exp(-pre[:, heads.shape[0] - 1 :]))
    d_out[...] = (opener * g_ref[...].astype(F32)).astype(BF16)
    hidden_part(x, d_out[...], 1.0, wg, wu, wd, hidden, d_gate, d_up)


def other_call(x, g, heads, w_gate, w_up, w_down, tile):
    count, features = x.shape
    units = w_gate.shape[1]

    def rows_spec(cols):
        return pl.BlockSpec((tile, cols), lambda b: (b, 0))

    def whole(a, b):
        return pl.BlockSpec((a, b), lambda b_: (0, 0), pipeline_mode=pl.Buffered(1))

    def shape(cols):
        return jax.ShapeDtypeStruct((count, cols), BF16)

    return pl.pallas_call(
        other_kernel,
        grid=(count // tile,),
        in_specs=[
            rows_spec(features),
            rows_spec(features),
            whole(heads.shape[0], features),
            whole(features, units),
            whole(features, units),
            whole(units, features),
        ],
        out_specs=[rows_spec(units)] * 3 + [rows_spec(features)],
        out_shape=[shape(units)] * 3 + [shape(features)],
        compiler_params=pltpu.CompilerParams(vmem_limit_bytes=62 * MIB),
    )(x, g, heads, w_gate, w_up, w_down)


class Line:
    def __init__(self, parts, inner, sources, outs, sib, recv, bufs, sems):
        self.parts, self.inner, self.sources, self.outs = parts, inner, sources, outs
        self.sib, self.recv = sib, recv
        self.own_v, self.sib_v, self.in_v, self.more_v, self.send_v, self.out_v, self.turned_v = bufs
        self.own_sem, self.sib_sem, self.in_sem, self.out_sem, self.sib_send, self.sib_recv, self.sent, self.got = sems
        self.chunks = len(sources) * parts
        self.slots = self.send_v.shape[0]
        self.rows = sources[0].shape[2] // parts
        g = lax.axis_index("grp")
        self.z, self.core = g // 2, lax.rem(g, 2)
        self.is_end = (self.z == 0) | (self.z == 3)
        self.is_mid = (self.z == 1) | (self.z == 2)

    def at(self, z, core):
        return {"grp": 2 * z + core}

    def span(self, q):
        return lax.div(q, self.parts), pl.ds(
            pl.multiple_of(lax.rem(q, self.parts) * self.rows, self.rows), self.rows
        )

    def swap(self, j, m, r, q):
        return pltpu.make_async_remote_copy(
            src_ref=self.sources[j].at[:, 1 - self.core, r],
            dst_ref=self.sib.at[m, :, r],
            send_sem=self.sib_send.at[q],
            recv_sem=self.sib_recv.at[q],
            device_id=self.at(self.z, 1 - self.core),
            device_id_type=MESH,
        )

    def swap_any(self, q):
        m, r = self.span(q)
        return self.swap(0, m, r, q)

    def when_summing(self, condition=None):
        if self.inner:
            condition = self.is_mid if condition is None else self.is_mid & condition
        return (lambda body: body()) if condition is None else pl.when(condition)

    def start_swaps(self):
        @self.when_summing()
        def _():
            for m in range(len(self.sources)):
                for h in range(self.parts):
                    self.swap(m, m, pl.ds(h * self.rows, self.rows), m * self.parts + h).start()

    def out_copy(self, j, r):
        ref, turned = self.outs[j]
        if turned:
            return pltpu.make_async_copy(self.turned_v, ref.at[:, r], self.out_sem)
        return pltpu.make_async_copy(self.out_v, ref.at[r], self.out_sem)

    def each_out(self, q, body):
        m, r = self.span(q)
        for j in range(len(self.sources)):

            @pl.when(m == j)
            def _():
                body(j, r)

    def hop(self, q, slot, target, place):
        m, r = self.span(q)
        return pltpu.make_async_remote_copy(
            src_ref=self.send_v.at[slot],
            dst_ref=self.recv.at[m, place, r],
            send_sem=self.sent.at[slot],
            recv_sem=self.got.at[q, place],
            device_id=self.at(target, self.core),
            device_id_type=MESH,
        )

    def arrived(self, q, place):
        self.hop(q, 0, self.z, place).wait_recv()

    def own_load(self, j, p, r, k):
        return pltpu.make_async_copy(self.sources[j].at[p, self.core, r], self.own_v.at[k], self.own_sem.at[k])

    def sib_load(self, m, p, r, k):
        return pltpu.make_async_copy(self.sib.at[m, p, r], self.sib_v.at[k], self.sib_sem.at[k])

    def start_base(self, q, p, k):
        m, r = self.span(q)
        for j in range(len(self.sources)):

            @pl.when(m == j)
            def _():
                self.own_load(j, p, r, k).start()

        self.sib_load(m, p, r, k).start()

    def base(self, k):
        r = pl.ds(0, self.rows)
        self.own_load(0, 0, r, k).wait()
        self.sib_load(0, 0, r, k).wait()
        return self.own_v[k].astype(F32) + self.sib_v[k].astype(F32)

    def fetch(self, q, place, buf, k):
        self.arrived(q, place)
        m, r = self.span(q)
        c = pltpu.make_async_copy(self.recv.at[m, place, r], buf, self.in_sem.at[k])
        c.start()
        c.wait()
        return buf[...].astype(F32)

    def send(self, t, k, q, p, target, place, more, first):
        depth = self.slots // 3
        slot = lax.rem(t, depth) * 3 + k

        @pl.when(t >= depth + first)
        def _():
            self.hop(q, slot, target, place).wait_send()

        if more:
            extra = self.fetch(q, p, self.in_v, 0)
            total = self.base(k) + extra
        else:
            total = self.base(k)
        self.send_v[slot] = total.astype(BF16)
        self.hop(q, slot, target, place).start()

    def turn(self, t):
        z, chunks = self.z, self.chunks
        to_end = self.is_end & (t >= 0) & (t < chunks)
        to_next = self.is_mid & (t >= 1) & (t < chunks + 1)
        to_last = self.is_mid & (t >= 2) & (t < chunks + 2)
        last = (t >= 3) & (t < chunks + 3)

        @self.when_summing((t >= 0) & (t < chunks))
        def _():
            self.swap_any(t).wait_recv()

        def end_piece(j):
            return jnp.where(z == 0, 3 - j, j)

        def next_piece(j):
            return jnp.where(z == 1, 3 - j, j)

        last_piece = jnp.where(z == 2, 3, 0)
        if not self.inner:

            @pl.when(to_end)
            def _():
                for j in range(3):
                    self.start_base(t, end_piece(j), j)

        @pl.when(to_next)
        def _():
            for j in range(2):
                self.start_base(t - 1, next_piece(j), j)

        @pl.when(to_last)
        def _():
            self.start_base(t - 2, last_piece, 2)

        @self.when_summing(last)
        def _():
            self.start_base(t - 3, z, 3)

        if not self.inner:

            @pl.when(to_end)
            def _():
                for j in range(3):
                    p = end_piece(j)
                    target = jnp.where(z == 0, 1, 2)
                    place = jnp.where((z == 3) & (p == 2), 4, p)
                    self.send(t, j, t, p, target, place, False, 0)

        @pl.when(to_next)
        def _():
            for j in range(2):
                p = next_piece(j)
                target = jnp.where(z == 1, 2, 1)
                place = jnp.where((z == 2) & (p == 1), 4, p)
                self.send(t, j, t - 1, p, target, place, not self.inner, 1)

        @pl.when(to_last)
        def _():
            place = jnp.where(z == 1, 4, last_piece)
            self.send(t, 2, t - 2, last_piece, last_piece, place, True, 2)

        @pl.when(last)
        def _():
            q = t - 3

            @pl.when(q >= 1)
            def _():
                self.each_out(q - 1, lambda j, r: self.out_copy(j, r).wait())

            if self.inner:

                @pl.when(z == 0)
                def _():
                    self.out_v[...] = self.fetch(q, 4, self.more_v, 1)

                @pl.when(z == 3)
                def _():
                    self.out_v[...] = self.fetch(q, 3, self.more_v, 1)

                @pl.when(z == 1)
                def _():
                    got = self.fetch(q, 4, self.more_v, 1)
                    self.out_v[...] = self.base(3) + got

                @pl.when(z == 2)
                def _():
                    got = self.fetch(q, 2, self.more_v, 1)
                    self.out_v[...] = self.base(3) + got

            else:
                self.out_v[...] = self.base(3)

                @pl.when(z > 0)
                def _():
                    self.out_v[...] = self.out_v[...] + self.fetch(q, z, self.in_v, 0)

                @pl.when(z < 3)
                def _():
                    self.out_v[...] = self.out_v[...] + self.fetch(q, 4, self.more_v, 1)

            def put(j, r):
                if self.outs[j][1]:
                    self.turned_v[...] = self.out_v[...].T
                self.out_copy(j, r).start()

            self.each_out(q, put)

    def finish(self):
        self.each_out(self.chunks - 1, lambda j, r: self.out_copy(j, r).wait())

        def body(q, carry):
            self.swap_any(q).wait_send()
            return carry

        @self.when_summing()
        def _():
            lax.fori_loop(0, self.chunks, body, 0)

        assert self.chunks >= self.slots // 3

        @self.when_summing()
        def _():
            for slot in range(self.slots):
                self.hop(0, slot, self.z, 0).wait_send()


def line_bufs(shape, slots, turned):
    return [pltpu.VMEM((4,) + shape, BF16)] * 2 + [
        pltpu.VMEM(shape, BF16),
        pltpu.VMEM(shape, BF16),
        pltpu.VMEM((slots,) + shape, BF16),
        pltpu.VMEM(shape, F32),
        pltpu.VMEM(shape[::-1] if turned else (8, 128), F32),
    ]


def line_sems(q, slots):
    return [
        pltpu.SemaphoreType.DMA((4,)),
        pltpu.SemaphoreType.DMA((4,)),
        pltpu.SemaphoreType.DMA((2,)),
        pltpu.SemaphoreType.DMA,
        pltpu.SemaphoreType.DMA((q,)),
        pltpu.SemaphoreType.DMA((q,)),
        pltpu.SemaphoreType.DMA((slots,)),
        pltpu.SemaphoreType.DMA((q, 5)),
    ]


def line_kernel(n_down, n_shared, parts, shift, *refs):
    def take(n):
        nonlocal refs
        taken, refs = refs[:n], refs[n:]
        return taken

    downs, shared = take(n_down), take(n_shared)
    three, part_out, out_part, mixed, vec, bias_add = take(6)
    out_down, out_gate, out_up, out_sdown, out_four, output, vec_out = take(7)
    sib_a, recv_a, att, sib_b, recv_b, sib_c, recv_c, out_in = take(8)
    bufs_a, bufs_b, bufs_c = take(7), take(7), take(7)
    vec_in, vec_own, vec_sib, vec_line, vec_send, parts_v, mixed_v, sum_v = take(8)
    sems_a, sems_b, sems_c = take(8), take(8), take(8)
    plane_send, plane_recv, local_sems, vec_send_sems, vec_recv_sems, out_send, out_recv = take(7)

    a = Line(parts, False, downs, [(out_down.at[j], True) for j in range(n_down)], sib_a, recv_a, bufs_a, sems_a)
    b = Line(1, False, [att.at[j] for j in range(4)], [(out_four.at[j], True) for j in range(4)], sib_b, recv_b, bufs_b, sems_b)
    c = Line(parts, shift, shared, [(out_gate, False), (out_up, False), (out_sdown, True)], sib_c, recv_c, bufs_c, sems_c)
    z, core = a.z, a.core
    f = lax.axis_index("fsdp")
    fx = f + 1 - 2 * lax.rem(f, 2)
    fy = f + 2 - 4 * (f // 2)
    fd = fx + 2 - 4 * (fx // 2)
    peers = (fx, fy, fd)
    sibling = a.at(z, 1 - core)
    width = three.shape[3] // 4

    barrier = pltpu.get_barrier_semaphore()
    for other in (sibling,) + tuple({"fsdp": p} for p in peers):
        pl.semaphore_signal(barrier, inc=1, device_id=other, device_id_type=MESH)

    @pl.when(z > 0)
    def _():
        pl.semaphore_signal(barrier, inc=1, device_id=a.at(z - 1, core), device_id_type=MESH)

    @pl.when(z < 3)
    def _():
        pl.semaphore_signal(barrier, inc=1, device_id=a.at(z + 1, core), device_id_type=MESH)

    @pl.when(a.is_end)
    def _():
        pl.semaphore_wait(barrier, 5)

    @pl.when(a.is_mid)
    def _():
        pl.semaphore_wait(barrier, 6)

    a.start_swaps()
    c.start_swaps()

    def cols(p):
        return pl.ds(pl.multiple_of(p * width, width), width)

    def to_owner(k, p):
        return pltpu.make_async_remote_copy(
            src_ref=three.at[:, :, :, cols(p)], dst_ref=att.at[pl.ds(0, 3), f],
            send_sem=plane_send.at[k], recv_sem=plane_recv.at[k],
            device_id={"fsdp": p}, device_id_type=MESH,
        )

    def vec_owner(k, p):
        return pltpu.make_async_remote_copy(
            src_ref=vec.at[p], dst_ref=vec_in.at[k],
            send_sem=vec_send_sems.at[k], recv_sem=vec_recv_sems.at[k],
            device_id={"fsdp": p}, device_id_type=MESH,
        )

    def out_owner(k, p):
        return pltpu.make_async_remote_copy(
            src_ref=out_part.at[k + 1], dst_ref=out_in.at[k],
            send_sem=out_send.at[k], recv_sem=out_recv.at[k],
            device_id={"fsdp": p}, device_id_type=MESH,
        )

    for k, p in enumerate(peers):
        vec_owner(k, p).start()
    for k, p in enumerate(peers):
        to_owner(k, p).start()
    keep = (
        pltpu.make_async_copy(three.at[:, :, :, cols(f)], att.at[pl.ds(0, 3), f], local_sems.at[0]),
        pltpu.make_async_copy(part_out, att.at[3], local_sems.at[1]),
    )
    for copy in keep:
        copy.start()

    def vec_swap():
        return pltpu.make_async_remote_copy(
            src_ref=vec_own, dst_ref=vec_sib, send_sem=vec_send_sems.at[3], recv_sem=vec_recv_sems.at[3],
            device_id=sibling, device_id_type=MESH,
        )

    def vec_hop(k, target):
        return pltpu.make_async_remote_copy(
            src_ref=vec_send.at[k], dst_ref=vec_line.at[k], send_sem=vec_send_sems.at[4 + k],
            recv_sem=vec_recv_sems.at[4 + k], device_id=a.at(target, core), device_id_type=MESH,
        )

    def finish_output():
        for k, p in enumerate(peers):
            out_owner(k, p).wait_recv()
        step = parts_v.shape[1]

        def body(i, carry):
            r = pl.ds(pl.multiple_of(i * step, step), step)
            loads = [pltpu.make_async_copy(out_part.at[0, r], parts_v.at[0], local_sems.at[3])]
            loads += [
                pltpu.make_async_copy(out_in.at[k, r], parts_v.at[k + 1], local_sems.at[4 + k]) for k in range(3)
            ]
            loads.append(pltpu.make_async_copy(mixed.at[r], mixed_v, local_sems.at[7]))
            for copy in loads:
                copy.start()
            for copy in loads:
                copy.wait()
            total = (parts_v[0].astype(F32) + parts_v[1].astype(F32)) + (
                parts_v[2].astype(F32) + parts_v[3].astype(F32)
            )
            sum_v[...] = (mixed_v[...] + total).astype(BF16)
            copy = pltpu.make_async_copy(sum_v, output.at[r], local_sems.at[8])
            copy.start()
            copy.wait()
            return carry

        lax.fori_loop(0, mixed.shape[0] // step, body, 0)

    def side_work(t):
        @pl.when(t == 1)
        def _():
            for k, p in enumerate(peers):
                vec_owner(k, p).wait_recv()
            copy = pltpu.make_async_copy(vec.at[f], vec_own, local_sems.at[2])
            copy.start()
            copy.wait()
            vec_own[...] = (vec_own[...] + vec_in[0]) + (vec_in[1] + vec_in[2]) + bias_add[...]
            vec_swap().start()

        @pl.when(t == 2)
        def _():
            vec_swap().wait_recv()
            vec_sib[...] = vec_sib[...] + vec_own[...]

            @pl.when(z == 0)
            def _():
                vec_send[0] = vec_sib[...]
                vec_hop(0, 1).start()

            @pl.when(z == 3)
            def _():
                vec_send[1] = vec_sib[...]
                vec_hop(1, 2).start()

        @pl.when((t == 3) & (z == 1))
        def _():
            vec_hop(0, 1).wait_recv()
            vec_send[0] = vec_sib[...] + vec_line[0]
            vec_hop(0, 2).start()

        @pl.when((t == 3) & (z == 2))
        def _():
            vec_hop(1, 2).wait_recv()
            vec_send[1] = vec_sib[...] + vec_line[1]
            vec_hop(1, 1).start()

        @pl.when(t == 3)
        def _():
            for k, p in enumerate(peers):
                to_owner(k, p).wait_recv()
            for copy in keep:
                copy.wait()
            b.start_swaps()
            for k, p in enumerate(peers):
                out_owner(k, p).start()

        @pl.when((t == 4) & (z == 2))
        def _():
            vec_hop(0, 2).wait_recv()
            vec_send[0] = vec_sib[...] + vec_line[0]
            vec_hop(0, 3).start()
            vec_out[...] = vec_send[0] + vec_line[1]

        @pl.when((t == 4) & (z == 1))
        def _():
            vec_hop(1, 1).wait_recv()
            vec_send[1] = vec_sib[...] + vec_line[1]
            vec_hop(1, 0).start()
            vec_out[...] = vec_send[1] + vec_line[0]

        @pl.when((t == 5) & (z == 3))
        def _():
            vec_hop(0, 3).wait_recv()
            vec_out[...] = vec_sib[...] + vec_line[0]

        @pl.when((t == 5) & (z == 0))
        def _():
            vec_hop(1, 0).wait_recv()
            vec_out[...] = vec_sib[...] + vec_line[1]

        @pl.when(t == 6)
        def _():
            finish_output()

    def slower(t):
        if a.chunks + b.chunks < c.chunks + 2:
            c.turn(t)
            return

        @pl.when((t != 2) & (t != 5))
        def _():
            c.turn(t - jnp.where(t > 2, 1, 0) - jnp.where(t > 5, 1, 0))

    def first_loop(t, carry):
        a.turn(t)
        b.turn(t - a.chunks)
        slower(t)
        side_work(t)
        return carry

    def last_loop(t, carry):
        b.turn(t - a.chunks)
        slower(t)
        return carry

    turns = max(a.chunks + b.chunks, c.chunks + 2) + 3
    lax.fori_loop(0, max(7, a.chunks + 3), first_loop, 0)
    lax.fori_loop(max(7, a.chunks + 3), turns, last_loop, 0)
    a.finish()
    b.finish()
    c.finish()
    for k, p in enumerate(peers):
        vec_owner(k, p).wait_send()
        to_owner(k, p).wait_send()
        out_owner(k, p).wait_send()
    vec_swap().wait_send()

    @pl.when(z < 3)
    def _():
        vec_hop(0, 3).wait_send()

    @pl.when(z > 0)
    def _():
        vec_hop(1, 0).wait_send()


def line_call(downs, shared, three, part_out, out_part, mixed, vec, bias_add, parts, shift, collective_id):
    _, _, rows, cols = shared[0].shape
    m, s = len(downs), len(shared)
    _, _, share, features = three.shape
    width = features // 4
    own_rows = mixed.shape[0]
    r = rows // parts
    slots = 9
    small = (16, width)
    step = own_rows // 4

    def shape(*dims, dtype=BF16):
        return jax.ShapeDtypeStruct(dims, dtype)

    outs = pl.pallas_call(
        functools.partial(line_kernel, m, s, parts, shift),
        out_shape=(
            shape(m, cols, rows, dtype=F32),
            shape(rows, cols, dtype=F32),
            shape(rows, cols, dtype=F32),
            shape(cols, rows, dtype=F32),
            shape(4, width, share, dtype=F32),
            shape(own_rows, features),
            shape(*small, dtype=F32),
            shape(m, 4, rows, cols),
            shape(m, 5, rows, cols),
            shape(4, 4, 2, share, width),
            shape(4, 4, share, width),
            shape(4, 5, share, width),
            shape(s, 4, rows, cols),
            shape(s, 5, rows, cols),
            shape(3, own_rows, features),
        ),
        in_specs=[ANY] * (m + s + 5) + [VMEM],
        out_specs=(ANY,) * 6 + (VMEM,) + (ANY,) * 8,
        scratch_shapes=line_bufs((r, cols), slots, True)
        + line_bufs((share, width), slots, True)
        + line_bufs((r, cols), slots, True)
        + [
            pltpu.VMEM((3,) + small, F32),
            pltpu.VMEM(small, F32),
            pltpu.VMEM(small, F32),
            pltpu.VMEM((2,) + small, F32),
            pltpu.VMEM((2,) + small, F32),
            pltpu.VMEM((4, step, features), BF16),
            pltpu.VMEM((step, features), F32),
            pltpu.VMEM((step, features), BF16),
        ]
        + line_sems(m * parts, slots)
        + line_sems(4, slots)
        + line_sems(s * parts, slots)
        + [
            pltpu.SemaphoreType.DMA((3,)),
            pltpu.SemaphoreType.DMA((3,)),
            pltpu.SemaphoreType.DMA((9,)),
            pltpu.SemaphoreType.DMA((6,)),
            pltpu.SemaphoreType.DMA((6,)),
            pltpu.SemaphoreType.DMA((3,)),
            pltpu.SemaphoreType.DMA((3,)),
        ],
        compiler_params=pltpu.CompilerParams(
            collective_id=collective_id, has_side_effects=True, vmem_limit_bytes=60 * MIB
        ),
    )(*downs, *shared, three, part_out, out_part, mixed, vec, bias_add)
    return outs[:7]


def plane_neighbours():
    f = lax.axis_index("fsdp")
    by_x = f + 1 - 2 * lax.rem(f, 2)
    by_y = f + 2 - 4 * (f // 2)
    return {"fsdp": by_x}, {"fsdp": by_y}


def plane_barrier(by_x, by_y):
    barrier = pltpu.get_barrier_semaphore()
    for other in (by_x, by_y):
        pl.semaphore_signal(barrier, inc=1, device_id=other, device_id_type=MESH)
    pl.semaphore_wait(barrier, 2)


class Side:
    block = 512

    def __init__(self, arrays, jobs):
        self.arrays, self.jobs = list(arrays), list(jobs)
        self.operands = sorted({o for job in self.jobs for pair in job for o in pair}, key=str)

    def shape(self, operand):
        number, axis, _ = operand
        full = self.arrays[number].shape
        return full if axis is None else full[:axis] + full[axis + 1 :]

    def out_shapes(self):
        return [
            jax.ShapeDtypeStruct((self.shape(job[0][0])[-1], self.shape(job[0][1])[-1]), BF16)
            for job in self.jobs
        ]

    def scratch(self):
        stages = sorted({self.shape(job[0][1])[-1] for job in self.jobs})
        self.stage_of = {n: k for k, n in enumerate(stages)}
        return (
            [pltpu.VMEM(self.shape(o), BF16) for o in self.operands]
            + [pltpu.VMEM((2, self.block, n), BF16) for n in stages]
            + [
                pltpu.SemaphoreType.DMA((max(1, len(self.operands)),)),
                pltpu.SemaphoreType.DMA((max(1, 2 * len(stages)),)),
            ]
        )

    def bind(self, ins, outs, scratch):
        n = len(self.operands)
        self.ins, self.outs = ins, outs
        self.bufs, self.stages = scratch[:n], scratch[n:-2]
        self.load_sems, self.out_sems = scratch[-2:]
        self.loaded, self.pending, self.turn_of = set(), {}, {}
        self.units = [
            (j, k)
            for j, job in enumerate(self.jobs)
            for k in range(self.shape(job[0][0])[-1] // self.block)
        ]

    def load(self, k):
        number, axis, entry = self.operands[k]
        ref = self.ins[number]
        if axis is not None:
            ref = ref.at[(slice(None),) * axis + (entry,)]
        return pltpu.make_async_copy(ref, self.bufs[k], self.load_sems.at[k])

    def begin(self):
        for o in [o for job in self.jobs for pair in job for o in pair]:
            k = self.operands.index(o)
            if k not in self.loaded:
                self.loaded.add(k)
                self.load(k).start()
        self.loaded = set()

    def step(self, number):
        for _ in range(number):
            if not self.units:
                return
            j, block = self.units.pop(0)
            pairs = [tuple(self.operands.index(o) for o in pair) for pair in self.jobs[j]]
            for k in [k for pair in pairs for k in pair]:
                if k not in self.loaded:
                    self.loaded.add(k)
                    self.load(k).wait()
            n = self.shape(self.jobs[j][0][1])[-1]
            stage = self.stage_of[n]
            slot = self.turn_of.get(stage, 0)
            self.turn_of[stage] = 1 - slot
            if (stage, slot) in self.pending:
                self.pending.pop((stage, slot)).wait()
            rows = pl.ds(block * self.block, self.block)
            total = None
            for ka, kb in pairs:
                left = self.bufs[ka][..., rows].reshape(-1, self.block)
                part = rows_dot(left, self.bufs[kb][...].reshape(-1, n))
                total = part if total is None else total + part
            self.stages[stage][slot] = total.astype(BF16)
            copy = pltpu.make_async_copy(
                self.stages[stage].at[slot], self.outs[j].at[rows], self.out_sems.at[2 * stage + slot]
            )
            copy.start()
            self.pending[(stage, slot)] = copy

    def end(self):
        self.step(len(self.units))
        for copy in self.pending.values():
            copy.wait()


def mid_kernel(middle, chunks, gathers, n_in, n_out, side, *refs):
    n_side, n_jobs = len(side.arrays), len(side.jobs)
    partial, ins = refs[0], refs[1 : 1 + n_in]
    side_ins, refs = refs[1 + n_in : 1 + n_in + n_side], refs[1 + n_in + n_side :]
    outs, refs = refs[:n_out], refs[n_out:]
    gathered = None
    if gathers:
        gathered, refs = refs[0], refs[1:]
    side_outs, refs = refs[:n_jobs], refs[n_jobs:]
    relay_x, relay_y, got_x, got_y, sum_x, sum_y, own, send_sems, recv_sems, local_sems = refs[:10]
    if n_jobs:
        side.bind(side_ins, side_outs, refs[10:])
    rows = partial.shape[1]
    r = rows // chunks
    h = r // 2
    by_x, by_y = plane_neighbours()
    plane_barrier(by_x, by_y)

    def copy(i, kind, src, dst, target):
        return pltpu.make_async_remote_copy(
            src_ref=src, dst_ref=dst, send_sem=send_sems.at[i, kind], recv_sem=recv_sems.at[i, kind],
            device_id=target, device_id_type=MESH,
        )

    def sends(i):
        lo, hi = pl.ds(i * r, h), pl.ds(i * r + h, h)
        half = pl.ds(i * h, h)
        made = {
            0: lambda: copy(i, 0, partial.at[3, lo], relay_x.at[half], by_x),
            1: lambda: copy(i, 1, partial.at[3, hi], relay_y.at[half], by_y),
            2: lambda: copy(i, 2, partial.at[1, lo], got_x.at[lo], by_x),
            3: lambda: copy(i, 3, partial.at[2, hi], got_y.at[hi], by_y),
            4: lambda: copy(i, 4, sum_y.at[half], got_y.at[lo], by_y),
            5: lambda: copy(i, 5, sum_x.at[half], got_x.at[hi], by_x),
        }
        if gathers:
            made |= {
                6: lambda: copy(i, 6, own.at[lo], gathered.at[1, lo], by_x),
                7: lambda: copy(i, 7, own.at[hi], gathered.at[2, hi], by_y),
                8: lambda: copy(i, 8, own.at[hi], gathered.at[1, hi], by_x),
                9: lambda: copy(i, 9, own.at[lo], gathered.at[2, lo], by_y),
                10: lambda: copy(i, 10, gathered.at[1, lo], gathered.at[3, lo], by_y),
                11: lambda: copy(i, 11, gathered.at[2, hi], gathered.at[3, hi], by_x),
            }
        return made

    def keep(i):
        span = pl.ds(i * r, r)
        return pltpu.make_async_copy(own.at[span], gathered.at[0, span], local_sems.at[i])

    def stage(n, i):
        s = sends(i)
        lo, hi = pl.ds(i * r, h), pl.ds(i * r + h, h)
        half, span = pl.ds(i * h, h), pl.ds(i * r, r)
        if n == 0:
            for kind in (0, 1, 2, 3):
                s[kind]().start()
        elif n == 1:
            s[0]().wait_recv()
            sum_y[half] = (partial[2, lo].astype(F32) + relay_x[half].astype(F32)).astype(BF16)
            s[4]().start()
            s[1]().wait_recv()
            sum_x[half] = (partial[1, hi].astype(F32) + relay_y[half].astype(F32)).astype(BF16)
            s[5]().start()
        elif n == 2:
            for kind in (2, 3, 4, 5):
                s[kind]().wait_recv()
            total = partial[0, span].astype(F32) + (got_x[span].astype(F32) + got_y[span].astype(F32))
            given = middle(total, span, ins, outs)
            if gathers:
                own[span] = given
                for kind in (6, 7, 8, 9):
                    s[kind]().start()
                keep(i).start()
        elif n == 3 and gathers:
            s[6]().wait_recv()
            s[10]().start()
            s[7]().wait_recv()
            s[11]().start()
        elif n == 4:
            if gathers:
                for kind in (8, 9, 10, 11):
                    s[kind]().wait_recv()
                keep(i).wait()
            for kind in s:
                s[kind]().wait_send()

    turns = chunks + 4
    if n_jobs:
        side.begin()
        each = -(-len(side.units) // turns)
    for t in range(turns):
        for n in range(5):
            if 0 <= t - n < chunks:
                stage(n, t - n)
        if n_jobs:
            side.step(each)
    if n_jobs:
        side.end()


def mid_call(middle, partial, ins, out_shapes, gathers, side, collective_id, chunks=4):
    _, rows, cols = partial.shape
    outs = tuple(out_shapes)
    specs = (VMEM,) * len(outs)
    if gathers:
        outs += (jax.ShapeDtypeStruct((4, rows, cols), BF16),)
        specs += (ANY,)
    outs += tuple(side.out_shapes())
    specs += (ANY,) * len(side.jobs)
    return pl.pallas_call(
        functools.partial(mid_kernel, middle, chunks, gathers, len(ins), len(out_shapes), side),
        out_shape=outs,
        in_specs=[VMEM] * (1 + len(ins)) + [ANY] * len(side.arrays),
        out_specs=specs,
        scratch_shapes=[
            pltpu.VMEM((rows // 2, cols), BF16),
            pltpu.VMEM((rows // 2, cols), BF16),
            pltpu.VMEM((rows, cols), BF16),
            pltpu.VMEM((rows, cols), BF16),
            pltpu.VMEM((rows // 2, cols), BF16),
            pltpu.VMEM((rows // 2, cols), BF16),
            pltpu.VMEM((rows, cols), BF16),
            pltpu.SemaphoreType.DMA((chunks, 12)),
            pltpu.SemaphoreType.DMA((chunks, 12)),
            pltpu.SemaphoreType.DMA((chunks,)),
        ]
        + (side.scratch() if side.jobs else []),
        compiler_params=pltpu.CompilerParams(
            collective_id=collective_id, has_side_effects=True, vmem_limit_bytes=60 * MIB
        ),
    )(partial, *ins, *side.arrays)


def start_kernel(
    tokens, small, marks, w_q, w_k, w_v,
    tokens_all, small_all, marks_all, w_cols, relay,
    send_sems, recv_sems, local_sems,
):
    f = lax.axis_index("fsdp")
    g = lax.axis_index("grp")
    core = lax.rem(g, 2)
    rows = tokens.shape[0]
    depth = w_q.shape[0]
    width = w_q.shape[1] // 4
    by_x, by_y = plane_neighbours()
    fx, fy = by_x["fsdp"], by_y["fsdp"]
    fd = fx + 2 - 4 * (fx // 2)
    by_d, sibling = {"fsdp": fd}, {"grp": g + 1 - 2 * core}
    barrier = pltpu.get_barrier_semaphore()
    for other in (by_x, by_y, by_d, sibling):
        pl.semaphore_signal(barrier, inc=1, device_id=other, device_id_type=MESH)
    pl.semaphore_wait(barrier, 4)

    def copy(n, src, dst, target):
        return pltpu.make_async_remote_copy(
            src_ref=src, dst_ref=dst, send_sem=send_sems.at[n], recv_sem=recv_sems.at[n],
            device_id=target, device_id_type=MESH,
        )

    def columns(j):
        return pl.ds(pl.multiple_of(j * width, width), width)

    def block_rows(owner, c):
        return pl.ds(pl.multiple_of(owner * depth + c * (depth // 2), depth // 2), depth // 2)

    half = depth // 2
    mine = pl.ds(pl.multiple_of(core * half, half), half)
    all_sends = []

    def go(c):
        c.start()
        all_sends.append(c)
        return c

    waits = []
    n = 0
    for k, target in ((1, by_x), (2, by_y), (3, by_d)):
        waits.append(go(copy(n, small, small_all.at[k], target)))
        waits.append(go(copy(n + 1, marks, marks_all.at[k], target)))
        n += 2
    locals_ = [
        pltpu.make_async_copy(small, small_all.at[0], local_sems.at[0]),
        pltpu.make_async_copy(marks, marks_all.at[0], local_sems.at[1]),
        pltpu.make_async_copy(tokens, tokens_all.at[0], local_sems.at[2]),
    ]
    for j, w in enumerate((w_q, w_k, w_v)):
        locals_.append(
            pltpu.make_async_copy(
                w.at[:, columns(f)],
                w_cols.at[pl.ds(pl.multiple_of(f * depth, depth), depth), pl.ds(j * width, width)],
                local_sems.at[3 + j],
            )
        )
    for c in locals_:
        c.start()

    quarter = half // 2
    first = pl.ds(pl.multiple_of(core * half, quarter), quarter)
    second = pl.ds(pl.multiple_of(core * half + quarter, quarter), quarter)
    relays_x, relays_y, direct_x, direct_y = [], [], [], []
    for j, w in enumerate((w_q, w_k, w_v)):
        relays_x.append(go(copy(n, w.at[first, columns(fd)], relay.at[0, j], by_x)))
        relays_y.append(go(copy(n + 1, w.at[second, columns(fd)], relay.at[1, j], by_y)))
        n += 2
    for j, w in enumerate((w_q, w_k, w_v)):
        place = w_cols.at[block_rows(f, core), pl.ds(j * width, width)]
        direct_x.append(go(copy(n, w.at[mine, columns(fx)], place, by_x)))
        direct_y.append(go(copy(n + 1, w.at[mine, columns(fy)], place, by_y)))
        n += 2
    low, high = pl.ds(0, rows // 2), pl.ds(rows // 2, rows // 2)
    t_x0 = go(copy(n, tokens.at[low], tokens_all.at[1, low], by_x))
    t_y1 = go(copy(n + 1, tokens.at[high], tokens_all.at[2, high], by_y))
    t_x1 = go(copy(n + 2, tokens.at[high], tokens_all.at[1, high], by_x))
    t_y0 = go(copy(n + 3, tokens.at[low], tokens_all.at[2, low], by_y))
    n += 4
    forwarded = []
    for j in range(3):
        relays_x[j].wait_recv()
        forwarded.append(
            go(copy(
                n, relay.at[0, j],
                w_cols.at[pl.ds(pl.multiple_of(fx * depth + core * half, quarter), quarter), pl.ds(j * width, width)],
                by_y,
            ))
        )
        relays_y[j].wait_recv()
        forwarded.append(
            go(copy(
                n + 1, relay.at[1, j],
                w_cols.at[pl.ds(pl.multiple_of(fy * depth + core * half + quarter, quarter), quarter), pl.ds(j * width, width)],
                by_x,
            ))
        )
        n += 2
    shares = []

    def share(owner):
        nonlocal n
        place = w_cols.at[block_rows(owner, core)]
        shares.append(go(copy(n, place, place, sibling)))
        n += 1

    for c in direct_x:
        c.wait_recv()
    share(fx)
    for c in direct_y:
        c.wait_recv()
    share(fy)
    t_x0.wait_recv()
    t_d0 = go(copy(n, tokens_all.at[1, low], tokens_all.at[3, low], by_y))
    t_y1.wait_recv()
    t_d1 = go(copy(n + 1, tokens_all.at[2, high], tokens_all.at[3, high], by_x))
    n += 2
    for c in forwarded:
        c.wait_recv()
    share(fd)
    for c in waits + shares + [t_x1, t_y0, t_d0, t_d1]:
        c.wait_recv()
    for c in locals_:
        c.wait()
    for c in all_sends:
        c.wait_send()


def start_call(tokens, small, marks, w_q, w_k, w_v, collective_id):
    depth, features = w_q.shape
    width = features // 4
    n = 6 + 6 + 6 + 4 + 6 + 2 + 3
    return pl.pallas_call(
        start_kernel,
        out_shape=(
            jax.ShapeDtypeStruct((4,) + tokens.shape, tokens.dtype),
            jax.ShapeDtypeStruct((4,) + small.shape, small.dtype),
            jax.ShapeDtypeStruct((4,) + marks.shape, marks.dtype),
            jax.ShapeDtypeStruct((4 * depth, 3 * width), BF16),
            jax.ShapeDtypeStruct((2, 3, depth // 4, width), BF16),
        ),
        in_specs=[ANY] * 6,
        out_specs=(ANY,) * 5,
        scratch_shapes=[
            pltpu.SemaphoreType.DMA((n,)),
            pltpu.SemaphoreType.DMA((n,)),
            pltpu.SemaphoreType.DMA((6,)),
        ],
        compiler_params=pltpu.CompilerParams(
            collective_id=collective_id, has_side_effects=True, vmem_limit_bytes=16 * MIB
        ),
    )(tokens, small, marks, w_q, w_k, w_v)[:4]


def turn_half(x):
    return pltpu.roll(x, HEAD_DIM // 2, 1)


def hidden_bias(of_keys, of_queries):
    key_segment, key_position = of_keys[0], of_keys[4]
    seen = (
        (key_segment == of_queries[1]) | (key_segment == of_queries[2]) | (key_segment == of_queries[3])
    ) & (key_position <= of_queries[4])
    return jnp.where(seen, 0.0, MASK_FILL)


def attend_kernel(
    tokens, gain, w_cols, bias, w_out, cosine, sine, mark_cols, mark_rows,
    normed, three, attended, branch, mask,
):
    count = tokens.shape[0]
    width = w_out.shape[0]
    scale = HEAD_DIM**-0.5
    step = 256
    rows_of = [mark_rows[j : j + 1, :] for j in range(5)]
    for a, n in pieces(count, step):
        s = pl.ds(a, n)
        x = tokens[s, :].astype(F32)
        factor = lax.rsqrt(jnp.mean(x * x, axis=-1, keepdims=True) + EPSILON)
        normed[s, :] = (x * factor * gain[...]).astype(BF16)
        cols_of = [mark_cols[s, j : j + 1] for j in range(5)]
        mask[s, :] = hidden_bias(rows_of, cols_of)
    for b, m in pieces(3 * width, 256):
        c = pl.ds(b, m)
        pre = plain_dot(normed[...], w_cols[:, c]) + bias[:, c]
        if b < 2 * width:
            for d in range(0, m, HEAD_DIM):
                x = pre[:, d : d + HEAD_DIM]
                three[:, b + d : b + d + HEAD_DIM] = (
                    x * cosine[...] + turn_half(x) * sine[...]
                ).astype(BF16)
        else:
            three[:, c] = pre.astype(BF16)
    for h in range(width // HEAD_DIM):
        q_cols = pl.ds(h * HEAD_DIM, HEAD_DIM)
        k_cols = pl.ds(width + h * HEAD_DIM, HEAD_DIM)
        v_cols = pl.ds(2 * width + h * HEAD_DIM, HEAD_DIM)
        for a, n in pieces(count, step):
            s = pl.ds(a, n)
            scores = trans_dot(three[s, q_cols], three[:, k_cols]) + mask[s, :]
            peak = jnp.max(scores, axis=-1, keepdims=True)
            expo = jnp.exp((scores - peak) * scale)
            total = jnp.sum(expo, axis=-1, keepdims=True)
            weights = (expo * (1.0 / total)).astype(BF16)
            attended[s, q_cols] = plain_dot(weights, three[:, v_cols]).astype(BF16)
    for b, m in pieces(w_out.shape[1], 512):
        c = pl.ds(b, m)
        branch[:, c] = plain_dot(attended[...], w_out[:, c]).astype(BF16)


def attend_call(tokens, gain, w_cols, bias, w_out, cosine, sine, mark_cols, mark_rows):
    count, features = tokens.shape
    width = w_out.shape[0]

    def shape(cols):
        return jax.ShapeDtypeStruct((count, cols), BF16)

    return pl.pallas_call(
        attend_kernel,
        in_specs=[VMEM] * 9,
        out_specs=(VMEM,) * 4,
        out_shape=(shape(features), shape(3 * width), shape(width), shape(features)),
        scratch_shapes=[pltpu.VMEM((count, count), F32)],
        compiler_params=pltpu.CompilerParams(vmem_limit_bytes=60 * MIB),
    )(tokens, gain, w_cols, bias, w_out, cosine, sine, mark_cols, mark_rows)


def attend_back_kernel(
    grad, w_out, three, w_cols, cosine, sine, mark_cols, mark_rows,
    grad_three, partial, grad_bias, mask, grad_att,
):
    count = grad.shape[0]
    width = w_out.shape[0]
    scale = HEAD_DIM**-0.5
    step = 256
    for b, m in pieces(width, 256):
        c = pl.ds(b, m)
        grad_att[:, c] = trans_dot(grad[...], w_out[c, :]).astype(BF16)
    rows_of = [mark_rows[j : j + 1, :] for j in range(5)]
    for a, n in pieces(count, step):
        s = pl.ds(a, n)
        mask[s, :] = hidden_bias([mark_cols[s, j : j + 1] for j in range(5)], rows_of)
    for h in range(width // HEAD_DIM):
        q_cols = pl.ds(h * HEAD_DIM, HEAD_DIM)
        k_cols = pl.ds(width + h * HEAD_DIM, HEAD_DIM)
        v_cols = pl.ds(2 * width + h * HEAD_DIM, HEAD_DIM)
        grad_k = grad_v = None
        for a, n in pieces(count, step):
            s = pl.ds(a, n)
            query, g = three[s, q_cols], grad_att[s, q_cols]
            scores = trans_dot(three[:, k_cols], query) + mask[:, s]
            peak = jnp.max(scores, axis=0, keepdims=True)
            expo = jnp.exp((scores - peak) * scale)
            probs = expo * (1.0 / jnp.sum(expo, axis=0, keepdims=True))
            weight_grad = trans_dot(three[:, v_cols], g)
            diagonal = jnp.sum(probs * weight_grad, axis=0, keepdims=True)
            score_grad = (probs * (weight_grad - diagonal)).astype(BF16)
            part_v = plain_dot(probs.astype(BF16), g)
            part_k = plain_dot(score_grad, query)
            grad_v = part_v if grad_v is None else grad_v + part_v
            grad_k = part_k if grad_k is None else grad_k + part_k
            grad_q = rows_dot(score_grad, three[:, k_cols]) * scale
            grad_three[s, q_cols] = (
                grad_q * cosine[s, :] - turn_half(grad_q) * sine[s, :]
            ).astype(BF16)
        grad_k = grad_k * scale
        grad_three[:, k_cols] = (grad_k * cosine[...] - turn_half(grad_k) * sine[...]).astype(BF16)
        grad_three[:, v_cols] = grad_v.astype(BF16)
    for b, m in pieces(3 * width, 512):
        c = pl.ds(b, m)
        grad_bias[:, c] = jnp.sum(grad_three[:, c].astype(F32), axis=0, keepdims=True)
    for b, m in pieces(w_cols.shape[0], 512):
        c = pl.ds(b, m)
        partial[:, c] = trans_dot(grad_three[...], w_cols[c, :]).astype(BF16)


def attend_back_call(grad, w_out, three, w_cols, cosine, sine, mark_cols, mark_rows):
    count, features = grad.shape
    width = w_out.shape[0]

    def shape(rows, cols, dtype=BF16):
        return jax.ShapeDtypeStruct((rows, cols), dtype)

    return pl.pallas_call(
        attend_back_kernel,
        in_specs=[VMEM] * 8,
        out_specs=(VMEM,) * 3,
        out_shape=(shape(count, 3 * width), shape(count, features), shape(1, 3 * width, F32)),
        scratch_shapes=[pltpu.VMEM((count, count), F32), pltpu.VMEM((count, width), BF16)],
        compiler_params=pltpu.CompilerParams(vmem_limit_bytes=60 * MIB),
    )(grad, w_out, three, w_cols, cosine, sine, mark_cols, mark_rows)


class Load:
    def __init__(self, value):
        self.value = value

    def __getitem__(self, place):
        return self.value[place]


class Store:
    def __init__(self, shape):
        self.value = jnp.zeros(shape.shape, shape.dtype)

    def __getitem__(self, place):
        return self.value[place]

    def __setitem__(self, place, value):
        self.value = value.astype(self.value.dtype)


def first_middle(total, span, ins, outs):
    tokens, gain = ins
    mixed = tokens[span].astype(F32) + total
    factor = lax.rsqrt(jnp.mean(mixed * mixed, axis=-1, keepdims=True) + EPSILON)
    outs[0][span] = mixed
    return (mixed * factor * gain[...]).astype(BF16)


def norm_back(values, gain, grad):
    factor = lax.rsqrt(jnp.mean(values * values, axis=-1, keepdims=True) + EPSILON)
    weighted = gain * grad
    back = factor * weighted - values * (factor * factor * factor) * jnp.mean(
        weighted * values, axis=-1, keepdims=True
    )
    return back, jnp.sum(grad * values * factor, axis=0, keepdims=True)


def back_middle(total, span, ins, outs):
    values, gain, base = ins
    back, grad_gain = norm_back(values[span].astype(F32), gain[...], total)
    grad = base[span].astype(F32) + back
    outs[0][span] = grad
    outs[1][span if span == slice(None) else pl.ds(span.start // span.size, 1)] = grad_gain
    return grad.astype(BF16)


class Wires:
    def __init__(self, mesh):
        self.nf = mesh.shape["fsdp"]
        self.ng = mesh.shape["grp"]
        self.nz = self.ng // 2
        self.fast = self.nf == 4 and self.ng == 8
        self.chunks = 4 if self.fast else 1

    def xor(self, value, k):
        return lax.ppermute(value, "fsdp", [(i, i ^ k) for i in range(self.nf)])

    def inwards(self, value):
        if not self.fast:
            return None
        return lax.ppermute(value, "grp", [(0, 2), (1, 3), (6, 4), (7, 5)])

    def gather_list(self, value):
        return [value] + [self.xor(value, k) for k in range(1, self.nf)]

    def gather(self, value):
        return jnp.concatenate(self.gather_list(value), axis=0)

    def scatter_sum(self, value):
        rows = value.shape[0] // self.nf
        total = value[:rows].astype(F32)
        for k in range(1, self.nf):
            part = value[k * rows : (k + 1) * rows].astype(BF16)
            total = total + self.xor(part, k).astype(F32)
        return total

    def reduce_background(self, partial):
        return lax.psum_scatter(partial, "grp", scatter_dimension=0, tiled=True)

    def gather_start(self, tokens, small, marks, weights):
        if self.fast:
            return start_call(tokens, small, marks, *weights, 1)
        cols = jnp.concatenate(
            [lax.all_to_all(w, "fsdp", split_axis=1, concat_axis=0, tiled=True) for w in weights],
            axis=1,
        )
        return tuple(jnp.stack(self.gather_list(v)) for v in (tokens, small, marks)) + (cols,)

    def middle(self, body, partial, ins, out_shapes, gathers, number, arrays=(), jobs=()):
        nf = self.nf
        rows, cols = partial.shape[0] // nf, partial.shape[1]
        if self.fast:
            side = Side(arrays, jobs)
            return mid_call(body, partial.reshape(nf, rows, cols), ins, out_shapes, gathers, side, number)
        total = self.scatter_sum(partial)
        outs = [Store(s) for s in out_shapes]
        given = body(total, slice(None), [Load(v) for v in ins], outs)
        results = tuple(o.value for o in outs)
        if gathers:
            results += (jnp.stack(self.gather_list(given)),)

        def operand(o):
            number, axis, entry = o
            v = arrays[number] if axis is None else lax.index_in_dim(arrays[number], entry, axis, False)
            return v.reshape(-1, v.shape[-1])

        return results + tuple(
            sum(rows_dot(operand(a), operand(b)) for a, b in job).astype(BF16) for job in jobs
        )

    def last_sums(self, downs, shared, part_three, part_output, out_part, mixed, vec, bias_add, number):
        nf, ng, nz = self.nf, self.ng, self.nz
        features, width = part_output.shape
        share = features // ng
        if self.fast:
            outs = line_call(
                [v.reshape(nz, 2, share, -1) for v in downs],
                [v.reshape(nz, 2, share, -1) for v in shared],
                part_three.reshape(3, 2, share, features),
                part_output.reshape(nz, 2, share, width),
                out_part.reshape(nf, -1, features),
                mixed,
                vec.reshape(16, nf, width).transpose(1, 0, 2),
                bias_add,
                2,
                True,
                number,
            )
            return outs[0], outs[1:4], outs[4], outs[5], outs[6]
        down = jnp.stack([self.reduce_background(v).astype(F32).T for v in downs], axis=0)
        sums = [self.reduce_background(v).astype(F32) for v in shared]
        three = lax.all_to_all(
            part_three.reshape(3, width, features), "fsdp", split_axis=2, concat_axis=1, tiled=True
        )
        four = jnp.concatenate([three, part_output[None]], axis=0)
        four = lax.psum_scatter(four, "grp", scatter_dimension=1, tiled=True).astype(F32)
        vec = lax.psum_scatter(vec, "fsdp", scatter_dimension=1, tiled=True) + bias_add
        output = (mixed + self.scatter_sum(out_part)).astype(BF16)
        return down, (sums[0], sums[1], sums[2].T), four.transpose(0, 2, 1), output, lax.psum(vec, "grp")


def on_device(
    wires,
    tokens,
    cotangent,
    segment,
    ancestry,
    position,
    routes,
    attn_gain,
    w_query,
    w_key,
    w_value,
    b_query,
    b_key,
    b_value,
    w_output,
    moe_gain,
    w_router,
    shared_switch,
    shared_gate,
    shared_up,
    shared_down,
    expert_gate,
    routed_up_weight,
    expert_down,
):
    nf, ng = wires.nf, wires.ng
    me = lax.axis_index("fsdp")
    rows_dev, features = tokens.shape
    count = rows_dev * nf
    width = features // nf
    experts = w_router.shape[1]
    local_experts = experts // nf
    capacity = 5 * rows_dev // 8
    choose = routes.shape[1]

    small = jnp.concatenate([attn_gain[None], moe_gain[None], w_router.T, shared_switch[None]], axis=0)
    small = jnp.pad(small, ((0, -small.shape[0] % 16), (0, 0)))
    marks = jnp.concatenate([segment[None], ancestry.T, position[None], routes.T], axis=0)
    marks = jnp.pad(marks, ((0, -marks.shape[0] % 16), (0, 0)))
    tokens_all, small_blocks, marks_all, w_cols = wires.gather_start(
        tokens, small, marks, (w_query, w_key, w_value)
    )
    tokens_all = tokens_all.reshape(count, features)
    small_all = jnp.concatenate(
        [lax.dynamic_index_in_dim(small_blocks, me ^ i, 0, keepdims=False) for i in range(nf)], axis=1
    )
    gain_one = small_all[0:1].astype(F32)
    gain_two = small_all[1:2].astype(F32)
    heads_rows = small_all[2 : experts + 3]
    mark_rows = jnp.concatenate([marks_all[k] for k in range(nf)], axis=1)
    mark_cols = mark_rows.T
    routes_rows = mark_rows[5 : 5 + choose]

    tokens_all, cotangent = lax.optimization_barrier((tokens_all, cotangent))
    cot_all = wires.gather(cotangent)

    halfway = HEAD_DIM // 2
    freqs = ROPE_BASE ** (-(jnp.arange(halfway, dtype=F32) * 2.0 / HEAD_DIM))
    turns = mark_cols[:, 4:5].astype(F32) * jnp.concatenate([freqs, freqs])[None, :]
    cosine = jnp.cos(turns)
    sine = jnp.sin(turns) * jnp.where(jnp.arange(HEAD_DIM) < halfway, -1.0, 1.0)[None, :]
    bias = jnp.concatenate([b_query, b_key, b_value]).astype(F32)[None]
    normed, three, attended, branch = attend_call(
        tokens_all, gain_one, w_cols, bias, w_output, cosine, sine, mark_cols, mark_rows
    )

    numbers = me * local_experts + jnp.arange(local_experts, dtype=jnp.int32)
    named = jnp.any(routes_rows[None] == numbers[:, None, None], axis=1)
    named = named.reshape(local_experts, nf, rows_dev)
    earlier = (jnp.arange(rows_dev)[None, :] < jnp.arange(rows_dev)[:, None]).astype(BF16)
    slot = jnp.einsum("ts,ebs->bet", earlier, named.astype(BF16), preferred_element_type=F32)
    slot = jnp.where(named.transpose(1, 0, 2), slot.astype(jnp.int32), -1)
    pick = jnp.arange(capacity, dtype=jnp.int32)[None, None, :, None] == slot[:, :, None, :]
    pick_b = pick.astype(BF16).reshape(nf, local_experts * capacity, rows_dev)

    branch, cot_all = lax.optimization_barrier((branch, cot_all))
    cot_other = wires.inwards(cot_all)
    mixed, moe_blocks = wires.middle(
        first_middle,
        branch,
        (tokens, gain_two),
        (jax.ShapeDtypeStruct((rows_dev, features), F32),),
        True,
        2,
    )
    moe_in = moe_blocks.reshape(count, features)
    moe_other = wires.inwards(moe_in)

    head_pre = trans_dot(moe_in, heads_rows)
    router_probs = jax.nn.softmax(head_pre[:, :experts], axis=-1)
    opener = jax.nn.sigmoid(head_pre[:, experts:])
    local = jnp.stack(
        [
            jnp.sum(jnp.where(jnp.arange(experts)[None] == numbers[i], router_probs, 0.0), axis=1)
            for i in range(local_experts)
        ],
        axis=0,
    )
    local = local.reshape(local_experts, nf, rows_dev).transpose(1, 0, 2)
    gate = jnp.sum(jnp.where(pick, local[:, :, None, :], 0.0), axis=3, keepdims=True)

    def dispatch(x):
        return jnp.einsum(
            "bst,btd->bsd", pick_b, x.reshape(nf, rows_dev, -1), preferred_element_type=F32
        ).astype(BF16)

    shape = (nf, local_experts, capacity, -1)
    rows_in = dispatch(moe_in).reshape(shape)
    rows_cot = dispatch(cot_all).reshape(shape)
    if wires.fast:
        rows_cot, cot_other = lax.optimization_barrier((rows_cot, cot_other))
    hidden, d_gate, d_up, d_out, y_rows, dx_rows, sens_rows = expert_call(
        rows_in, rows_cot, gate, expert_gate, routed_up_weight, expert_down, nf // 2
    )

    def slot_rows(x, i):
        return x[:, i].reshape(nf * capacity, features)

    gate_parts = [rows_dot(slot_rows(rows_in, i), d_gate[i]).astype(BF16) for i in range(local_experts)]
    up_part = rows_dot(slot_rows(rows_in, 0), d_up[0]).astype(BF16)
    gate_parts, up_part, hidden, sens_rows, y_rows, moe_other = lax.optimization_barrier(
        (gate_parts, up_part, hidden, sens_rows, y_rows, moe_other)
    )
    gate_sums = [wires.reduce_background(v) for v in gate_parts]
    up_sums = [wires.reduce_background(up_part)]

    gate_grad = jnp.sum(jnp.where(pick, sens_rows, 0.0), axis=2)
    gate_grad = gate_grad.transpose(1, 0, 2).reshape(local_experts, count)
    prob_grad = sum(
        jnp.where(jnp.arange(experts)[None] == numbers[i], gate_grad[i][:, None], 0.0)
        for i in range(local_experts)
    )
    logit_grad = router_probs * (
        prob_grad - jnp.sum(prob_grad * router_probs, axis=-1, keepdims=True)
    )
    high = logit_grad.astype(BF16)
    lanes = jnp.concatenate([high, (logit_grad - high.astype(F32)).astype(BF16)], axis=1)
    router_rows = heads_rows[:experts]
    taken = (nf, local_experts * capacity, features)
    s_hidden, sd_gate, sd_up, sd_out, out_part, moe_part, gate_sens = shared_call(
        moe_in,
        cot_all,
        opener,
        pick_b,
        y_rows.reshape(taken),
        dx_rows.reshape(taken),
        lanes,
        jnp.concatenate([router_rows, router_rows], axis=0),
        heads_rows[experts:].astype(F32),
        shared_gate,
        shared_up,
        shared_down,
    )
    sens_high = gate_sens.astype(BF16)
    sens_low = (gate_sens - sens_high.astype(F32)).astype(BF16)
    grad_heads = rows_dot(jnp.concatenate([lanes, sens_high, sens_low], axis=1), moe_in)
    grad_heads = jnp.concatenate(
        [
            grad_heads[:experts] + grad_heads[experts : 2 * experts],
            grad_heads[2 * experts : 2 * experts + 1] + grad_heads[2 * experts + 1 :],
        ],
        axis=0,
    )
    arrays = (rows_in, d_gate, d_up, moe_in, sd_gate, sd_up, sd_out)
    if wires.fast:
        o_hidden, od_gate, od_up, od_out = other_call(
            moe_other, cot_other, heads_rows, shared_gate, shared_up, shared_down, rows_dev
        )
        arrays += (moe_other, od_gate, od_up, s_hidden, od_out, o_hidden)
    else:
        arrays += (None, None, None, s_hidden)
    jobs = []
    for i in range(1, local_experts):
        jobs += [(((0, 1, i), (2, 0, i)),)]

    def whole(*numbers):
        return tuple((n, None, 0) for n in numbers)

    if wires.fast:
        jobs += [(whole(3, 4), whole(7, 8)), (whole(3, 5), whole(7, 9)), (whole(6, 10), whole(11, 12))]
    else:
        jobs += [(whole(3, 4),), (whole(3, 5),), (whole(6, 10),)]
    grad_mixed, grad_gain_two, branch_grad, *parts = wires.middle(
        back_middle,
        moe_part,
        (mixed, gain_two, cotangent),
        (
            jax.ShapeDtypeStruct((rows_dev, features), F32),
            jax.ShapeDtypeStruct((wires.chunks, features), F32),
        ),
        True,
        3,
        arrays,
        jobs,
    )
    late = local_experts - 1
    parts, up_sums = lax.optimization_barrier((parts, up_sums))
    up_sums += [wires.reduce_background(v) for v in parts[:late]]
    shared_parts = parts[late:]
    branch_grad = branch_grad.reshape(count, features)
    grad_three, normed_part, grad_bias = attend_back_call(
        branch_grad, w_output, three, w_cols, cosine, sine, mark_cols, mark_rows
    )
    grad_tokens, grad_gain_one, part_output, part_three, *down_parts = wires.middle(
        back_middle,
        normed_part,
        (tokens, gain_one, grad_mixed),
        (
            jax.ShapeDtypeStruct((rows_dev, features), F32),
            jax.ShapeDtypeStruct((wires.chunks, features), F32),
        ),
        False,
        4,
        (branch_grad, attended, grad_three, normed, d_out, hidden),
        [(whole(0, 1),), (whole(2, 3),)] + [(((4, 1, i), (5, 0, i)),) for i in range(local_experts)],
    )

    vec = jnp.concatenate(
        [
            jnp.sum(grad_gain_one, axis=0, keepdims=True),
            jnp.sum(grad_gain_two, axis=0, keepdims=True),
            grad_heads,
        ],
        axis=0,
    )
    vec = jnp.pad(vec, ((0, 16 - vec.shape[0]), (0, 0)))
    bias_add = jnp.pad(grad_bias.reshape(3, width), ((experts + 3, 16 - experts - 6), (0, 0)))
    down_sums, shared_sums, four, output, vec = wires.last_sums(
        down_parts, shared_parts, part_three, part_output, out_part, mixed, vec, bias_add, 5
    )
    own = width // ng
    vec = lax.dynamic_slice_in_dim(vec, lax.axis_index("grp") * own, own, 1)
    return (
        output,
        grad_tokens,
        vec[0],
        four[0],
        four[1],
        four[2],
        vec[experts + 3],
        vec[experts + 4],
        vec[experts + 5],
        four[3],
        vec[1],
        vec[2 : experts + 2].T,
        vec[experts + 2],
        shared_sums[0],
        shared_sums[1],
        shared_sums[2],
        jnp.stack(gate_sums, axis=0).astype(F32),
        jnp.stack(up_sums, axis=0).astype(F32),
        down_sums,
    )


def solution(mesh):
    wires = Wires(mesh)

    def step(*args):
        return on_device(wires, *args)

    rows = P(("grp", "fsdp"))
    shard = P("fsdp")
    small = P(("fsdp", "grp"))
    return jax.shard_map(
        step,
        mesh=mesh,
        in_specs=(rows,) * 6
        + (shard,) * 11
        + (P(None, "fsdp"), P(None, "fsdp"), shard, shard, shard, shard),
        out_specs=(
            rows,
            rows,
            small,
            P("fsdp", "grp"),
            P("fsdp", "grp"),
            P("fsdp", "grp"),
            small,
            small,
            small,
            P("fsdp", "grp"),
            small,
            small,
            small,
            P("grp", "fsdp"),
            P("grp", "fsdp"),
            P("fsdp", "grp"),
            P("fsdp", "grp", None),
            P("fsdp", "grp", None),
            P("fsdp", None, "grp"),
        ),
        check_vma=False,
    )
```

time: 1340 us -> 902 us (0.67)
  matrix products: 359 us -> 43.7 us
  local copies, waits for them, and re-layouts: 148 us -> 37.4 us
  Pallas kernels: 638 us -> 746 us
  other arithmetic: 89.7 us -> 23.3 us
  waiting for transfers between devices: 62.5 us -> 11.7 us
    dot_general x36 -> x5, matrix products: 293 us -> 31.9 us  [dot(): lax.dot_general(left, right, (dims, ((), ())), preferred_element_type=out)]
    pallas_call x2 -> x6, Pallas kernels: 384 us -> 459 us  [the longest x1 245 us: line_call(): pl.pallas_call(functools.partial(line_kernel, m, s, parts, shift), out_sh...]
    reduce_scatter x4, waiting for transfers between devices: 54.2 us -> 0.03 us  [reduce_background(): return lax.psum_scatter(partial, 'grp', scatter_dimension=0, tiled=True)]
    dot_general x16 -> x3, matrix products: 65.8 us -> 11.9 us  [the longest x2 11.7 us: dispatch(): jnp.einsum('bst,btd->bsd', pick_b, x.reshape(nf, rows_dev, -1), preferred...]
    unnamed x260 -> x49, local copies, waits for them, and re-layouts: 68.3 us -> 19.8 us
    pallas_call x3, Pallas kernels: 179 us -> 213 us  [mid_call(): pl.pallas_call(functools.partial(mid_kernel, middle, chunks, gathers, len...]
    convert_element_type x13 -> x6, other arithmetic: 41.2 us -> 7.74 us  [the longest x1 3.24 us: on_device(): jnp.stack(up_sums, axis=0).astype(F32)]
    another operation x4 -> x0, other arithmetic: 21.1 us -> none
  transfers between devices with their start and end apart: 14 -> 9, of which waited for: 3 -> 2; matrix products, arithmetic and copies ran while one was open for 23% -> 8% of each run, Pallas kernels for 5% -> 76%
where the time goes in v2:
time: 902 us; the launch traced here: 889 us
  Pallas kernels  746 us (83%)
  matrix products  43.7 us (5%)
  local copies, waits for them, and re-layouts  37.4 us (4%)
  other arithmetic  23.3 us (3%)
  between operations  14.3 us (2%)
  starting transfers between devices  12.4 us (1%)
  waiting for transfers between devices  11.7 us (1%)
    pallas_call x1, Pallas kernels, line_call(): pl.pallas_call(functools.partial(line_kernel, m, s, parts, shift), out_sh...  245 us
    pallas_call x3, Pallas kernels, mid_call(): pl.pallas_call(functools.partial(mid_kernel, middle, chunks, gathers, len...  213 us
    pallas_call x1, Pallas kernels, start_call(): pl.pallas_call(start_kernel, out_shape=(jax.ShapeDtypeStruct((4,) + token...  74.4 us
    pallas_call x1, Pallas kernels, expert_call(): pl.pallas_call(expert_kernel, grid=(experts, steps), in_specs=[slot_spec(...  59.9 us
    pallas_call x1, Pallas kernels, shared_call(): pl.pallas_call(shared_kernel, grid=(blocks,), in_specs=[rows_spec(feature...  57 us
    pallas_call x1, Pallas kernels, attend_back_call(): pl.pallas_call(attend_back_kernel, in_specs=[VMEM] * 8, out_specs=(VMEM,)...  38.6 us
    dot_general x5, matrix products, dot(): lax.dot_general(left, right, (dims, ((), ())), preferred_element_type=out)  31.9 us
    pallas_call x1, Pallas kernels, other_call(): pl.pallas_call(other_kernel, grid=(count // tile,), in_specs=[rows_spec(f...  30 us
  transfers between devices with their start and end apart: 9, of which 2 were waited for; matrix products, arithmetic and copies ran while one was open for 8% of the time, Pallas kernels for 76%

profile of v2, /device:TPU:0, one launch (start us, length us, event | category | flops | bytes accessed | tf_op | source)
XLA Modules:
  0.0 889.3 jit_solution(802743718489292)
XLA Ops:
  10.8 1.2 copy-done.1
  12.0 1.6 copy-done.3
  13.6 1.6 copy-done.4
  15.2 1.6 copy-done.5
  16.8 74.4 %shard_map.366 = (bf16[4,256,2048]{2,1,0:T(8,128)(2,1)S(1)}, bf16[4,16,512]{2,1,0:T(8,128)(2,1)S(1)}, s32[4,16,256]{2,1,0:T(8,128)S(1)}, bf16[2048,1536]{1,0:T(8,128)(2,1)S(1)}, bf16[2,3,128,512]{3,2,1,0:T(8,128)(2,1)}) custom-call(bf16[256,2048]{1,0:T(8,128)(2,1)S(1)} %copy-done.1, bf16[16,512]{1,0:T(8,128)(2,1)S(1)} %fusion.28.small, ...), custom_call_target="tpu_custom_call" | custom-call | tf_op jit(solution)/shard_map/pallas_call | solution.py:1178
  91.2 2.7 copy-done
  93.9 2.0 copy-done.2
  95.9 1.5 collective-permute-start.2
  97.4 1.5 collective-permute-start.1
  100.2 1.0 copy.72.mark_cols
  102.4 3.1 fusion.8
  105.5 28.1 %shard_map.367 = (bf16[1024,2048]{1,0:T(8,128)(2,1)}, bf16[1024,1536]{1,0:T(8,128)(2,1)}, bf16[1024,512]{1,0:T(8,128)(2,1)}, bf16[1024,2048]{1,0:T(8,128)(2,1)}) custom-call(bf16[1024,2048]{1,0:T(8,128)(2,1)} %bitcast.118, f32[1,2048]{1,0:T(1,128)} %get-tuple-element.171.gain.refs_2_, bf16[2048,1536]{1,0:T(8,128)(2,1)} %copy-done, ...), custom_call_target="tpu_custom_call" | custom-call | tf_op jit(solution)/shard_map/pallas_call | solution.py:1263
  133.6 10.0 %collective-permute-done.1 = bf16[256,2048]{1,0:T(8,128)(2,1)S(1)} collective-permute-done((bf16[256,2048]{1,0:T(8,128)(2,1)S(1)}, bf16[256,2048]{1,0:T(8,128)(2,1)S(1)}, u32[]{:S(2)}, u32[]{:S(2)}) %collective-permute-start.1) | collective-permute-done | bytes 1048608 | tf_op jit(solution)/shard_map/ppermute | solution.py:1393
  143.8 3.3 pad_maximum_fusion.g_ref
  147.1 5.5 collective-permute-start.3
  153.9 1.1 bitcast_compare_fusion
  155.6 1.3 iota_compare_fusion.4
  156.9 74.5 %shard_map.368 = (f32[256,2048]{1,0:T(8,128)}, bf16[4,256,2048]{2,1,0:T(8,128)(2,1)}) custom-call(bf16[4,256,2048]{2,1,0:T(8,128)(2,1)} %bitcast.139, bf16[256,2048]{1,0:T(8,128)(2,1)} %refs_1_.3, f32[1,2048]{1,0:T(1,128)} %get-tuple-element.170.refs_2_), custom_call_target="tpu_custom_call" | custom-call | tf_op jit(solution)/shard_map/pallas_call | solution.py:1019
  231.4 3.3 collective-permute-start.4
  234.7 3.4 fusion.31
  238.6 1.1 copy.77.gate_ref
  239.7 3.7 convolution_convert_fusion.4
  243.5 8.0 convolution_convert_fusion.3
  251.5 3.0 fusion.35
  254.5 59.9 %shard_map.369 = (bf16[2,640,1408]{2,1,0:T(8,128)(2,1)}, bf16[2,640,1408]{2,1,0:T(8,128)(2,1)}, bf16[2,640,1408]{2,1,0:T(8,128)(2,1)}, bf16[4,2,160,2048]{3,2,1,...) custom-call(bf16[4,2,160,2048]{3,2,1,0:T(8,128)(2,1)} %bitcast.125, ...), custom_call_target="tpu_custom_call" | custom-call | tf_op jit(solution)/shard_map/pallas_call | solution.py:101
  314.4 9.1 %convolution_convert_fusion.1 = bf16[2048,1408]{1,0:T(8,128)(2,1)} fusion(bf16[640,2048]{1,0:T(8,128)(2,1)} %bitcast.144, bf16[2,640,1408]{2,1,0:T(8,128)(2,1)} %get-tuple-element.99.refs_5_), kind=kOutput, calls=%fused_computation.1 | convolution fusion | flops 3693871104 | bytes 10190848 | tf_op jit(solution)/shard_map/dot_general | solution.py:25
  323.5 8.3 convolution_convert_fusion.2
  331.8 8.2 convolution_convert_fusion
  343.1 0.9 add_divide_fusion.head_ref
  345.8 30.0 %shard_map.371 = (bf16[1024,1408]{1,0:T(8,128)(2,1)}, bf16[1024,1408]{1,0:T(8,128)(2,1)}, bf16[1024,1408]{1,0:T(8,128)(2,1)}, bf16[1024,2048]{1,0:T(8,128)(2,1)}) custom-call(bf16[1024,2048]{1,0:T(8,128)(2,1)} %collective-permute-done.4.x_ref.refs_11_, bf16[1024,2048]{1,0:T(8,128)(2,1)} %collective-permute-done.3.g_ref, bf16[9,2048]{1,0:T(8,128)(2,1)} %slice.156.heads, ...), custom_call_target="tpu_custom_call" | custom-call | tf_op jit(solution)/shard_map/pallas_call | solution.py:206
  375.8 57.0 %shard_map.370 = (bf16[1024,1408]{1,0:T(8,128)(2,1)}, bf16[1024,1408]{1,0:T(8,128)(2,1)}, bf16[1024,1408]{1,0:T(8,128)(2,1)}, bf16[1024,2048]{1,0:T(8,128)(2,1)}...) custom-call(bf16[1024,2048]{1,0:T(8,128)(2,1)} %bitcast.121, ...), custom_call_target="tpu_custom_call" | custom-call | tf_op jit(solution)/shard_map/pallas_call | solution.py:162
  432.8 87.5 %shard_map.372 = (f32[256,2048]{1,0:T(8,128)}, f32[4,2048]{1,0:T(4,128)}, bf16[4,256,2048]{2,1,0:T(8,128)(2,1)}, bf16[2048,1408]{1,0:T(8,128)(2,1)}, bf16[2048,1...) custom-call(bf16[4,256,2048]{2,1,0:T(8,128)(2,1)} %bitcast.141, ...), custom_call_target="tpu_custom_call" | custom-call | tf_op jit(solution)/shard_map/pallas_call | solution.py:1019
  520.3 1.0 copy-done.16
  521.7 38.6 %shard_map.373 = (bf16[1024,1536]{1,0:T(8,128)(2,1)}, bf16[1024,2048]{1,0:T(8,128)(2,1)}, f32[1,1536]{1,0:T(1,128)}) custom-call(bf16[1024,2048]{1,0:T(8,128)(2,1)} %bitcast.128, bf16[512,2048]{1,0:T(8,128)(2,1)} %w_out.3, bf16[1024,1536]{1,0:T(8,128)(2,1)} %get-tuple-element.120.three, bf16[2048,1536]{1,0:T(8,128)(2,1)} %copy-done, ...), custom_call_target="tpu_custom_call" | custom-call | tf_op jit(solution)/shard_map/pallas_call | solution.py:1329
  561.0 51.5 %shard_map.374 = (f32[256,2048]{1,0:T(8,128)}, f32[4,2048]{1,0:T(4,128)}, bf16[2048,512]{1,0:T(8,128)(2,1)}, bf16[1536,2048]{1,0:T(8,128)(2,1)}, bf16[2048,1408]{1,0:T(8,128)(2,1)}, /*index=5*/bf16[2048,1408]{1,0:T(8,128)(2,1)}) custom-call(bf16[4,256,2048]{2,1,0:T(8,128)(2,1)} %bitcast.140, bf16[256,2048]{1,0:T(8,128)(2,1)} %refs_1_.3, ...), custom_call_target="tpu_custom_call" | custom-call | tf_op jit(solution)/shard_map/pallas_call | solution.py:1019
  614.0 2.8 fusion.11
  617.6 244.9 %shard_map.375 = (f32[2,1408,256]{2,1,0:T(8,128)}, f32[256,1408]{1,0:T(8,128)}, f32[256,1408]{1,0:T(8,128)}, f32[1408,256]{1,0:T(8,128)}, f32[4,512,256]{2,1,0:T...) custom-call(bf16[4,2,256,1408]{3,2,1,0:T(8,128)(2,1)} %bitcast.134, ...), custom_call_target="tpu_custom_call" | custom-call | tf_op jit(solution)/shard_map/pallas_call | solution.py:750
  862.5 1.4 dynamic-slice_bitcast_fusion.5
  864.0 1.4 dynamic-slice_bitcast_fusion.4
  865.3 2.9 slice_bitcast_fusion
  868.2 3.2 maximum_convert_fusion
  871.4 3.2 maximum_convert_fusion.1
  874.6 1.0 copy.96
  875.6 1.3 copy.97
  876.9 1.1 copy.98
  878.0 1.1 copy.99
  879.1 1.1 copy.100
  881.0 1.6 copy.101
  (108 shorter events, 17.5 us)
Async XLA Ops:
  7.2 513.1 %reduce-scatter.5.cloned.1.call-start = ((), (), s32[]{:S(2)}) async-start(), calls=%async_computation.4 | async-start | bytes 6488064 | tf_op jit(solution)/shard_map/reduce_scatter | solution.py:1415
  10.8 1.2 copy-start.1
  12.0 1.6 copy-start.3
  13.6 1.6 copy-start.4
  15.2 1.6 copy-start.5
  16.8 79.1 %copy-start.7 = (bf16[256,2048]{1,0:T(8,128)(2,1)S(1)}, bf16[256,2048]{1,0:T(8,128)(2,1)}, u32[]{:S(2)}) copy-start(bf16[256,2048]{1,0:T(8,128)(2,1)} %refs_3_) | copy-start | bytes 3145732
  16.8 83.4 %copy-start.18 = (bf16[512]{0:T(512)(128)(2,1)S(1)}, bf16[512]{0:T(512)(128)(2,1)}, u32[]{:S(2)}) copy-start(bf16[512]{0:T(512)(128)(2,1)} %param.33) | copy-start | bytes 3076
  16.8 83.4 %copy-start.19 = (bf16[512]{0:T(512)(128)(2,1)S(1)}, bf16[512]{0:T(512)(128)(2,1)}, u32[]{:S(2)}) copy-start(bf16[512]{0:T(512)(128)(2,1)} %param.34) | copy-start | bytes 3076
  16.8 83.4 %copy-start.20 = (bf16[512]{0:T(512)(128)(2,1)S(1)}, bf16[512]{0:T(512)(128)(2,1)}, u32[]{:S(2)}) copy-start(bf16[512]{0:T(512)(128)(2,1)} %param.35) | copy-start | bytes 3076
  91.2 2.7 copy-start
  93.9 2.0 copy-start.2
  95.9 37.7 %collective-permute-start.2 = (bf16[256,2048]{1,0:T(8,128)(2,1)S(1)}, bf16[256,2048]{1,0:T(8,128)(2,1)S(1)}, u32[]{:S(2)}, u32[]{:S(2)}) collective-permute-start(bf16[256,2048]{1,0:T(8,128)(2,1)S(1)} %copy-done.7), channel_id=1, source_target_pairs={{0,3},{1,2},{2,1},{3,0},{4,7},{5,6},{6,5},{7,4},{8,11},{9,10},{10,... | collective-permute-start | bytes 3145736 | tf_op jit(solution)/shard_map/ppermute | solution.py:1393
  97.4 46.2 %collective-permute-start.1 = (bf16[256,2048]{1,0:T(8,128)(2,1)S(1)}, bf16[256,2048]{1,0:T(8,128)(2,1)S(1)}, u32[]{:S(2)}, u32[]{:S(2)}) collective-permute-start(bf16[256,2048]{1,0:T(8,128)(2,1)S(1)} %copy-done.7), channel_id=1, source_target_pairs={{0,2},{1,3},{2,0},{3,1},{4,6},{5,7},{6,4},{7,5},{8,10},{9,11},{10,... | collective-permute-start | bytes 3145736 | tf_op jit(solution)/shard_map/ppermute | solution.py:1393
  98.8 45.0 %collective-permute-start = (bf16[256,2048]{1,0:T(8,128)(2,1)S(1)}, bf16[256,2048]{1,0:T(8,128)(2,1)}, u32[]{:S(2)}, u32[]{:S(2)}) collective-permute-start(bf16[256,2048]{1,0:T(8,128)(2,1)S(1)} %copy-done.7), channel_id=1, source_target_pairs={{0,1},{1,0},{2,3},{3,2},{4,5},{5,4},{6,7},{7,6},{8,9},{9,8},{10,11... | collective-permute-start | bytes 3145736 | tf_op jit(solution)/shard_map/ppermute | solution.py:1393
  147.1 107.4 %collective-permute-start.3 = (bf16[1024,2048]{1,0:T(8,128)(2,1)}, bf16[1024,2048]{1,0:T(8,128)(2,1)}, u32[]{:S(2)}, u32[]{:S(2)}) collective-permute-start(bf16[1024,2048]{1,0:T(8,128)(2,1)} %pad_maximum_fusion.g_ref), channel_id=1, source_target_pairs={{0,8},{4,12},{24,16},{28,20},{1,9},{5,13},{25,17},{29,21},{2,10},{... | collective-permute-start | bytes 12582920 | tf_op jit(solution)/shard_map/ppermute | solution.py:1398
  231.4 108.7 %collective-permute-start.4 = (bf16[1024,2048]{1,0:T(8,128)(2,1)}, bf16[1024,2048]{1,0:T(8,128)(2,1)}, u32[]{:S(2)}, u32[]{:S(2)}) collective-permute-start(bf16[1024,2048]{1,0:T(8,128)(2,1)} %bitcast.119), channel_id=1, source_target_pairs={{0,8},{4,12},{24,16},{28,20},{1,9},{5,13},{25,17},{29,21},{2,10},{... | collective-permute-start | bytes 12582920 | tf_op jit(solution)/shard_map/ppermute | solution.py:1398
  243.5 8.0 copy-start.6
  314.4 9.1 %copy-start.9 = (bf16[4,1,160,2048]{3,2,1,0:T(8,128)(2,1)S(1)}, bf16[4,1,160,2048]{3,2,1,0:T(8,128)(2,1)}, u32[]{:S(2)}) copy-start(bf16[4,1,160,2048]{3,2,1,0:T(8,128)(2,1)} %get-tuple-element.162) | copy-start | bytes 7864324
  340.1 528.1 %reduce-scatter.7.cloned.1.call-start = ((), (), s32[]{:S(2)}) async-start(), calls=%async_computation.5 | async-start | bytes 6488064 | tf_op jit(solution)/shard_map/reduce_scatter | solution.py:1415
  340.8 3.3 copy-start.15
  340.8 527.4 %reduce-scatter.9.cloned.1.call-start = ((), (), s32[]{:S(2)}) async-start(), calls=%async_computation.6 | async-start | bytes 6488064 | tf_op jit(solution)/shard_map/reduce_scatter | solution.py:1415
  341.6 529.8 %reduce-scatter.11.cloned.1.call-start = ((), (), s32[]{:S(2)}) async-start(), calls=%async_computation.7 | async-start | bytes 6488064 | tf_op jit(solution)/shard_map/reduce_scatter | solution.py:1415
  520.3 1.0 copy-start.16
  561.0 52.3 %copy-start.17 = (f32[4,2048]{1,0:T(4,128)S(1)}, f32[4,2048]{1,0:T(4,128)}, u32[]{:S(2)}) copy-start(f32[4,2048]{1,0:T(4,128)} %get-tuple-element.142) | copy-start | bytes 98308
  868.2 6.4 copy-start.14
  871.4 4.2 copy-start.10
  874.6 2.3 copy-start.13
  875.6 2.4 copy-start.12
  876.9 2.2 copy-start.11
  878.0 3.0 copy-start.8
Sparse Core Ops, SparseCore 0:
  340.2 63.9 reduce-scatter.4
  406.5 63.2 reduce-scatter.6
  472.1 63.2 reduce-scatter.8
  537.5 63.2 reduce-scatter.10

commit v3 on v2

--- a/solution.py
+++ b/solution.py
@@ -220,12 +220,81 @@
     )(x, g, heads, w_gate, w_up, w_down)
 
 
+def dispatch_kernel(x_ref, g_ref, slot_ref, heads, rows_in, rows_cot, gate_ref, pick_ref, probs_ref, opener_ref):
+    x, g = x_ref[...], g_ref[...]
+    local, slots = rows_in.shape[1], rows_in.shape[2]
+    count = heads.shape[0] - 1
+    pre = trans_dot(x, heads[...])
+    opener_ref[...] = 1.0 / (1.0 + jnp.exp(-pre[:, count:]))
+    pre = pre[:, :count]
+    expo = jnp.exp(pre - jnp.max(pre, axis=-1, keepdims=True))
+    probs = expo / jnp.sum(expo, axis=-1, keepdims=True)
+    probs_ref[...] = probs
+    parts, rest = [], probs
+    for _ in range(3):
+        parts.append(rest.astype(BF16))
+        rest = rest - parts[-1].astype(F32)
+    numbers = lax.broadcasted_iota(jnp.int32, (slots, count), 1)
+    places = lax.broadcasted_iota(jnp.int32, (slots, x.shape[0]), 0)
+    for i in range(local):
+        pick = jnp.where(places == slot_ref[0, i : i + 1, :], 1.0, 0.0).astype(BF16)
+        pick_ref[0, i * slots : (i + 1) * slots, :] = pick
+        rows_in[0, i] = plain_dot(pick, x).astype(BF16)
+        rows_cot[0, i] = plain_dot(pick, g).astype(BF16)
+        found = plain_dot(pick, parts[0]) + (plain_dot(pick, parts[1]) + plain_dot(pick, parts[2]))
+        number = lax.axis_index("fsdp") * local + i
+        gate_ref[0, i] = jnp.sum(jnp.where(numbers == number, found, 0.0), axis=-1, keepdims=True)
+
+
+def dispatch_call(x, g, slot, heads, slots):
+    count, features = x.shape
+    blocks, local, rows = slot.shape
+    experts = heads.shape[0] - 1
+
+    def rows_spec(cols):
+        return pl.BlockSpec((rows, cols), lambda b: (b, 0))
+
+    def slots_spec(cols):
+        return pl.BlockSpec((1, local, slots, cols), lambda b: (b, 0, 0, 0))
+
+    def slots_shape(cols, dtype=BF16):
+        return jax.ShapeDtypeStruct((blocks, local, slots, cols), dtype)
+
+    return pl.pallas_call(
+        dispatch_kernel,
+        grid=(blocks,),
+        in_specs=[
+            rows_spec(features),
+            rows_spec(features),
+            pl.BlockSpec((1, local, rows), lambda b: (b, 0, 0)),
+            pl.BlockSpec(heads.shape, lambda b: (0, 0)),
+        ],
+        out_specs=[
+            slots_spec(features),
+            slots_spec(features),
+            slots_spec(1),
+            pl.BlockSpec((1, local * slots, rows), lambda b: (b, 0, 0)),
+            rows_spec(experts),
+            rows_spec(1),
+        ],
+        out_shape=[
+            slots_shape(features),
+            slots_shape(features),
+            slots_shape(1, F32),
+            jax.ShapeDtypeStruct((blocks, local * slots, rows), BF16),
+            jax.ShapeDtypeStruct((count, experts), F32),
+            jax.ShapeDtypeStruct((count, 1), F32),
+        ],
+        compiler_params=pltpu.CompilerParams(vmem_limit_bytes=60 * MIB),
+    )(x, g, slot, heads)
+
+
 class Line:
     def __init__(self, parts, inner, sources, outs, sib, recv, bufs, sems):
         self.parts, self.inner, self.sources, self.outs = parts, inner, sources, outs
         self.sib, self.recv = sib, recv
-        self.own_v, self.sib_v, self.in_v, self.more_v, self.send_v, self.out_v, self.turned_v = bufs
-        self.own_sem, self.sib_sem, self.in_sem, self.out_sem, self.sib_send, self.sib_recv, self.sent, self.got = sems
+        self.own_v, self.sib_v, self.send_v, self.out_v, self.turned_v = bufs
+        self.own_sem, self.sib_sem, self.out_sem, self.sib_send, self.sib_recv, self.sent, self.got = sems
         self.chunks = len(sources) * parts
         self.slots = self.send_v.shape[0]
         self.rows = sources[0].shape[2] // parts
@@ -318,13 +387,10 @@
         self.sib_load(0, 0, r, k).wait()
         return self.own_v[k].astype(F32) + self.sib_v[k].astype(F32)
 
-    def fetch(self, q, place, buf, k):
+    def fetch(self, q, place):
         self.arrived(q, place)
         m, r = self.span(q)
-        c = pltpu.make_async_copy(self.recv.at[m, place, r], buf, self.in_sem.at[k])
-        c.start()
-        c.wait()
-        return buf[...].astype(F32)
+        return self.recv[m, place, r].astype(F32)
 
     def send(self, t, k, q, p, target, place, more, first):
         depth = self.slots // 3
@@ -335,7 +401,7 @@
             self.hop(q, slot, target, place).wait_send()
 
         if more:
-            extra = self.fetch(q, p, self.in_v, 0)
+            extra = self.fetch(q, p)
             total = self.base(k) + extra
         else:
             total = self.base(k)
@@ -415,20 +481,20 @@
 
                 @pl.when(z == 0)
                 def _():
-                    self.out_v[...] = self.fetch(q, 4, self.more_v, 1)
+                    self.out_v[...] = self.fetch(q, 4)
 
                 @pl.when(z == 3)
                 def _():
-                    self.out_v[...] = self.fetch(q, 3, self.more_v, 1)
+                    self.out_v[...] = self.fetch(q, 3)
 
                 @pl.when(z == 1)
                 def _():
-                    got = self.fetch(q, 4, self.more_v, 1)
+                    got = self.fetch(q, 4)
                     self.out_v[...] = self.base(3) + got
 
                 @pl.when(z == 2)
                 def _():
-                    got = self.fetch(q, 2, self.more_v, 1)
+                    got = self.fetch(q, 2)
                     self.out_v[...] = self.base(3) + got
 
             else:
@@ -436,11 +502,11 @@
 
                 @pl.when(z > 0)
                 def _():
-                    self.out_v[...] = self.out_v[...] + self.fetch(q, z, self.in_v, 0)
+                    self.out_v[...] = self.out_v[...] + self.fetch(q, z)
 
                 @pl.when(z < 3)
                 def _():
-                    self.out_v[...] = self.out_v[...] + self.fetch(q, 4, self.more_v, 1)
+                    self.out_v[...] = self.out_v[...] + self.fetch(q, 4)
 
             def put(j, r):
                 if self.outs[j][1]:
@@ -470,8 +536,6 @@
 
 def line_bufs(shape, slots, turned):
     return [pltpu.VMEM((4,) + shape, BF16)] * 2 + [
-        pltpu.VMEM(shape, BF16),
-        pltpu.VMEM(shape, BF16),
         pltpu.VMEM((slots,) + shape, BF16),
         pltpu.VMEM(shape, F32),
         pltpu.VMEM(shape[::-1] if turned else (8, 128), F32),
@@ -482,7 +546,6 @@
     return [
         pltpu.SemaphoreType.DMA((4,)),
         pltpu.SemaphoreType.DMA((4,)),
-        pltpu.SemaphoreType.DMA((2,)),
         pltpu.SemaphoreType.DMA,
         pltpu.SemaphoreType.DMA((q,)),
         pltpu.SemaphoreType.DMA((q,)),
@@ -499,15 +562,18 @@
 
     downs, shared = take(n_down), take(n_shared)
     three, part_out, out_part, mixed, vec, bias_add = take(6)
-    out_down, out_gate, out_up, out_sdown, out_four, output, vec_out = take(7)
-    sib_a, recv_a, att, sib_b, recv_b, sib_c, recv_c, out_in = take(8)
-    bufs_a, bufs_b, bufs_c = take(7), take(7), take(7)
+    out_down, out_gate, out_up, out_sdown = take(4)
+    out_four = take(4)
+    output, vec_out = take(2)
+    sib_a, att, sib_b, sib_c, out_in = take(5)
+    bufs_a, bufs_b, bufs_c = take(5), take(5), take(5)
+    recv_a, recv_b, recv_c = take(3)
     vec_in, vec_own, vec_sib, vec_line, vec_send, parts_v, mixed_v, sum_v = take(8)
-    sems_a, sems_b, sems_c = take(8), take(8), take(8)
+    sems_a, sems_b, sems_c = take(7), take(7), take(7)
     plane_send, plane_recv, local_sems, vec_send_sems, vec_recv_sems, out_send, out_recv = take(7)
 
     a = Line(parts, False, downs, [(out_down.at[j], True) for j in range(n_down)], sib_a, recv_a, bufs_a, sems_a)
-    b = Line(1, False, [att.at[j] for j in range(4)], [(out_four.at[j], True) for j in range(4)], sib_b, recv_b, bufs_b, sems_b)
+    b = Line(1, False, [att.at[j] for j in range(4)], [(v, True) for v in out_four], sib_b, recv_b, bufs_b, sems_b)
     c = Line(parts, shift, shared, [(out_gate, False), (out_up, False), (out_sdown, True)], sib_c, recv_c, bufs_c, sems_c)
     z, core = a.z, a.core
     f = lax.axis_index("fsdp")
@@ -691,28 +757,19 @@
         def _():
             finish_output()
 
-    def slower(t):
-        if a.chunks + b.chunks < c.chunks + 2:
-            c.turn(t)
-            return
-
-        @pl.when((t != 2) & (t != 5))
-        def _():
-            c.turn(t - jnp.where(t > 2, 1, 0) - jnp.where(t > 5, 1, 0))
-
     def first_loop(t, carry):
         a.turn(t)
         b.turn(t - a.chunks)
-        slower(t)
+        c.turn(t)
         side_work(t)
         return carry
 
     def last_loop(t, carry):
         b.turn(t - a.chunks)
-        slower(t)
+        c.turn(t)
         return carry
 
-    turns = max(a.chunks + b.chunks, c.chunks + 2) + 3
+    turns = max(a.chunks + b.chunks, c.chunks) + 3
     lax.fori_loop(0, max(7, a.chunks + 3), first_loop, 0)
     lax.fori_loop(max(7, a.chunks + 3), turns, last_loop, 0)
     a.finish()
@@ -754,24 +811,27 @@
             shape(rows, cols, dtype=F32),
             shape(rows, cols, dtype=F32),
             shape(cols, rows, dtype=F32),
-            shape(4, width, share, dtype=F32),
+            shape(width, share, dtype=F32),
+            shape(width, share, dtype=F32),
+            shape(width, share, dtype=F32),
+            shape(width, share, dtype=F32),
             shape(own_rows, features),
             shape(*small, dtype=F32),
             shape(m, 4, rows, cols),
-            shape(m, 5, rows, cols),
             shape(4, 4, 2, share, width),
             shape(4, 4, share, width),
-            shape(4, 5, share, width),
             shape(s, 4, rows, cols),
-            shape(s, 5, rows, cols),
             shape(3, own_rows, features),
         ),
         in_specs=[ANY] * (m + s + 5) + [VMEM],
-        out_specs=(ANY,) * 6 + (VMEM,) + (ANY,) * 8,
+        out_specs=(ANY,) * 9 + (VMEM,) + (ANY,) * 5,
         scratch_shapes=line_bufs((r, cols), slots, True)
         + line_bufs((share, width), slots, True)
         + line_bufs((r, cols), slots, True)
         + [
+            pltpu.VMEM((m, 5, rows, cols), BF16),
+            pltpu.VMEM((4, 5, share, width), BF16),
+            pltpu.VMEM((s, 5, rows, cols), BF16),
             pltpu.VMEM((3,) + small, F32),
             pltpu.VMEM(small, F32),
             pltpu.VMEM(small, F32),
@@ -797,7 +857,7 @@
             collective_id=collective_id, has_side_effects=True, vmem_limit_bytes=60 * MIB
         ),
     )(*downs, *shared, three, part_out, out_part, mixed, vec, bias_add)
-    return outs[:7]
+    return outs[0], outs[1:4], outs[4:8], outs[8], outs[9]
 
 
 def plane_neighbours():
@@ -996,13 +1056,16 @@
     turns = chunks + 4
     if n_jobs:
         side.begin()
-        each = -(-len(side.units) // turns)
+        each = len(side.units) / (5 * chunks)
+    steps = done = 0
     for t in range(turns):
         for n in range(5):
             if 0 <= t - n < chunks:
                 stage(n, t - n)
-        if n_jobs:
-            side.step(each)
+                steps += 1
+                if n_jobs and int(steps * each) > done:
+                    side.step(int(steps * each) - done)
+                    done = int(steps * each)
     if n_jobs:
         side.end()
 
@@ -1054,11 +1117,14 @@
     by_x, by_y = plane_neighbours()
     fx, fy = by_x["fsdp"], by_y["fsdp"]
     fd = fx + 2 - 4 * (fx // 2)
+    z = g // 2
+    odd = lax.rem(z, 2)
     by_d, sibling = {"fsdp": fd}, {"grp": g + 1 - 2 * core}
+    by_z = {"grp": g + 2 - 4 * odd}
     barrier = pltpu.get_barrier_semaphore()
-    for other in (by_x, by_y, by_d, sibling):
+    for other in (by_x, by_y, by_d, sibling, by_z):
         pl.semaphore_signal(barrier, inc=1, device_id=other, device_id_type=MESH)
-    pl.semaphore_wait(barrier, 4)
+    pl.semaphore_wait(barrier, 5)
 
     def copy(n, src, dst, target):
         return pltpu.make_async_remote_copy(
@@ -1069,11 +1135,14 @@
     def columns(j):
         return pl.ds(pl.multiple_of(j * width, width), width)
 
-    def block_rows(owner, c):
-        return pl.ds(pl.multiple_of(owner * depth + c * (depth // 2), depth // 2), depth // 2)
-
-    half = depth // 2
-    mine = pl.ds(pl.multiple_of(core * half, half), half)
+    quarter = depth // 4
+    eighth = quarter // 2
+    here, there = 2 * odd + core, 2 * (1 - odd) + core
+
+    def block_rows(owner, q):
+        return pl.ds(pl.multiple_of(owner * depth + q * quarter, quarter), quarter)
+
+    mine = pl.ds(pl.multiple_of(here * quarter, quarter), quarter)
     all_sends = []
 
     def go(c):
@@ -1103,16 +1172,15 @@
     for c in locals_:
         c.start()
 
-    quarter = half // 2
-    first = pl.ds(pl.multiple_of(core * half, quarter), quarter)
-    second = pl.ds(pl.multiple_of(core * half + quarter, quarter), quarter)
+    first = pl.ds(pl.multiple_of(here * quarter, eighth), eighth)
+    second = pl.ds(pl.multiple_of(here * quarter + eighth, eighth), eighth)
     relays_x, relays_y, direct_x, direct_y = [], [], [], []
     for j, w in enumerate((w_q, w_k, w_v)):
         relays_x.append(go(copy(n, w.at[first, columns(fd)], relay.at[0, j], by_x)))
         relays_y.append(go(copy(n + 1, w.at[second, columns(fd)], relay.at[1, j], by_y)))
         n += 2
     for j, w in enumerate((w_q, w_k, w_v)):
-        place = w_cols.at[block_rows(f, core), pl.ds(j * width, width)]
+        place = w_cols.at[block_rows(f, here), pl.ds(j * width, width)]
         direct_x.append(go(copy(n, w.at[mine, columns(fx)], place, by_x)))
         direct_y.append(go(copy(n + 1, w.at[mine, columns(fy)], place, by_y)))
         n += 2
@@ -1128,7 +1196,7 @@
         forwarded.append(
             go(copy(
                 n, relay.at[0, j],
-                w_cols.at[pl.ds(pl.multiple_of(fx * depth + core * half, quarter), quarter), pl.ds(j * width, width)],
+                w_cols.at[pl.ds(pl.multiple_of(fx * depth + here * quarter, eighth), eighth), pl.ds(j * width, width)],
                 by_y,
             ))
         )
@@ -1136,25 +1204,32 @@
         forwarded.append(
             go(copy(
                 n + 1, relay.at[1, j],
-                w_cols.at[pl.ds(pl.multiple_of(fy * depth + core * half + quarter, quarter), quarter), pl.ds(j * width, width)],
+                w_cols.at[
+                    pl.ds(pl.multiple_of(fy * depth + here * quarter + eighth, eighth), eighth), pl.ds(j * width, width)
+                ],
                 by_x,
             ))
         )
         n += 2
-    shares = []
-
-    def share(owner):
+    shares, lent = [], []
+
+    def share(owner, q, target):
         nonlocal n
-        place = w_cols.at[block_rows(owner, core)]
-        shares.append(go(copy(n, place, place, sibling)))
+        place = w_cols.at[block_rows(owner, q)]
+        c = go(copy(n, place, place, target))
         n += 1
+        return c
+
+    def fetched(owner):
+        lent.append(share(owner, here, by_z))
+        shares.append(share(owner, here, sibling))
 
     for c in direct_x:
         c.wait_recv()
-    share(fx)
+    fetched(fx)
     for c in direct_y:
         c.wait_recv()
-    share(fy)
+    fetched(fy)
     t_x0.wait_recv()
     t_d0 = go(copy(n, tokens_all.at[1, low], tokens_all.at[3, low], by_y))
     t_y1.wait_recv()
@@ -1162,7 +1237,10 @@
     n += 2
     for c in forwarded:
         c.wait_recv()
-    share(fd)
+    fetched(fd)
+    for owner, c in zip((fx, fy, fd), lent):
+        c.wait_recv()
+        shares.append(share(owner, there, sibling))
     for c in waits + shares + [t_x1, t_y0, t_d0, t_d1]:
         c.wait_recv()
     for c in locals_:
@@ -1174,7 +1252,7 @@
 def start_call(tokens, small, marks, w_q, w_k, w_v, collective_id):
     depth, features = w_q.shape
     width = features // 4
-    n = 6 + 6 + 6 + 4 + 6 + 2 + 3
+    n = 6 + 6 + 6 + 4 + 6 + 2 + 9
     return pl.pallas_call(
         start_kernel,
         out_shape=(
@@ -1182,7 +1260,7 @@
             jax.ShapeDtypeStruct((4,) + small.shape, small.dtype),
             jax.ShapeDtypeStruct((4,) + marks.shape, marks.dtype),
             jax.ShapeDtypeStruct((4 * depth, 3 * width), BF16),
-            jax.ShapeDtypeStruct((2, 3, depth // 4, width), BF16),
+            jax.ShapeDtypeStruct((2, 3, depth // 8, width), BF16),
         ),
         in_specs=[ANY] * 6,
         out_specs=(ANY,) * 5,
@@ -1209,10 +1287,60 @@
     return jnp.where(seen, 0.0, MASK_FILL)
 
 
+class Spread:
+    def __init__(self, own, everyone, send_sems, recv_sems, local_sem):
+        self.everyone, self.send_sems, self.recv_sems = everyone, send_sems, recv_sems
+        self.by_x, self.by_y = plane_neighbours()
+        rows = own.shape[0]
+        low, high = pl.ds(0, rows // 2), pl.ds(rows // 2, rows // 2)
+        self.kept = pltpu.make_async_copy(own, everyone.at[0], local_sem)
+        self.first = [
+            self.copy(0, own.at[low], (1, low), self.by_x),
+            self.copy(1, own.at[high], (2, high), self.by_y),
+            self.copy(2, own.at[high], (1, high), self.by_x),
+            self.copy(3, own.at[low], (2, low), self.by_y),
+        ]
+        self.second = [
+            self.copy(4, everyone.at[1, low], (3, low), self.by_y),
+            self.copy(5, everyone.at[2, high], (3, high), self.by_x),
+        ]
+
+    def copy(self, n, src, place, target):
+        return pltpu.make_async_remote_copy(
+            src_ref=src, dst_ref=self.everyone.at[place], send_sem=self.send_sems.at[n],
+            recv_sem=self.recv_sems.at[n], device_id=target, device_id_type=MESH,
+        )
+
+    def begin(self):
+        plane_barrier(self.by_x, self.by_y)
+        for c in self.first:
+            c.start()
+        self.kept.start()
+
+    def middle(self):
+        for got, onward in zip(self.first[:2], self.second):
+            got.wait_recv()
+            onward.start()
+
+    def end(self):
+        for c in self.first[2:] + self.second:
+            c.wait_recv()
+        for c in self.first + self.second:
+            c.wait_send()
+        self.kept.wait()
+
+
 def attend_kernel(
-    tokens, gain, w_cols, bias, w_out, cosine, sine, mark_cols, mark_rows,
-    normed, three, attended, branch, mask,
+    tokens, gain, w_cols, bias, w_out, cosine, sine, mark_cols, mark_rows, *refs
 ):
+    spread = None
+    if len(refs) > 5:
+        own, refs = refs[0], refs[1:]
+        normed, three, attended, branch, everyone, mask = refs[:6]
+        spread = Spread(own, everyone, *refs[6:])
+        spread.begin()
+    else:
+        normed, three, attended, branch, mask = refs
     count = tokens.shape[0]
     width = w_out.shape[0]
     scale = HEAD_DIM**-0.5
@@ -1236,6 +1364,8 @@
                 ).astype(BF16)
         else:
             three[:, c] = pre.astype(BF16)
+    if spread:
+        spread.middle()
     for h in range(width // HEAD_DIM):
         q_cols = pl.ds(h * HEAD_DIM, HEAD_DIM)
         k_cols = pl.ds(width + h * HEAD_DIM, HEAD_DIM)
@@ -1251,23 +1381,37 @@
     for b, m in pieces(w_out.shape[1], 512):
         c = pl.ds(b, m)
         branch[:, c] = plain_dot(attended[...], w_out[:, c]).astype(BF16)
-
-
-def attend_call(tokens, gain, w_cols, bias, w_out, cosine, sine, mark_cols, mark_rows):
+    if spread:
+        spread.end()
+
+
+def attend_call(tokens, gain, w_cols, bias, w_out, cosine, sine, mark_cols, mark_rows, own=None, collective_id=None):
     count, features = tokens.shape
     width = w_out.shape[0]
 
     def shape(cols):
         return jax.ShapeDtypeStruct((count, cols), BF16)
 
+    ins = [tokens, gain, w_cols, bias, w_out, cosine, sine, mark_cols, mark_rows]
+    in_specs, out_specs = [VMEM] * 9, (VMEM,) * 4
+    out_shape = (shape(features), shape(3 * width), shape(width), shape(features))
+    scratch = [pltpu.VMEM((count, count), F32)]
+    params = {}
+    if own is not None:
+        ins.append(own)
+        in_specs.append(ANY)
+        out_specs += (ANY,)
+        out_shape += (jax.ShapeDtypeStruct((4,) + own.shape, own.dtype),)
+        scratch += [pltpu.SemaphoreType.DMA((6,)), pltpu.SemaphoreType.DMA((6,)), pltpu.SemaphoreType.DMA]
+        params = {"collective_id": collective_id, "has_side_effects": True}
     return pl.pallas_call(
         attend_kernel,
-        in_specs=[VMEM] * 9,
-        out_specs=(VMEM,) * 4,
-        out_shape=(shape(features), shape(3 * width), shape(width), shape(features)),
-        scratch_shapes=[pltpu.VMEM((count, count), F32)],
-        compiler_params=pltpu.CompilerParams(vmem_limit_bytes=60 * MIB),
-    )(tokens, gain, w_cols, bias, w_out, cosine, sine, mark_cols, mark_rows)
+        in_specs=in_specs,
+        out_specs=out_specs,
+        out_shape=out_shape,
+        scratch_shapes=scratch,
+        compiler_params=pltpu.CompilerParams(vmem_limit_bytes=60 * MIB, **params),
+    )(*ins)
 
 
 def attend_back_kernel(
@@ -1463,7 +1607,7 @@
                 True,
                 number,
             )
-            return outs[0], outs[1:4], outs[4], outs[5], outs[6]
+            return outs
         down = jnp.stack([self.reduce_background(v).astype(F32).T for v in downs], axis=0)
         sums = [self.reduce_background(v).astype(F32) for v in shared]
         three = lax.all_to_all(
@@ -1530,8 +1674,6 @@
     mark_cols = mark_rows.T
     routes_rows = mark_rows[5 : 5 + choose]
 
-    tokens_all, cotangent = lax.optimization_barrier((tokens_all, cotangent))
-    cot_all = wires.gather(cotangent)
 
     halfway = HEAD_DIM // 2
     freqs = ROPE_BASE ** (-(jnp.arange(halfway, dtype=F32) * 2.0 / HEAD_DIM))
@@ -1539,9 +1681,13 @@
     cosine = jnp.cos(turns)
     sine = jnp.sin(turns) * jnp.where(jnp.arange(HEAD_DIM) < halfway, -1.0, 1.0)[None, :]
     bias = jnp.concatenate([b_query, b_key, b_value]).astype(F32)[None]
-    normed, three, attended, branch = attend_call(
-        tokens_all, gain_one, w_cols, bias, w_output, cosine, sine, mark_cols, mark_rows
-    )
+    operands = (tokens_all, gain_one, w_cols, bias, w_output, cosine, sine, mark_cols, mark_rows)
+    if wires.fast:
+        normed, three, attended, branch, cot_all = attend_call(*operands, cotangent, 6)
+        cot_all = cot_all.reshape(count, features)
+    else:
+        normed, three, attended, branch = attend_call(*operands)
+        cot_all = wires.gather(cotangent)
 
     numbers = me * local_experts + jnp.arange(local_experts, dtype=jnp.int32)
     named = jnp.any(routes_rows[None] == numbers[:, None, None], axis=1)
@@ -1550,9 +1696,7 @@
     slot = jnp.einsum("ts,ebs->bet", earlier, named.astype(BF16), preferred_element_type=F32)
     slot = jnp.where(named.transpose(1, 0, 2), slot.astype(jnp.int32), -1)
     pick = jnp.arange(capacity, dtype=jnp.int32)[None, None, :, None] == slot[:, :, None, :]
-    pick_b = pick.astype(BF16).reshape(nf, local_experts * capacity, rows_dev)
-
-    branch, cot_all = lax.optimization_barrier((branch, cot_all))
+
     cot_other = wires.inwards(cot_all)
     mixed, moe_blocks = wires.middle(
         first_middle,
@@ -1565,27 +1709,9 @@
     moe_in = moe_blocks.reshape(count, features)
     moe_other = wires.inwards(moe_in)
 
-    head_pre = trans_dot(moe_in, heads_rows)
-    router_probs = jax.nn.softmax(head_pre[:, :experts], axis=-1)
-    opener = jax.nn.sigmoid(head_pre[:, experts:])
-    local = jnp.stack(
-        [
-            jnp.sum(jnp.where(jnp.arange(experts)[None] == numbers[i], router_probs, 0.0), axis=1)
-            for i in range(local_experts)
-        ],
-        axis=0,
+    rows_in, rows_cot, gate, pick_b, router_probs, opener = dispatch_call(
+        moe_in, cot_all, slot, heads_rows, capacity
     )
-    local = local.reshape(local_experts, nf, rows_dev).transpose(1, 0, 2)
-    gate = jnp.sum(jnp.where(pick, local[:, :, None, :], 0.0), axis=3, keepdims=True)
-
-    def dispatch(x):
-        return jnp.einsum(
-            "bst,btd->bsd", pick_b, x.reshape(nf, rows_dev, -1), preferred_element_type=F32
-        ).astype(BF16)
-
-    shape = (nf, local_experts, capacity, -1)
-    rows_in = dispatch(moe_in).reshape(shape)
-    rows_cot = dispatch(cot_all).reshape(shape)
     if wires.fast:
         rows_cot, cot_other = lax.optimization_barrier((rows_cot, cot_other))
     hidden, d_gate, d_up, d_out, y_rows, dx_rows, sens_rows = expert_call(

time: 902 us -> 855 us (0.948)
  matrix products: 43.7 us -> 29.6 us
  Pallas kernels: 746 us -> 734 us
  waiting for transfers between devices: 11.7 us -> 1.44 us
    pallas_call x1 -> x2, Pallas kernels: 28.1 us -> 58.4 us  [the longest x1 46.8 us: attend_call(): pl.pallas_call(attend_kernel, in_specs=in_specs, out_specs=out_specs, out...]
    pallas_call x1, Pallas kernels: 74.4 us -> 57.8 us  [start_call(): pl.pallas_call(start_kernel, out_shape=(jax.ShapeDtypeStruct((4,) + token...]
    pallas_call x1, Pallas kernels: 245 us -> 230 us  [line_call(): pl.pallas_call(functools.partial(line_kernel, m, s, parts, shift), out_sh...]
    dot_general x2 -> x0, matrix products: 11.7 us -> none  [dispatch(): jnp.einsum('bst,btd->bsd', pick_b, x.reshape(nf, rows_dev, -1), preferred...]
    pallas_call x3, Pallas kernels: 213 us -> 202 us  [mid_call(): pl.pallas_call(functools.partial(mid_kernel, middle, chunks, gathers, len...]
    ppermute x3 -> x0, waiting for transfers between devices: 10.2 us -> none  [xor(): return lax.ppermute(value, 'fsdp', [(i, i ^ k) for i in range(self.nf)])]
    dot_general x5 -> x4, matrix products: 31.9 us -> 28.8 us  [dot(): lax.dot_general(left, right, (dims, ((), ())), preferred_element_type=out)]
    unnamed x49 -> x62, local copies, waits for them, and re-layouts: 19.8 us -> 22.5 us
  transfers between devices with their start and end apart: 9 -> 6, of which waited for: 2 -> 0; matrix products, arithmetic and copies ran while one was open for 8% -> 6% of each run, Pallas kernels for 76% -> 75%
where the time goes in v3:
time: 855 us; the launch traced here: 844 us
  Pallas kernels  734 us (86%)
  local copies, waits for them, and re-layouts  38.4 us (4%)
  matrix products  29.6 us (3%)
  other arithmetic  18.2 us (2%)
  between operations  14.6 us (2%)
    pallas_call x1, Pallas kernels, line_call(): pl.pallas_call(functools.partial(line_kernel, m, s, parts, shift), out_sh...  230 us
    pallas_call x3, Pallas kernels, mid_call(): pl.pallas_call(functools.partial(mid_kernel, middle, chunks, gathers, len...  202 us
    pallas_call x1, Pallas kernels, expert_call(): pl.pallas_call(expert_kernel, grid=(experts, steps), in_specs=[slot_spec(...  59.5 us
    pallas_call x1, Pallas kernels, start_call(): pl.pallas_call(start_kernel, out_shape=(jax.ShapeDtypeStruct((4,) + token...  57.8 us
    pallas_call x1, Pallas kernels, shared_call(): pl.pallas_call(shared_kernel, grid=(blocks,), in_specs=[rows_spec(feature...  56.7 us
    pallas_call x1, Pallas kernels, attend_call(): pl.pallas_call(attend_kernel, in_specs=in_specs, out_specs=out_specs, out...  46.8 us
    pallas_call x1, Pallas kernels, attend_back_call(): pl.pallas_call(attend_back_kernel, in_specs=[VMEM] * 8, out_specs=(VMEM,)...  38.4 us
    pallas_call x1, Pallas kernels, other_call(): pl.pallas_call(other_kernel, grid=(count // tile,), in_specs=[rows_spec(f...  30.5 us
  transfers between devices with their start and end apart: 6, of which 0 were waited for; matrix products, arithmetic and copies ran while one was open for 6% of the time, Pallas kernels for 75%

profile of v3, /device:TPU:0, one launch (start us, length us, event | category | flops | bytes accessed | tf_op | source)
XLA Modules:
  0.0 843.5 jit_solution(5839308389190464046)
XLA Ops:
  9.3 0.7 pad_add_fusion.1
  10.1 0.7 fusion.25.small
  10.8 1.2 copy-done.1
  12.0 1.6 copy-done.3
  13.6 1.6 copy-done.4
  15.2 1.6 copy-done.5
  16.8 57.8 %shard_map.366 = (bf16[4,256,2048]{2,1,0:T(8,128)(2,1)S(1)}, bf16[4,16,512]{2,1,0:T(8,128)(2,1)S(1)}, s32[4,16,256]{2,1,0:T(8,128)S(1)}, bf16[2048,1536]{1,0:T(8,128)(2,1)S(1)}, bf16[2,3,64,512]{3,2,1,0:T(8,128)(2,1)}) custom-call(bf16[256,2048]{1,0:T(8,128)(2,1)S(1)} %copy-done.1, bf16[16,512]{1,0:T(8,128)(2,1)S(1)} %fusion.25.small, ...), custom_call_target="tpu_custom_call" | custom-call | tf_op jit(solution)/shard_map/pallas_call | solution.py:1256
  74.6 2.7 copy-done
  77.3 2.0 copy-done.2
  79.9 1.0 copy.72.mark_cols
  81.7 3.0 fusion.8
  85.3 46.8 %shard_map.367 = (bf16[1024,2048]{1,0:T(8,128)(2,1)}, bf16[1024,1536]{1,0:T(8,128)(2,1)}, bf16[1024,512]{1,0:T(8,128)(2,1)}, bf16[1024,2048]{1,0:T(8,128)(2,1)}, bf16[4,256,2048]{2,1,0:T(8,128)(2,1)}) custom-call(bf16[1024,2048]{1,0:T(8,128)(2,1)} %bitcast.95, f32[1,2048]{1,0:T(1,128)} %get-tuple-element.177.gain.refs_2_, bf16[2048,1536]{1,0:T(8,128)(2,1)} %copy-done, ...), custom_call_target="tpu_custom_call" | custom-call | tf_op jit(solution)/shard_map/pallas_call | solution.py:1407
  132.1 4.2 collective-permute-start
  136.4 73.6 %shard_map.368 = (f32[256,2048]{1,0:T(8,128)}, bf16[4,256,2048]{2,1,0:T(8,128)(2,1)}) custom-call(bf16[4,256,2048]{2,1,0:T(8,128)(2,1)} %bitcast.115, bf16[256,2048]{1,0:T(8,128)(2,1)} %refs_1_.3, f32[1,2048]{1,0:T(1,128)} %get-tuple-element.176.refs_2_), custom_call_target="tpu_custom_call" | custom-call | tf_op jit(solution)/shard_map/pallas_call | solution.py:1082
  209.9 3.3 collective-permute-start.1
  213.2 0.8 slice.130
  214.8 0.8 fusion.7.slot_ref
  215.6 11.6 %shard_map.369 = (bf16[4,2,160,2048]{3,2,1,0:T(8,128)(2,1)}, bf16[4,2,160,2048]{3,2,1,0:T(8,128)(2,1)}, f32[4,2,160,1]{3,2,1,0:T(8,128)}, bf16[4,320,256]{2,1,0:...) custom-call(bf16[1024,2048]{1,0:T(8,128)(2,1)} %bitcast.97, bf16[1024,2048]{1,0:T(8,128)(2,1)} %bitcast.102, ...), custom_call_target="tpu_custom_call" | custom-call | tf_op jit(solution)/shard_map/pallas_call | solution.py:263
  227.2 5.7 fusion.29
  232.9 59.5 %shard_map.370 = (bf16[2,640,1408]{2,1,0:T(8,128)(2,1)}, bf16[2,640,1408]{2,1,0:T(8,128)(2,1)}, bf16[2,640,1408]{2,1,0:T(8,128)(2,1)}, bf16[4,2,160,2048]{3,2,1,...) custom-call(bf16[4,2,160,2048]{3,2,1,0:T(8,128)(2,1)} %get-tuple-ele, ...), custom_call_target="tpu_custom_call" | custom-call | tf_op jit(solution)/shard_map/pallas_call | solution.py:101
  292.4 9.4 %convolution_convert_fusion.1 = bf16[2048,1408]{1,0:T(8,128)(2,1)} fusion(bf16[640,2048]{1,0:T(8,128)(2,1)} %bitcast.120, bf16[2,640,1408]{2,1,0:T(8,128)(2,1)} %get-tuple-element.107.refs_5_), kind=kOutput, calls=%fused_computation.1 | convolution fusion | flops 3693871104 | bytes 10190848 | tf_op jit(solution)/shard_map/dot_general | solution.py:25
  301.8 8.3 convolution_convert_fusion.2
  310.0 8.3 convolution_convert_fusion
  320.6 1.3 iota_compare_fusion.4
  323.9 30.5 %shard_map.372 = (bf16[1024,1408]{1,0:T(8,128)(2,1)}, bf16[1024,1408]{1,0:T(8,128)(2,1)}, bf16[1024,1408]{1,0:T(8,128)(2,1)}, bf16[1024,2048]{1,0:T(8,128)(2,1)}) custom-call(bf16[1024,2048]{1,0:T(8,128)(2,1)} %collective-permute-done.1.x_ref.refs_11_, bf16[1024,2048]{1,0:T(8,128)(2,1)} %collective-permute-done.g_ref, bf16[9,2048]{1,0:T(8,128)(2,1)} %slice.131.heads, ...), custom_call_target="tpu_custom_call" | custom-call | tf_op jit(solution)/shard_map/pallas_call | solution.py:206
  354.5 0.9 pad_maximum_fusion.lane_ref
  355.3 56.7 %shard_map.371 = (bf16[1024,1408]{1,0:T(8,128)(2,1)}, bf16[1024,1408]{1,0:T(8,128)(2,1)}, bf16[1024,1408]{1,0:T(8,128)(2,1)}, bf16[1024,2048]{1,0:T(8,128)(2,1)}...) custom-call(bf16[1024,2048]{1,0:T(8,128)(2,1)} %bitcast.98, ...), custom_call_target="tpu_custom_call" | custom-call | tf_op jit(solution)/shard_map/pallas_call | solution.py:162
  412.1 80.7 %shard_map.373 = (f32[256,2048]{1,0:T(8,128)}, f32[4,2048]{1,0:T(4,128)}, bf16[4,256,2048]{2,1,0:T(8,128)(2,1)}, bf16[2048,1408]{1,0:T(8,128)(2,1)}, bf16[2048,1...) custom-call(bf16[4,256,2048]{2,1,0:T(8,128)(2,1)} %bitcast.117, ...), custom_call_target="tpu_custom_call" | custom-call | tf_op jit(solution)/shard_map/pallas_call | solution.py:1082
  493.1 0.8 copy-done.16
  494.2 38.4 %shard_map.374 = (bf16[1024,1536]{1,0:T(8,128)(2,1)}, bf16[1024,2048]{1,0:T(8,128)(2,1)}, f32[1,1536]{1,0:T(1,128)}) custom-call(bf16[1024,2048]{1,0:T(8,128)(2,1)} %bitcast.104, bf16[512,2048]{1,0:T(8,128)(2,1)} %w_out.3, bf16[1024,1536]{1,0:T(8,128)(2,1)} %get-tuple-element.129.three, bf16[2048,1536]{1,0:T(8,128)(2,1)} %copy-done, ...), custom_call_target="tpu_custom_call" | custom-call | tf_op jit(solution)/shard_map/pallas_call | solution.py:1473
  533.4 47.7 %shard_map.375 = (f32[256,2048]{1,0:T(8,128)}, f32[4,2048]{1,0:T(4,128)}, bf16[2048,512]{1,0:T(8,128)(2,1)}, bf16[1536,2048]{1,0:T(8,128)(2,1)}, bf16[2048,1408]{1,0:T(8,128)(2,1)}, /*index=5*/bf16[2048,1408]{1,0:T(8,128)(2,1)}) custom-call(bf16[4,256,2048]{2,1,0:T(8,128)(2,1)} %bitcast.116, bf16[256,2048]{1,0:T(8,128)(2,1)} %refs_1_.3, ...), custom_call_target="tpu_custom_call" | custom-call | tf_op jit(solution)/shard_map/pallas_call | solution.py:1082
  581.1 0.8 reduce_sum.38
  582.5 2.8 fusion.11
  586.2 230.4 %shard_map.376 = (f32[2,1408,256]{2,1,0:T(8,128)}, f32[256,1408]{1,0:T(8,128)}, f32[256,1408]{1,0:T(8,128)}, f32[1408,256]{1,0:T(8,128)}, f32[512,256]{1,0:T(8,1...) custom-call(bf16[4,2,256,1408]{3,2,1,0:T(8,128)(2,1)} %bitcast.110, ...), custom_call_target="tpu_custom_call" | custom-call | tf_op jit(solution)/shard_map/pallas_call | solution.py:807
  816.6 1.4 dynamic-slice_bitcast_fusion.5
  818.0 1.4 dynamic-slice_bitcast_fusion.4
  819.4 3.1 maximum_convert_fusion
  822.5 3.0 maximum_convert_fusion.1
  825.5 1.0 copy.99
  826.5 1.3 copy.100
  827.8 0.8 copy.101
  828.6 0.8 copy.102
  829.4 0.8 copy.103
  830.2 0.8 copy.104
  831.0 1.1 copy.105
  832.1 1.1 copy.106
  833.2 1.1 copy.107
  835.0 1.6 copy.108
  (103 shorter events, 12.5 us)
Async XLA Ops:
  7.2 485.6 %reduce-scatter.5.cloned.1.call-start = ((), (), s32[]{:S(2)}) async-start(), calls=%async_computation.4 | async-start | bytes 6488064 | tf_op jit(solution)/shard_map/reduce_scatter | solution.py:1559
  10.8 1.2 copy-start.1
  12.0 1.6 copy-start.3
  13.6 1.6 copy-start.4
  15.2 1.6 copy-start.5
  16.8 64.2 %copy-start.23 = (bf16[512]{0:T(512)(128)(2,1)S(1)}, bf16[512]{0:T(512)(128)(2,1)}, u32[]{:S(2)}) copy-start(bf16[512]{0:T(512)(128)(2,1)} %param.33) | copy-start | bytes 3076
  16.8 64.2 %copy-start.24 = (bf16[512]{0:T(512)(128)(2,1)S(1)}, bf16[512]{0:T(512)(128)(2,1)}, u32[]{:S(2)}) copy-start(bf16[512]{0:T(512)(128)(2,1)} %param.34) | copy-start | bytes 3076
  16.8 64.2 %copy-start.25 = (bf16[512]{0:T(512)(128)(2,1)S(1)}, bf16[512]{0:T(512)(128)(2,1)}, u32[]{:S(2)}) copy-start(bf16[512]{0:T(512)(128)(2,1)} %param.35) | copy-start | bytes 3076
  74.6 2.7 copy-start
  77.3 2.0 copy-start.2
  132.1 100.8 %collective-permute-start = (bf16[1024,2048]{1,0:T(8,128)(2,1)}, bf16[1024,2048]{1,0:T(8,128)(2,1)}, u32[]{:S(2)}, u32[]{:S(2)}) collective-permute-start(bf16[1024,2048]{1,0:T(8,128)(2,1)} %bitcast.101), channel_id=1, source_target_pairs={{0,8},{4,12},{24,16},{28,20},{1,9},{5,13},{25,17},{29,21},{2,10},{... | collective-permute-start | bytes 12582920 | tf_op jit(solution)/shard_map/ppermute | solution.py:1542
  209.9 108.5 %collective-permute-start.1 = (bf16[1024,2048]{1,0:T(8,128)(2,1)}, bf16[1024,2048]{1,0:T(8,128)(2,1)}, u32[]{:S(2)}, u32[]{:S(2)}) collective-permute-start(bf16[1024,2048]{1,0:T(8,128)(2,1)} %bitcast.96), channel_id=1, source_target_pairs={{0,8},{4,12},{24,16},{28,20},{1,9},{5,13},{25,17},{29,21},{2,10},{... | collective-permute-start | bytes 12582920 | tf_op jit(solution)/shard_map/ppermute | solution.py:1542
  292.4 9.4 %copy-start.7 = (bf16[4,1,160,2048]{3,2,1,0:T(8,128)(2,1)S(1)}, bf16[4,1,160,2048]{3,2,1,0:T(8,128)(2,1)}, u32[]{:S(2)}) copy-start(bf16[4,1,160,2048]{3,2,1,0:T(8,128)(2,1)} %get-tuple-element.172) | copy-start | bytes 7864324
  318.4 501.0 %reduce-scatter.7.cloned.1.call-start = ((), (), s32[]{:S(2)}) async-start(), calls=%async_computation.5 | async-start | bytes 6488064 | tf_op jit(solution)/shard_map/reduce_scatter | solution.py:1559
  319.1 3.4 copy-start.15
  319.2 3.7 copy-start.21
  319.2 4.3 copy-start.8
  319.2 500.2 %reduce-scatter.9.cloned.1.call-start = ((), (), s32[]{:S(2)}) async-start(), calls=%async_computation.6 | async-start | bytes 6488064 | tf_op jit(solution)/shard_map/reduce_scatter | solution.py:1559
  319.9 502.6 %reduce-scatter.11.cloned.1.call-start = ((), (), s32[]{:S(2)}) async-start(), calls=%async_computation.7 | async-start | bytes 6488064 | tf_op jit(solution)/shard_map/reduce_scatter | solution.py:1559
  492.8 1.0 copy-start.16
  533.4 48.5 %copy-start.22 = (f32[4,2048]{1,0:T(4,128)S(1)}, f32[4,2048]{1,0:T(4,128)}, u32[]{:S(2)}) copy-start(f32[4,2048]{1,0:T(4,128)} %get-tuple-element.151) | copy-start | bytes 98308
  816.6 5.9 copy-start.14
  822.5 3.0 copy-start.13
  822.5 4.0 copy-start.9
  825.5 2.3 copy-start.20
  826.5 2.1 copy-start.19
  826.5 2.9 copy-start.18
  826.5 3.7 copy-start.17
  827.8 3.2 copy-start.12
  828.6 3.5 copy-start.11
  830.2 3.0 copy-start.10
  832.1 2.9 copy-start.6
Sparse Core Ops, SparseCore 0:
  318.5 65.9 reduce-scatter.4
  386.8 63.2 reduce-scatter.6
  452.4 63.2 reduce-scatter.8
  517.8 63.2 reduce-scatter.10

commit v4 on v3

--- a/solution.py
+++ b/solution.py
@@ -289,6 +289,27 @@
     )(x, g, slot, heads)
 
 
+def outer_kernel(a_ref, b_ref, out_ref):
+    out_ref[...] = rows_dot(a_ref[...].reshape(-1, a_ref.shape[-1]), b_ref[0]).astype(BF16)
+
+
+def outer_call(rows, i, units):
+    blocks, _, slots, features = rows.shape
+    _, depth, n = units.shape
+    tile = 512
+    return pl.pallas_call(
+        outer_kernel,
+        grid=(features // tile,),
+        in_specs=[
+            pl.BlockSpec((blocks, 1, slots, tile), lambda j: (0, i, 0, j)),
+            pl.BlockSpec((1, depth, n), lambda j: (i, 0, 0)),
+        ],
+        out_specs=pl.BlockSpec((tile, n), lambda j: (j, 0)),
+        out_shape=jax.ShapeDtypeStruct((features, n), BF16),
+        compiler_params=pltpu.CompilerParams(vmem_limit_bytes=40 * MIB),
+    )(rows, units)
+
+
 class Line:
     def __init__(self, parts, inner, sources, outs, sib, recv, bufs, sems):
         self.parts, self.inner, self.sources, self.outs = parts, inner, sources, outs
@@ -561,16 +582,17 @@
         return taken
 
     downs, shared = take(n_down), take(n_shared)
-    three, part_out, out_part, mixed, vec, bias_add = take(6)
+    three, part_out, out_part, mixed, normed_part, tokens, base, vec, gain, bias_add = take(10)
     out_down, out_gate, out_up, out_sdown = take(4)
     out_four = take(4)
-    output, vec_out = take(2)
+    output, grad_tokens, vec_out = take(3)
     sib_a, att, sib_b, sib_c, out_in = take(5)
     bufs_a, bufs_b, bufs_c = take(5), take(5), take(5)
     recv_a, recv_b, recv_c = take(3)
     vec_in, vec_own, vec_sib, vec_line, vec_send, parts_v, mixed_v, sum_v = take(8)
+    relay_x, relay_y, got_x, got_y, sum_x, sum_y, gain_v, grad_v, vec_v = take(9)
     sems_a, sems_b, sems_c = take(7), take(7), take(7)
-    plane_send, plane_recv, local_sems, vec_send_sems, vec_recv_sems, out_send, out_recv = take(7)
+    plane_send, plane_recv, local_sems, vec_send_sems, vec_recv_sems, out_send, out_recv, norm_send, norm_recv = take(9)
 
     a = Line(parts, False, downs, [(out_down.at[j], True) for j in range(n_down)], sib_a, recv_a, bufs_a, sems_a)
     b = Line(1, False, [att.at[j] for j in range(4)], [(v, True) for v in out_four], sib_b, recv_b, bufs_b, sems_b)
@@ -619,7 +641,7 @@
 
     def vec_owner(k, p):
         return pltpu.make_async_remote_copy(
-            src_ref=vec.at[p], dst_ref=vec_in.at[k],
+            src_ref=vec_v.at[p], dst_ref=vec_in.at[k],
             send_sem=vec_send_sems.at[k], recv_sem=vec_recv_sems.at[k],
             device_id={"fsdp": p}, device_id_type=MESH,
         )
@@ -632,9 +654,79 @@
         )
 
     for k, p in enumerate(peers):
-        vec_owner(k, p).start()
-    for k, p in enumerate(peers):
         to_owner(k, p).start()
+
+    rows_half = mixed.shape[0] // 2
+    low, high = pl.ds(0, rows_half), pl.ds(rows_half, rows_half)
+
+    def norm_copy(n, src, dst, target):
+        return pltpu.make_async_remote_copy(
+            src_ref=src, dst_ref=dst, send_sem=norm_send.at[n], recv_sem=norm_recv.at[n],
+            device_id={"fsdp": target}, device_id_type=MESH,
+        )
+
+    norm_copies = [
+        norm_copy(0, normed_part.at[3, low], relay_x, fx),
+        norm_copy(1, normed_part.at[3, high], relay_y, fy),
+        norm_copy(2, normed_part.at[1, low], got_x.at[low], fx),
+        norm_copy(3, normed_part.at[2, high], got_y.at[high], fy),
+        norm_copy(4, sum_y, got_y.at[low], fy),
+        norm_copy(5, sum_x, got_x.at[high], fx),
+    ]
+    for copy in norm_copies[:4]:
+        copy.start()
+
+    def relay():
+        loads = [
+            pltpu.make_async_copy(normed_part.at[2, low], sum_y, local_sems.at[3]),
+            pltpu.make_async_copy(normed_part.at[1, high], sum_x, local_sems.at[4]),
+        ]
+        for copy in loads:
+            copy.start()
+        for copy in loads:
+            copy.wait()
+        norm_copies[0].wait_recv()
+        sum_y[...] = (sum_y[...].astype(F32) + relay_x[...].astype(F32)).astype(BF16)
+        norm_copies[4].start()
+        norm_copies[1].wait_recv()
+        sum_x[...] = (sum_x[...].astype(F32) + relay_y[...].astype(F32)).astype(BF16)
+        norm_copies[5].start()
+
+    def finish_norm():
+        for copy in norm_copies[2:]:
+            copy.wait_recv()
+        step = parts_v.shape[1]
+        gain_v[...] = jnp.zeros_like(gain_v)
+
+        def body(i, carry):
+            r = pl.ds(pl.multiple_of(i * step, step), step)
+            loads = [
+                pltpu.make_async_copy(normed_part.at[0, r], parts_v.at[0], local_sems.at[3]),
+                pltpu.make_async_copy(tokens.at[r], parts_v.at[1], local_sems.at[4]),
+                pltpu.make_async_copy(base.at[r], mixed_v, local_sems.at[5]),
+            ]
+            for copy in loads:
+                copy.start()
+            for copy in loads:
+                copy.wait()
+            total = parts_v[0].astype(F32) + (got_x[r].astype(F32) + got_y[r].astype(F32))
+            back, grad_gain = norm_back(parts_v[1].astype(F32), gain[...], total)
+            gain_v[...] = gain_v[...] + grad_gain
+            grad_v[...] = mixed_v[...] + back
+            copy = pltpu.make_async_copy(grad_v, grad_tokens.at[r], local_sems.at[6])
+            copy.start()
+            copy.wait()
+            return carry
+
+        lax.fori_loop(0, mixed.shape[0] // step, body, 0)
+        copy = pltpu.make_async_copy(vec, vec_v, local_sems.at[2])
+        copy.start()
+        copy.wait()
+        for k in range(4):
+            vec_v[k, 0:1, :] = gain_v[:, k * width : (k + 1) * width]
+        for k, p in enumerate(peers):
+            vec_owner(k, p).start()
+
     keep = (
         pltpu.make_async_copy(three.at[:, :, :, cols(f)], att.at[pl.ds(0, 3), f], local_sems.at[0]),
         pltpu.make_async_copy(part_out, att.at[3], local_sems.at[1]),
@@ -682,43 +774,6 @@
         lax.fori_loop(0, mixed.shape[0] // step, body, 0)
 
     def side_work(t):
-        @pl.when(t == 1)
-        def _():
-            for k, p in enumerate(peers):
-                vec_owner(k, p).wait_recv()
-            copy = pltpu.make_async_copy(vec.at[f], vec_own, local_sems.at[2])
-            copy.start()
-            copy.wait()
-            vec_own[...] = (vec_own[...] + vec_in[0]) + (vec_in[1] + vec_in[2]) + bias_add[...]
-            vec_swap().start()
-
-        @pl.when(t == 2)
-        def _():
-            vec_swap().wait_recv()
-            vec_sib[...] = vec_sib[...] + vec_own[...]
-
-            @pl.when(z == 0)
-            def _():
-                vec_send[0] = vec_sib[...]
-                vec_hop(0, 1).start()
-
-            @pl.when(z == 3)
-            def _():
-                vec_send[1] = vec_sib[...]
-                vec_hop(1, 2).start()
-
-        @pl.when((t == 3) & (z == 1))
-        def _():
-            vec_hop(0, 1).wait_recv()
-            vec_send[0] = vec_sib[...] + vec_line[0]
-            vec_hop(0, 2).start()
-
-        @pl.when((t == 3) & (z == 2))
-        def _():
-            vec_hop(1, 2).wait_recv()
-            vec_send[1] = vec_sib[...] + vec_line[1]
-            vec_hop(1, 1).start()
-
         @pl.when(t == 3)
         def _():
             for k, p in enumerate(peers):
@@ -726,52 +781,91 @@
             for copy in keep:
                 copy.wait()
             b.start_swaps()
+
+        @pl.when(t == 4)
+        def _():
+            relay()
             for k, p in enumerate(peers):
                 out_owner(k, p).start()
 
-        @pl.when((t == 4) & (z == 2))
+        @pl.when(t == 5)
+        def _():
+            finish_norm()
+
+        @pl.when(t == 6)
+        def _():
+            for k, p in enumerate(peers):
+                vec_owner(k, p).wait_recv()
+            vec_own[...] = (vec_v[f] + vec_in[0]) + (vec_in[1] + vec_in[2]) + bias_add[...]
+            vec_swap().start()
+
+        @pl.when(t == 7)
+        def _():
+            vec_swap().wait_recv()
+            vec_sib[...] = vec_sib[...] + vec_own[...]
+
+            @pl.when(z == 0)
+            def _():
+                vec_send[0] = vec_sib[...]
+                vec_hop(0, 1).start()
+
+            @pl.when(z == 3)
+            def _():
+                vec_send[1] = vec_sib[...]
+                vec_hop(1, 2).start()
+
+        @pl.when((t == 8) & (z == 1))
+        def _():
+            vec_hop(0, 1).wait_recv()
+            vec_send[0] = vec_sib[...] + vec_line[0]
+            vec_hop(0, 2).start()
+
+        @pl.when((t == 8) & (z == 2))
+        def _():
+            vec_hop(1, 2).wait_recv()
+            vec_send[1] = vec_sib[...] + vec_line[1]
+            vec_hop(1, 1).start()
+
+        @pl.when(t == 8)
+        def _():
+            finish_output()
+
+        @pl.when((t == 9) & (z == 2))
         def _():
             vec_hop(0, 2).wait_recv()
             vec_send[0] = vec_sib[...] + vec_line[0]
             vec_hop(0, 3).start()
             vec_out[...] = vec_send[0] + vec_line[1]
 
-        @pl.when((t == 4) & (z == 1))
+        @pl.when((t == 9) & (z == 1))
         def _():
             vec_hop(1, 1).wait_recv()
             vec_send[1] = vec_sib[...] + vec_line[1]
             vec_hop(1, 0).start()
             vec_out[...] = vec_send[1] + vec_line[0]
 
-        @pl.when((t == 5) & (z == 3))
+        @pl.when((t == 10) & (z == 3))
         def _():
             vec_hop(0, 3).wait_recv()
             vec_out[...] = vec_sib[...] + vec_line[0]
 
-        @pl.when((t == 5) & (z == 0))
+        @pl.when((t == 10) & (z == 0))
         def _():
             vec_hop(1, 0).wait_recv()
             vec_out[...] = vec_sib[...] + vec_line[1]
 
-        @pl.when(t == 6)
-        def _():
-            finish_output()
-
-    def first_loop(t, carry):
+    def loop(t, carry):
         a.turn(t)
         b.turn(t - a.chunks)
         c.turn(t)
         side_work(t)
         return carry
 
-    def last_loop(t, carry):
-        b.turn(t - a.chunks)
-        c.turn(t)
-        return carry
-
     turns = max(a.chunks + b.chunks, c.chunks) + 3
-    lax.fori_loop(0, max(7, a.chunks + 3), first_loop, 0)
-    lax.fori_loop(max(7, a.chunks + 3), turns, last_loop, 0)
+    assert turns == 11
+    lax.fori_loop(0, turns, loop, 0)
+    for copy in norm_copies:
+        copy.wait_send()
     a.finish()
     b.finish()
     c.finish()
@@ -790,7 +884,9 @@
         vec_hop(1, 0).wait_send()
 
 
-def line_call(downs, shared, three, part_out, out_part, mixed, vec, bias_add, parts, shift, collective_id):
+def line_call(
+    downs, shared, three, part_out, out_part, mixed, normed_part, tokens, base, vec, gain, bias_add, parts, shift, collective_id
+):
     _, _, rows, cols = shared[0].shape
     m, s = len(downs), len(shared)
     _, _, share, features = three.shape
@@ -816,6 +912,7 @@
             shape(width, share, dtype=F32),
             shape(width, share, dtype=F32),
             shape(own_rows, features),
+            shape(own_rows, features, dtype=F32),
             shape(*small, dtype=F32),
             shape(m, 4, rows, cols),
             shape(4, 4, 2, share, width),
@@ -823,8 +920,8 @@
             shape(s, 4, rows, cols),
             shape(3, own_rows, features),
         ),
-        in_specs=[ANY] * (m + s + 5) + [VMEM],
-        out_specs=(ANY,) * 9 + (VMEM,) + (ANY,) * 5,
+        in_specs=[ANY] * (m + s + 8) + [VMEM] * 2,
+        out_specs=(ANY,) * 10 + (VMEM,) + (ANY,) * 5,
         scratch_shapes=line_bufs((r, cols), slots, True)
         + line_bufs((share, width), slots, True)
         + line_bufs((r, cols), slots, True)
@@ -840,6 +937,15 @@
             pltpu.VMEM((4, step, features), BF16),
             pltpu.VMEM((step, features), F32),
             pltpu.VMEM((step, features), BF16),
+            pltpu.VMEM((own_rows // 2, features), BF16),
+            pltpu.VMEM((own_rows // 2, features), BF16),
+            pltpu.VMEM((own_rows, features), BF16),
+            pltpu.VMEM((own_rows, features), BF16),
+            pltpu.VMEM((own_rows // 2, features), BF16),
+            pltpu.VMEM((own_rows // 2, features), BF16),
+            pltpu.VMEM((1, features), F32),
+            pltpu.VMEM((step, features), F32),
+            pltpu.VMEM((4,) + small, F32),
         ]
         + line_sems(m * parts, slots)
         + line_sems(4, slots)
@@ -852,12 +958,14 @@
             pltpu.SemaphoreType.DMA((6,)),
             pltpu.SemaphoreType.DMA((3,)),
             pltpu.SemaphoreType.DMA((3,)),
+            pltpu.SemaphoreType.DMA((6,)),
+            pltpu.SemaphoreType.DMA((6,)),
         ],
         compiler_params=pltpu.CompilerParams(
             collective_id=collective_id, has_side_effects=True, vmem_limit_bytes=60 * MIB
         ),
-    )(*downs, *shared, three, part_out, out_part, mixed, vec, bias_add)
-    return outs[0], outs[1:4], outs[4:8], outs[8], outs[9]
+    )(*downs, *shared, three, part_out, out_part, mixed, normed_part, tokens, base, vec, gain, bias_add)
+    return outs[0], outs[1:4], outs[4:8], outs[8], outs[9], outs[10]
 
 
 def plane_neighbours():
@@ -877,8 +985,8 @@
 class Side:
     block = 512
 
-    def __init__(self, arrays, jobs):
-        self.arrays, self.jobs = list(arrays), list(jobs)
+    def __init__(self, arrays, jobs, later=()):
+        self.arrays, self.jobs, self.later = list(arrays), list(jobs), dict(later)
         self.operands = sorted({o for job in self.jobs for pair in job for o in pair}, key=str)
 
     def shape(self, operand):
@@ -896,7 +1004,7 @@
         stages = sorted({self.shape(job[0][1])[-1] for job in self.jobs})
         self.stage_of = {n: k for k, n in enumerate(stages)}
         return (
-            [pltpu.VMEM(self.shape(o), BF16) for o in self.operands]
+            [pltpu.VMEM(self.shape(o), BF16) for o in self.operands if o not in self.later]
             + [pltpu.VMEM((2, self.block, n), BF16) for n in stages]
             + [
                 pltpu.SemaphoreType.DMA((max(1, len(self.operands)),)),
@@ -905,9 +1013,11 @@
         )
 
     def bind(self, ins, outs, scratch):
-        n = len(self.operands)
+        holders = [o for o in self.operands if o not in self.later]
+        n = len(holders)
         self.ins, self.outs = ins, outs
-        self.bufs, self.stages = scratch[:n], scratch[n:-2]
+        self.bufs = [scratch[holders.index(self.later.get(o, o))] for o in self.operands]
+        self.stages = scratch[n:-2]
         self.load_sems, self.out_sems = scratch[-2:]
         self.loaded, self.pending, self.turn_of = set(), {}, {}
         self.units = [
@@ -926,7 +1036,7 @@
     def begin(self):
         for o in [o for job in self.jobs for pair in job for o in pair]:
             k = self.operands.index(o)
-            if k not in self.loaded:
+            if k not in self.loaded and o not in self.later:
                 self.loaded.add(k)
                 self.load(k).start()
         self.loaded = set()
@@ -959,6 +1069,11 @@
             )
             copy.start()
             self.pending[(stage, slot)] = copy
+            if not self.units or self.units[0][0] != j:
+                for o in [o for pair in self.jobs[j] for o in pair]:
+                    for k, heir in enumerate(self.operands):
+                        if self.later.get(heir) == o:
+                            self.load(k).start()
 
     def end(self):
         self.step(len(self.units))
@@ -1399,8 +1514,8 @@
     params = {}
     if own is not None:
         ins.append(own)
-        in_specs.append(ANY)
-        out_specs += (ANY,)
+        in_specs.append(VMEM)
+        out_specs += (VMEM,)
         out_shape += (jax.ShapeDtypeStruct((4,) + own.shape, own.dtype),)
         scratch += [pltpu.SemaphoreType.DMA((6,)), pltpu.SemaphoreType.DMA((6,)), pltpu.SemaphoreType.DMA]
         params = {"collective_id": collective_id, "has_side_effects": True}
@@ -1567,11 +1682,11 @@
         )
         return tuple(jnp.stack(self.gather_list(v)) for v in (tokens, small, marks)) + (cols,)
 
-    def middle(self, body, partial, ins, out_shapes, gathers, number, arrays=(), jobs=()):
+    def middle(self, body, partial, ins, out_shapes, gathers, number, arrays=(), jobs=(), later=()):
         nf = self.nf
         rows, cols = partial.shape[0] // nf, partial.shape[1]
         if self.fast:
-            side = Side(arrays, jobs)
+            side = Side(arrays, jobs, later)
             return mid_call(body, partial.reshape(nf, rows, cols), ins, out_shapes, gathers, side, number)
         total = self.scatter_sum(partial)
         outs = [Store(s) for s in out_shapes]
@@ -1589,7 +1704,9 @@
             sum(rows_dot(operand(a), operand(b)) for a, b in job).astype(BF16) for job in jobs
         )
 
-    def last_sums(self, downs, shared, part_three, part_output, out_part, mixed, vec, bias_add, number):
+    def last_sums(
+        self, downs, shared, part_three, part_output, out_part, mixed, normed_part, tokens, base, vec, gain, bias_add, number
+    ):
         nf, ng, nz = self.nf, self.ng, self.nz
         features, width = part_output.shape
         share = features // ng
@@ -1601,7 +1718,11 @@
                 part_output.reshape(nz, 2, share, width),
                 out_part.reshape(nf, -1, features),
                 mixed,
+                normed_part.reshape(nf, -1, features),
+                tokens,
+                base,
                 vec.reshape(16, nf, width).transpose(1, 0, 2),
+                gain,
                 bias_add,
                 2,
                 True,
@@ -1615,9 +1736,11 @@
         )
         four = jnp.concatenate([three, part_output[None]], axis=0)
         four = lax.psum_scatter(four, "grp", scatter_dimension=1, tiled=True).astype(F32)
+        back, grad_gain = norm_back(tokens.astype(F32), gain, self.scatter_sum(normed_part))
+        vec = jnp.concatenate([grad_gain, vec[1:]], axis=0)
         vec = lax.psum_scatter(vec, "fsdp", scatter_dimension=1, tiled=True) + bias_add
         output = (mixed + self.scatter_sum(out_part)).astype(BF16)
-        return down, (sums[0], sums[1], sums[2].T), four.transpose(0, 2, 1), output, lax.psum(vec, "grp")
+        return down, (sums[0], sums[1], sums[2].T), four.transpose(0, 2, 1), output, base + back, lax.psum(vec, "grp")
 
 
 def on_device(
@@ -1718,11 +1841,8 @@
         rows_in, rows_cot, gate, expert_gate, routed_up_weight, expert_down, nf // 2
     )
 
-    def slot_rows(x, i):
-        return x[:, i].reshape(nf * capacity, features)
-
-    gate_parts = [rows_dot(slot_rows(rows_in, i), d_gate[i]).astype(BF16) for i in range(local_experts)]
-    up_part = rows_dot(slot_rows(rows_in, 0), d_up[0]).astype(BF16)
+    gate_parts = [outer_call(rows_in, i, d_gate) for i in range(local_experts)]
+    up_part = outer_call(rows_in, 0, d_up)
     gate_parts, up_part, hidden, sens_rows, y_rows, moe_other = lax.optimization_barrier(
         (gate_parts, up_part, hidden, sens_rows, y_rows, moe_other)
     )
@@ -1766,17 +1886,20 @@
         ],
         axis=0,
     )
-    arrays = (rows_in, d_gate, d_up, moe_in, sd_gate, sd_up, sd_out)
+    arrays = (rows_in, d_up, hidden, moe_in, sd_gate, sd_up, sd_out)
     if wires.fast:
         o_hidden, od_gate, od_up, od_out = other_call(
             moe_other, cot_other, heads_rows, shared_gate, shared_up, shared_down, rows_dev
         )
-        arrays += (moe_other, od_gate, od_up, s_hidden, od_out, o_hidden)
+        arrays += (moe_other, od_gate, od_up, s_hidden, od_out, o_hidden, d_out)
+        later = {(13, 1, 1): (0, 1, 1), (2, 0, 1): (1, 0, 1)}
     else:
-        arrays += (None, None, None, s_hidden)
+        arrays += (None, None, None, s_hidden, None, None, d_out)
+        later = {}
     jobs = []
     for i in range(1, local_experts):
-        jobs += [(((0, 1, i), (2, 0, i)),)]
+        jobs += [(((0, 1, i), (1, 0, i)),)]
+    jobs += [(((13, 1, i), (2, 0, i)),) for i in range(local_experts)]
 
     def whole(*numbers):
         return tuple((n, None, 0) for n in numbers)
@@ -1797,32 +1920,22 @@
         3,
         arrays,
         jobs,
+        later,
     )
     late = local_experts - 1
     parts, up_sums = lax.optimization_barrier((parts, up_sums))
     up_sums += [wires.reduce_background(v) for v in parts[:late]]
-    shared_parts = parts[late:]
+    down_parts, shared_parts = parts[late : late + local_experts], parts[late + local_experts :]
     branch_grad = branch_grad.reshape(count, features)
     grad_three, normed_part, grad_bias = attend_back_call(
         branch_grad, w_output, three, w_cols, cosine, sine, mark_cols, mark_rows
     )
-    grad_tokens, grad_gain_one, part_output, part_three, *down_parts = wires.middle(
-        back_middle,
-        normed_part,
-        (tokens, gain_one, grad_mixed),
-        (
-            jax.ShapeDtypeStruct((rows_dev, features), F32),
-            jax.ShapeDtypeStruct((wires.chunks, features), F32),
-        ),
-        False,
-        4,
-        (branch_grad, attended, grad_three, normed, d_out, hidden),
-        [(whole(0, 1),), (whole(2, 3),)] + [(((4, 1, i), (5, 0, i)),) for i in range(local_experts)],
-    )
+    part_output = rows_dot(branch_grad, attended).astype(BF16)
+    part_three = rows_dot(grad_three, normed).astype(BF16)
 
     vec = jnp.concatenate(
         [
-            jnp.sum(grad_gain_one, axis=0, keepdims=True),
+            jnp.zeros_like(gain_one),
             jnp.sum(grad_gain_two, axis=0, keepdims=True),
             grad_heads,
         ],
@@ -1830,8 +1943,20 @@
     )
     vec = jnp.pad(vec, ((0, 16 - vec.shape[0]), (0, 0)))
     bias_add = jnp.pad(grad_bias.reshape(3, width), ((experts + 3, 16 - experts - 6), (0, 0)))
-    down_sums, shared_sums, four, output, vec = wires.last_sums(
-        down_parts, shared_parts, part_three, part_output, out_part, mixed, vec, bias_add, 5
+    down_sums, shared_sums, four, output, grad_tokens, vec = wires.last_sums(
+        down_parts,
+        shared_parts,
+        part_three,
+        part_output,
+        out_part,
+        mixed,
+        normed_part,
+        tokens,
+        grad_mixed,
+        vec,
+        gain_one,
+        bias_add,
+        5,
     )
     own = width // ng
     vec = lax.dynamic_slice_in_dim(vec, lax.axis_index("grp") * own, own, 1)

time: 855 us -> 842 us (0.985)
  Pallas kernels: 734 us -> 719 us
  local copies, waits for them, and re-layouts: 38.4 us -> 52.9 us
  matrix products: 29.6 us -> 16.9 us
    pallas_call x3 -> x2, Pallas kernels: 202 us -> 161 us  [mid_call(): pl.pallas_call(functools.partial(mid_kernel, middle, chunks, gathers, len...]
    unnamed x62 -> x84, local copies, waits for them, and re-layouts: 22.5 us -> 42.7 us
    pallas_call x0 -> x3, Pallas kernels: none -> 17.8 us  [outer_call(): pl.pallas_call(outer_kernel, grid=(features // tile,), in_specs=[pl.Block...]
    dot_general x4 -> x3, matrix products: 28.8 us -> 16.1 us  [dot(): lax.dot_general(left, right, (dims, ((), ())), preferred_element_type=out)]
  transfers between devices with their start and end apart: 6 -> 6, of which waited for: 0 -> 0; matrix products, arithmetic and copies ran while one was open for 6% -> 4% of each run, Pallas kernels for 75% -> 74%
where the time goes in v4:
time: 842 us; the launch traced here: 831 us
  Pallas kernels  719 us (85%)
  local copies, waits for them, and re-layouts  52.9 us (6%)
  other arithmetic  17.8 us (2%)
  matrix products  16.9 us (2%)
  between operations  14.7 us (2%)
    pallas_call x1, Pallas kernels, line_call(): pl.pallas_call(functools.partial(line_kernel, m, s, parts, shift), out_sh...  238 us
    pallas_call x2, Pallas kernels, mid_call(): pl.pallas_call(functools.partial(mid_kernel, middle, chunks, gathers, len...  161 us
    pallas_call x1, Pallas kernels, expert_call(): pl.pallas_call(expert_kernel, grid=(experts, steps), in_specs=[slot_spec(...  59.5 us
    pallas_call x1, Pallas kernels, start_call(): pl.pallas_call(start_kernel, out_shape=(jax.ShapeDtypeStruct((4,) + token...  57.8 us
    pallas_call x1, Pallas kernels, shared_call(): pl.pallas_call(shared_kernel, grid=(blocks,), in_specs=[rows_spec(feature...  56.9 us
    pallas_call x1, Pallas kernels, attend_call(): pl.pallas_call(attend_kernel, in_specs=in_specs, out_specs=out_specs, out...  48.1 us
    unnamed x84, local copies, waits for them, and re-layouts  42.7 us
    pallas_call x1, Pallas kernels, attend_back_call(): pl.pallas_call(attend_back_kernel, in_specs=[VMEM] * 8, out_specs=(VMEM,)...  38.3 us
  transfers between devices with their start and end apart: 6, of which 0 were waited for; matrix products, arithmetic and copies ran while one was open for 4% of the time, Pallas kernels for 74%

profile of v4, /device:TPU:0, one launch (start us, length us, event | category | flops | bytes accessed | tf_op | source)
XLA Modules:
  0.0 830.9 jit_solution(15608671556844549546)
XLA Ops:
  10.8 1.2 copy-done.10
  12.1 1.6 copy-done.12
  13.7 1.6 copy-done.13
  15.2 1.6 copy-done.14
  16.8 57.8 %shard_map.366 = (bf16[4,256,2048]{2,1,0:T(8,128)(2,1)S(1)}, bf16[4,16,512]{2,1,0:T(8,128)(2,1)S(1)}, s32[4,16,256]{2,1,0:T(8,128)S(1)}, bf16[2048,1536]{1,0:T(8,128)(2,1)S(1)}, bf16[2,3,64,512]{3,2,1,0:T(8,128)(2,1)}) custom-call(bf16[256,2048]{1,0:T(8,128)(2,1)S(1)} %copy-done.10, bf16[16,512]{1,0:T(8,128)(2,1)S(1)} %fusion.19.small, ...), custom_call_target="tpu_custom_call" | custom-call | tf_op jit(solution)/shard_map/pallas_call | solution.py:1371
  74.6 2.6 copy-done.3
  77.3 1.9 copy-done.11
  79.9 1.0 copy.72.mark_cols
  81.6 3.0 fusion.2
  85.3 48.1 %shard_map.367 = (bf16[1024,2048]{1,0:T(8,128)(2,1)}, bf16[1024,1536]{1,0:T(8,128)(2,1)}, bf16[1024,512]{1,0:T(8,128)(2,1)}, bf16[1024,2048]{1,0:T(8,128)(2,1)}, bf16[4,256,2048]{2,1,0:T(8,128)(2,1)}) custom-call(bf16[1024,2048]{1,0:T(8,128)(2,1)} %bitcast.85, f32[1,2048]{1,0:T(1,128)} %get-tuple-element.173.gain.refs_13_, bf16[2048,1536]{1,0:T(8,128)(2,1)} %copy-done.3, ...), custom_call_target="tpu_custom_call" | custom-call | tf_op jit(solution)/shard_map/pallas_call | solution.py:1522
  133.4 4.2 collective-permute-start
  137.6 73.6 %shard_map.368 = (f32[256,2048]{1,0:T(8,128)}, bf16[4,256,2048]{2,1,0:T(8,128)(2,1)}) custom-call(bf16[4,256,2048]{2,1,0:T(8,128)(2,1)} %bitcast.104, bf16[256,2048]{1,0:T(8,128)(2,1)} %refs_10_.1, f32[1,2048]{1,0:T(1,128)} %get-tuple-element.172.refs_2_), custom_call_target="tpu_custom_call" | custom-call | tf_op jit(solution)/shard_map/pallas_call | solution.py:1197
  211.2 3.4 collective-permute-start.1
  214.6 0.8 slice.109
  217.0 11.7 %shard_map.369 = (bf16[4,2,160,2048]{3,2,1,0:T(8,128)(2,1)}, bf16[4,2,160,2048]{3,2,1,0:T(8,128)(2,1)}, f32[4,2,160,1]{3,2,1,0:T(8,128)}, bf16[4,320,256]{2,1,0:...) custom-call(bf16[1024,2048]{1,0:T(8,128)(2,1)} %bitcast.87, bf16[1024,2048]{1,0:T(8,128)(2,1)} %bitcast.92, ...), custom_call_target="tpu_custom_call" | custom-call | tf_op jit(solution)/shard_map/pallas_call | solution.py:263
  228.8 59.5 %shard_map.370 = (bf16[2,640,1408]{2,1,0:T(8,128)(2,1)}, bf16[2,640,1408]{2,1,0:T(8,128)(2,1)}, bf16[2,640,1408]{2,1,0:T(8,128)(2,1)}, bf16[4,2,160,2048]{3,2,1,...) custom-call(bf16[4,2,160,2048]{3,2,1,0:T(8,128)(2,1)} %get-tuple-ele, ...), custom_call_target="tpu_custom_call" | custom-call | tf_op jit(solution)/shard_map/pallas_call | solution.py:101
  288.3 2.5 copy-done
  290.8 2.0 copy-done.7
  292.8 6.0 shard_map.372
  298.8 2.5 copy-done.4
  301.3 2.5 copy-done.1
  303.8 2.0 copy-done.8
  305.8 5.9 shard_map.371
  311.7 2.4 copy-done.5
  314.1 2.5 copy-done.2
  316.6 2.0 copy-done.9
  318.6 5.9 shard_map.373
  324.5 2.5 copy-done.6
  329.2 1.3 iota_compare_fusion.3
  332.6 30.5 %shard_map.375 = (bf16[1024,1408]{1,0:T(8,128)(2,1)}, bf16[1024,1408]{1,0:T(8,128)(2,1)}, bf16[1024,1408]{1,0:T(8,128)(2,1)}, bf16[1024,2048]{1,0:T(8,128)(2,1)}) custom-call(bf16[1024,2048]{1,0:T(8,128)(2,1)} %collective-permute-done.1.x_ref.refs_11_, bf16[1024,2048]{1,0:T(8,128)(2,1)} %collective-permute-done.g_ref, bf16[9,2048]{1,0:T(8,128)(2,1)} %slice.110.heads, ...), custom_call_target="tpu_custom_call" | custom-call | tf_op jit(solution)/shard_map/pallas_call | solution.py:206
  363.2 0.9 pad_maximum_fusion.lane_ref
  364.0 56.9 %shard_map.374 = (bf16[1024,1408]{1,0:T(8,128)(2,1)}, bf16[1024,1408]{1,0:T(8,128)(2,1)}, bf16[1024,1408]{1,0:T(8,128)(2,1)}, bf16[1024,2048]{1,0:T(8,128)(2,1)}...) custom-call(bf16[1024,2048]{1,0:T(8,128)(2,1)} %bitcast.88, ...), custom_call_target="tpu_custom_call" | custom-call | tf_op jit(solution)/shard_map/pallas_call | solution.py:162
  421.0 87.2 %shard_map.376 = (f32[256,2048]{1,0:T(8,128)}, f32[4,2048]{1,0:T(4,128)}, bf16[4,256,2048]{2,1,0:T(8,128)(2,1)}, bf16[2048,1408]{1,0:T(8,128)(2,1)}, bf16[2048,1...) custom-call(bf16[4,256,2048]{2,1,0:T(8,128)(2,1)} %bitcast.107, ...), custom_call_target="tpu_custom_call" | custom-call | tf_op jit(solution)/shard_map/pallas_call | solution.py:1197
  509.6 38.3 %shard_map.377 = (bf16[1024,1536]{1,0:T(8,128)(2,1)}, bf16[1024,2048]{1,0:T(8,128)(2,1)}, f32[1,1536]{1,0:T(1,128)}) custom-call(bf16[1024,2048]{1,0:T(8,128)(2,1)} %bitcast.105, bf16[512,2048]{1,0:T(8,128)(2,1)} %w_out.3, bf16[1024,1536]{1,0:T(8,128)(2,1)} %get-tuple-element.142.three, bf16[2048,1536]{1,0:T(8,128)(2,1)} %copy-done.3, ...), custom_call_target="tpu_custom_call" | custom-call | tf_op jit(solution)/shard_map/pallas_call | solution.py:1588
  549.4 3.3 fusion.5
  553.4 3.8 convolution_convert_fusion.1
  557.2 9.1 %convolution_convert_fusion = bf16[1536,2048]{1,0:T(8,128)(2,1)} fusion(bf16[1024,1536]{1,0:T(8,128)(2,1)S(1)} %copy-done.35, bf16[1024,2048]{1,0:T(8,128)(2,1)S(1)} %copy-done.34), kind=kOutput, calls=%fused_computation | convolution fusion | flops 6445596672 | bytes 13631488 | tf_op jit(solution)/shard_map/dot_general | solution.py:25
  566.3 238.0 %shard_map.378 = (f32[2,1408,256]{2,1,0:T(8,128)}, f32[256,1408]{1,0:T(8,128)}, f32[256,1408]{1,0:T(8,128)}, f32[1408,256]{1,0:T(8,128)}, f32[512,256]{1,0:T(8,1...) custom-call(bf16[4,2,256,1408]{3,2,1,0:T(8,128)(2,1)} %bitcast.95, ...), custom_call_target="tpu_custom_call" | custom-call | tf_op jit(solution)/shard_map/pallas_call | solution.py:903
  804.3 1.5 dynamic-slice_bitcast_fusion.5
  805.7 1.4 dynamic-slice_bitcast_fusion.4
  807.1 3.2 maximum_convert_fusion
  810.3 3.2 maximum_convert_fusion.1
  813.5 1.0 copy.99
  814.5 1.3 copy.100
  819.0 1.1 copy.105
  820.1 1.1 copy.106
  821.2 1.1 copy.107
  822.3 1.6 copy.108
  (126 shorter events, 18.2 us)
Async XLA Ops:
  7.2 501.0 %reduce-scatter.5.cloned.1.call-start = ((), (), s32[]{:S(2)}) async-start(), calls=%async_computation.4 | async-start | bytes 6488064 | tf_op jit(solution)/shard_map/reduce_scatter | solution.py:1674
  10.1 70.9 %copy-start.31 = (bf16[512]{0:T(512)(128)(2,1)S(1)}, bf16[512]{0:T(512)(128)(2,1)}, u32[]{:S(2)}) copy-start(bf16[512]{0:T(512)(128)(2,1)} %param.33) | copy-start | bytes 3076
  10.1 70.9 %copy-start.32 = (bf16[512]{0:T(512)(128)(2,1)S(1)}, bf16[512]{0:T(512)(128)(2,1)}, u32[]{:S(2)}) copy-start(bf16[512]{0:T(512)(128)(2,1)} %param.34) | copy-start | bytes 3076
  10.1 70.9 %copy-start.33 = (bf16[512]{0:T(512)(128)(2,1)S(1)}, bf16[512]{0:T(512)(128)(2,1)}, u32[]{:S(2)}) copy-start(bf16[512]{0:T(512)(128)(2,1)} %param.35) | copy-start | bytes 3076
  10.8 1.2 copy-start.10
  12.1 1.6 copy-start.12
  13.7 1.6 copy-start.13
  15.2 1.6 copy-start.14
  74.6 2.6 copy-start.3
  77.3 1.9 copy-start.11
  133.4 95.3 %collective-permute-start = (bf16[1024,2048]{1,0:T(8,128)(2,1)}, bf16[1024,2048]{1,0:T(8,128)(2,1)}, u32[]{:S(2)}, u32[]{:S(2)}) collective-permute-start(bf16[1024,2048]{1,0:T(8,128)(2,1)} %bitcast.91), channel_id=1, source_target_pairs={{0,8},{4,12},{24,16},{28,20},{1,9},{5,13},{25,17},{29,21},{2,10},{... | collective-permute-start | bytes 12582920 | tf_op jit(solution)/shard_map/ppermute | solution.py:1657
  211.2 115.8 %collective-permute-start.1 = (bf16[1024,2048]{1,0:T(8,128)(2,1)}, bf16[1024,2048]{1,0:T(8,128)(2,1)}, u32[]{:S(2)}, u32[]{:S(2)}) collective-permute-start(bf16[1024,2048]{1,0:T(8,128)(2,1)} %bitcast.86), channel_id=1, source_target_pairs={{0,8},{4,12},{24,16},{28,20},{1,9},{5,13},{25,17},{29,21},{2,10},{... | collective-permute-start | bytes 12582920 | tf_op jit(solution)/shard_map/ppermute | solution.py:1657
  288.3 2.5 copy-start
  290.8 2.0 copy-start.7
  298.8 2.5 copy-start.4
  301.3 2.5 copy-start.1
  303.8 2.0 copy-start.8
  311.7 2.5 copy-start.5
  314.1 2.5 copy-start.2
  316.6 2.0 copy-start.9
  324.5 2.5 copy-start.6
  327.0 480.0 %reduce-scatter.7.cloned.1.call-start = ((), (), s32[]{:S(2)}) async-start(), calls=%async_computation.5 | async-start | bytes 6488064 | tf_op jit(solution)/shard_map/reduce_scatter | solution.py:1674
  327.8 3.4 copy-start.23
  327.8 3.7 copy-start.29
  327.8 4.3 copy-start.17
  327.8 479.3 %reduce-scatter.9.cloned.1.call-start = ((), (), s32[]{:S(2)}) async-start(), calls=%async_computation.6 | async-start | bytes 6488064 | tf_op jit(solution)/shard_map/reduce_scatter | solution.py:1674
  328.6 481.7 %reduce-scatter.11.cloned.1.call-start = ((), (), s32[]{:S(2)}) async-start(), calls=%async_computation.7 | async-start | bytes 6488064 | tf_op jit(solution)/shard_map/reduce_scatter | solution.py:1674
  508.2 1.1 copy-start.24
  509.6 39.1 %copy-start.30 = (f32[4,2048]{1,0:T(4,128)S(1)}, f32[4,2048]{1,0:T(4,128)}, u32[]{:S(2)}) copy-start(f32[4,2048]{1,0:T(4,128)} %get-tuple-element.149) | copy-start | bytes 98308
  547.9 5.6 copy-start.36
  548.7 4.7 copy-start.15
  553.4 3.8 copy-start.34
  553.4 3.8 copy-start.35
  807.1 6.4 copy-start.22
  810.3 4.2 copy-start.18
  813.5 2.3 copy-start.28
  813.5 3.1 copy-start.27
  813.5 3.9 copy-start.26
  814.5 3.7 copy-start.25
  814.5 4.5 copy-start.21
  815.8 4.3 copy-start.20
  816.6 4.6 copy-start.19
  819.0 3.3 copy-start.16
Sparse Core Ops, SparseCore 0:
  327.2 65.9 reduce-scatter.4
  395.5 63.2 reduce-scatter.6
  461.0 63.2 reduce-scatter.8
  526.4 73.4 reduce-scatter.10

commit v5 on v4

--- a/solution.py
+++ b/solution.py
@@ -117,7 +117,7 @@
     )(rows_in, rows_cot, gate, w_gate, w_up, w_down)
 
 
-def shared_kernel(
+def own_kernel(
     x_ref, g_ref, head_ref, pick_ref, y_in, dx_in, lane_ref, heads_w, switch_row, wg, wu, wd,
     hidden, d_gate, d_up, d_out, y_ref, dx_ref, sens_ref,
 ):
@@ -141,47 +141,6 @@
         dx_ref[:, s] = dx.astype(BF16)
 
 
-def shared_call(x, g, opener, pick, y_in, dx_in, lanes, heads_w, switch_row, w_gate, w_up, w_down):
-    count, features = x.shape
-    units = w_gate.shape[1]
-    blocks, taken, tile = pick.shape
-    width = lanes.shape[1]
-
-    def rows_spec(cols):
-        return pl.BlockSpec((tile, cols), lambda b: (b, 0))
-
-    def block_spec(cols):
-        return pl.BlockSpec((1, taken, cols), lambda b: (b, 0, 0))
-
-    def whole(a, b):
-        return pl.BlockSpec((a, b), lambda b_: (0, 0), pipeline_mode=pl.Buffered(1))
-
-    def shape(cols, dtype=BF16):
-        return jax.ShapeDtypeStruct((count, cols), dtype)
-
-    return pl.pallas_call(
-        shared_kernel,
-        grid=(blocks,),
-        in_specs=[
-            rows_spec(features),
-            rows_spec(features),
-            rows_spec(1),
-            block_spec(tile),
-            block_spec(features),
-            block_spec(features),
-            rows_spec(width),
-            whole(width, features),
-            whole(1, features),
-            whole(features, units),
-            whole(features, units),
-            whole(units, features),
-        ],
-        out_specs=[rows_spec(units)] * 3 + [rows_spec(features)] * 3 + [rows_spec(1)],
-        out_shape=[shape(units)] * 3 + [shape(features)] * 3 + [shape(1, F32)],
-        compiler_params=pltpu.CompilerParams(vmem_limit_bytes=62 * MIB),
-    )(x, g, opener, pick, y_in, dx_in, lanes, heads_w, switch_row, w_gate, w_up, w_down)
-
-
 def other_kernel(x_ref, g_ref, heads, wg, wu, wd, hidden, d_gate, d_up, d_out):
     x = x_ref[...]
     pre = trans_dot(x, heads[...])
@@ -190,34 +149,77 @@
     hidden_part(x, d_out[...], 1.0, wg, wu, wd, hidden, d_gate, d_up)
 
 
-def other_call(x, g, heads, w_gate, w_up, w_down, tile):
+def shared_kernel(blocks, others, *refs):
+    if not others:
+        own_kernel(*refs)
+        return
+    ins, outs = refs[:15], refs[15:]
+    weights = ins[9:12]
+    step = pl.program_id(0)
+
+    @pl.when(step < blocks)
+    def _():
+        own_kernel(*ins[:12], *outs[:7])
+
+    @pl.when(step >= blocks)
+    def _():
+        other_kernel(*ins[12:15], *weights, *outs[7:])
+
+
+def shared_call(x, g, opener, pick, y_in, dx_in, lanes, heads_w, switch_row, w_gate, w_up, w_down, others=None):
     count, features = x.shape
     units = w_gate.shape[1]
-
-    def rows_spec(cols):
-        return pl.BlockSpec((tile, cols), lambda b: (b, 0))
+    blocks, taken, tile = pick.shape
+    width = lanes.shape[1]
+
+    def own(b):
+        return jnp.minimum(b, blocks - 1)
+
+    def other(b):
+        return jnp.maximum(b - blocks, 0)
+
+    def rows_spec(cols, place=own):
+        return pl.BlockSpec((tile, cols), lambda b: (place(b), 0))
+
+    def block_spec(cols):
+        return pl.BlockSpec((1, taken, cols), lambda b: (own(b), 0, 0))
 
     def whole(a, b):
         return pl.BlockSpec((a, b), lambda b_: (0, 0), pipeline_mode=pl.Buffered(1))
 
-    def shape(cols):
-        return jax.ShapeDtypeStruct((count, cols), BF16)
-
+    def shape(cols, dtype=BF16):
+        return jax.ShapeDtypeStruct((count, cols), dtype)
+
+    ins = [x, g, opener, pick, y_in, dx_in, lanes, heads_w, switch_row, w_gate, w_up, w_down]
+    in_specs = [
+        rows_spec(features),
+        rows_spec(features),
+        rows_spec(1),
+        block_spec(tile),
+        block_spec(features),
+        block_spec(features),
+        rows_spec(width),
+        whole(width, features),
+        whole(1, features),
+        whole(features, units),
+        whole(features, units),
+        whole(units, features),
+    ]
+    out_specs = [rows_spec(units)] * 3 + [rows_spec(features)] * 3 + [rows_spec(1)]
+    out_shape = [shape(units)] * 3 + [shape(features)] * 3 + [shape(1, F32)]
+    if others:
+        ins += others
+        in_specs += [rows_spec(features, other)] * 2 + [whole(others[2].shape[0], features)]
+        out_specs += [rows_spec(units, other)] * 3 + [rows_spec(features, other)]
+        out_shape += [shape(units)] * 3 + [shape(features)]
     return pl.pallas_call(
-        other_kernel,
-        grid=(count // tile,),
-        in_specs=[
-            rows_spec(features),
-            rows_spec(features),
-            whole(heads.shape[0], features),
-            whole(features, units),
-            whole(features, units),
-            whole(units, features),
-        ],
-        out_specs=[rows_spec(units)] * 3 + [rows_spec(features)],
-        out_shape=[shape(units)] * 3 + [shape(features)],
+        functools.partial(shared_kernel, blocks, bool(others)),
+        grid=(2 * blocks if others else blocks,),
+        in_specs=in_specs,
+        out_specs=out_specs,
+        out_shape=out_shape,
         compiler_params=pltpu.CompilerParams(vmem_limit_bytes=62 * MIB),
-    )(x, g, heads, w_gate, w_up, w_down)
+    )(*ins)
 
 
 def dispatch_kernel(x_ref, g_ref, slot_ref, heads, rows_in, rows_cot, gate_ref, pick_ref, probs_ref, opener_ref):
@@ -306,7 +308,7 @@
         ],
         out_specs=pl.BlockSpec((tile, n), lambda j: (j, 0)),
         out_shape=jax.ShapeDtypeStruct((features, n), BF16),
-        compiler_params=pltpu.CompilerParams(vmem_limit_bytes=40 * MIB),
+        compiler_params=pltpu.CompilerParams(vmem_limit_bytes=62 * MIB),
     )(rows, units)
 
 
@@ -1841,12 +1843,14 @@
         rows_in, rows_cot, gate, expert_gate, routed_up_weight, expert_down, nf // 2
     )
 
-    gate_parts = [outer_call(rows_in, i, d_gate) for i in range(local_experts)]
+    gate_part = outer_call(rows_in, 0, d_gate)
+    gate_sums = [wires.reduce_background(gate_part)]
+    late_gates = [outer_call(rows_in, i, d_gate) for i in range(1, local_experts)]
     up_part = outer_call(rows_in, 0, d_up)
-    gate_parts, up_part, hidden, sens_rows, y_rows, moe_other = lax.optimization_barrier(
-        (gate_parts, up_part, hidden, sens_rows, y_rows, moe_other)
+    gate_part, late_gates, up_part, hidden, sens_rows, y_rows, moe_other = lax.optimization_barrier(
+        (gate_part, late_gates, up_part, hidden, sens_rows, y_rows, moe_other)
     )
-    gate_sums = [wires.reduce_background(v) for v in gate_parts]
+    gate_sums += [wires.reduce_background(v) for v in late_gates]
     up_sums = [wires.reduce_background(up_part)]
 
     gate_grad = jnp.sum(jnp.where(pick, sens_rows, 0.0), axis=2)
@@ -1862,7 +1866,7 @@
     lanes = jnp.concatenate([high, (logit_grad - high.astype(F32)).astype(BF16)], axis=1)
     router_rows = heads_rows[:experts]
     taken = (nf, local_experts * capacity, features)
-    s_hidden, sd_gate, sd_up, sd_out, out_part, moe_part, gate_sens = shared_call(
+    s_hidden, sd_gate, sd_up, sd_out, out_part, moe_part, gate_sens, *of_other = shared_call(
         moe_in,
         cot_all,
         opener,
@@ -1875,6 +1879,7 @@
         shared_gate,
         shared_up,
         shared_down,
+        [moe_other, cot_other, heads_rows] if wires.fast else None,
     )
     sens_high = gate_sens.astype(BF16)
     sens_low = (gate_sens - sens_high.astype(F32)).astype(BF16)
@@ -1888,9 +1893,7 @@
     )
     arrays = (rows_in, d_up, hidden, moe_in, sd_gate, sd_up, sd_out)
     if wires.fast:
-        o_hidden, od_gate, od_up, od_out = other_call(
-            moe_other, cot_other, heads_rows, shared_gate, shared_up, shared_down, rows_dev
-        )
+        o_hidden, od_gate, od_up, od_out = of_other
         arrays += (moe_other, od_gate, od_up, s_hidden, od_out, o_hidden, d_out)
         later = {(13, 1, 1): (0, 1, 1), (2, 0, 1): (1, 0, 1)}
     else:

time: 842 us -> 827 us (0.982)
  local copies, waits for them, and re-layouts: 52.9 us -> 31.2 us
    unnamed x84 -> x66, local copies, waits for them, and re-layouts: 42.7 us -> 21 us
    pallas_call x3, Pallas kernels: 17.8 us -> 26.2 us  [outer_call(): pl.pallas_call(outer_kernel, grid=(features // tile,), in_specs=[pl.Block...]
    pallas_call x2 -> x1, Pallas kernels: 87.5 us -> 81.8 us  [shared_call(): pl.pallas_call(functools.partial(shared_kernel, blocks, bool(others)), gr...]
  transfers between devices with their start and end apart: 6 -> 6, of which waited for: 0 -> 1; matrix products, arithmetic and copies ran while one was open for 4% -> 4% of each run, Pallas kernels for 74% -> 76%
where the time goes in v5:
time: 827 us; the launch traced here: 815 us
  Pallas kernels  726 us (88%)
  local copies, waits for them, and re-layouts  31.2 us (4%)
  other arithmetic  17.8 us (2%)
  matrix products  16.6 us (2%)
  between operations  14.4 us (2%)
    pallas_call x1, Pallas kernels, line_call(): pl.pallas_call(functools.partial(line_kernel, m, s, parts, shift), out_sh...  242 us
    pallas_call x2, Pallas kernels, mid_call(): pl.pallas_call(functools.partial(mid_kernel, middle, chunks, gathers, len...  160 us
    pallas_call x1, Pallas kernels, shared_call(): pl.pallas_call(functools.partial(shared_kernel, blocks, bool(others)), gr...  81.8 us
    pallas_call x1, Pallas kernels, expert_call(): pl.pallas_call(expert_kernel, grid=(experts, steps), in_specs=[slot_spec(...  59.5 us
    pallas_call x1, Pallas kernels, start_call(): pl.pallas_call(start_kernel, out_shape=(jax.ShapeDtypeStruct((4,) + token...  57.8 us
    pallas_call x1, Pallas kernels, attend_call(): pl.pallas_call(attend_kernel, in_specs=in_specs, out_specs=out_specs, out...  48.1 us
    pallas_call x1, Pallas kernels, attend_back_call(): pl.pallas_call(attend_back_kernel, in_specs=[VMEM] * 8, out_specs=(VMEM,)...  38.5 us
    pallas_call x3, Pallas kernels, outer_call(): pl.pallas_call(outer_kernel, grid=(features // tile,), in_specs=[pl.Block...  26.2 us
  transfers between devices with their start and end apart: 6, of which 1 were waited for; matrix products, arithmetic and copies ran while one was open for 4% of the time, Pallas kernels for 76%

profile of v5, /device:TPU:0, one launch (start us, length us, event | category | flops | bytes accessed | tf_op | source)
XLA Modules:
  0.0 815.3 jit_solution(16422594396959605819)
XLA Ops:
  7.3 0.7 broadcast_in_dim.94
  9.3 0.7 pad_add_fusion.1
  10.1 0.7 fusion.19.small
  10.8 1.2 copy-done.1
  12.1 1.6 copy-done.3
  13.7 1.6 copy-done.4
  15.2 1.6 copy-done.5
  16.8 57.8 %shard_map.366 = (bf16[4,256,2048]{2,1,0:T(8,128)(2,1)S(1)}, bf16[4,16,512]{2,1,0:T(8,128)(2,1)S(1)}, s32[4,16,256]{2,1,0:T(8,128)S(1)}, bf16[2048,1536]{1,0:T(8,128)(2,1)S(1)}, bf16[2,3,64,512]{3,2,1,0:T(8,128)(2,1)}) custom-call(bf16[256,2048]{1,0:T(8,128)(2,1)S(1)} %copy-done.1, bf16[16,512]{1,0:T(8,128)(2,1)S(1)} %fusion.19.small, ...), custom_call_target="tpu_custom_call" | custom-call | tf_op jit(solution)/shard_map/pallas_call | solution.py:1373
  74.6 2.6 copy-done
  77.3 1.9 copy-done.2
  79.9 1.0 copy.72.mark_cols
  81.6 3.0 fusion.2
  85.3 48.1 %shard_map.367 = (bf16[1024,2048]{1,0:T(8,128)(2,1)}, bf16[1024,1536]{1,0:T(8,128)(2,1)}, bf16[1024,512]{1,0:T(8,128)(2,1)}, bf16[1024,2048]{1,0:T(8,128)(2,1)}, bf16[4,256,2048]{2,1,0:T(8,128)(2,1)}) custom-call(bf16[1024,2048]{1,0:T(8,128)(2,1)} %bitcast.85, f32[1,2048]{1,0:T(1,128)} %get-tuple-element.171.gain.refs_13_, bf16[2048,1536]{1,0:T(8,128)(2,1)} %copy-done, ...), custom_call_target="tpu_custom_call" | custom-call | tf_op jit(solution)/shard_map/pallas_call | solution.py:1524
  133.5 4.3 collective-permute-start
  137.7 73.6 %shard_map.368 = (f32[256,2048]{1,0:T(8,128)}, bf16[4,256,2048]{2,1,0:T(8,128)(2,1)}) custom-call(bf16[4,256,2048]{2,1,0:T(8,128)(2,1)} %bitcast.104, bf16[256,2048]{1,0:T(8,128)(2,1)} %refs_10_.3, f32[1,2048]{1,0:T(1,128)} %get-tuple-element.170.refs_2_), custom_call_target="tpu_custom_call" | custom-call | tf_op jit(solution)/shard_map/pallas_call | solution.py:1199
  211.3 3.3 collective-permute-start.1
  214.6 0.8 slice.109
  216.2 0.8 fusion.1.slot_ref
  217.0 11.5 %shard_map.369 = (bf16[4,2,160,2048]{3,2,1,0:T(8,128)(2,1)}, bf16[4,2,160,2048]{3,2,1,0:T(8,128)(2,1)}, f32[4,2,160,1]{3,2,1,0:T(8,128)}, bf16[4,320,256]{2,1,0:...) custom-call(bf16[1024,2048]{1,0:T(8,128)(2,1)} %bitcast.87, bf16[1024,2048]{1,0:T(8,128)(2,1)} %bitcast.92, ...), custom_call_target="tpu_custom_call" | custom-call | tf_op jit(solution)/shard_map/pallas_call | solution.py:265
  228.6 59.5 %shard_map.370 = (bf16[2,640,1408]{2,1,0:T(8,128)(2,1)}, bf16[2,640,1408]{2,1,0:T(8,128)(2,1)}, bf16[2,640,1408]{2,1,0:T(8,128)(2,1)}, bf16[4,2,160,2048]{3,2,1,...) custom-call(bf16[4,2,160,2048]{3,2,1,0:T(8,128)(2,1)} %get-tuple-ele, ...), custom_call_target="tpu_custom_call" | custom-call | tf_op jit(solution)/shard_map/pallas_call | solution.py:101
  288.1 8.8 %shard_map.371 = bf16[2048,1408]{1,0:T(8,128)(2,1)} custom-call(bf16[4,2,160,2048]{3,2,1,0:T(8,128)(2,1)} %get-tuple-element.101.x_ref.a_ref.refs_4_, bf16[2,640,1408]{2,1,0:T(8,128)(2,1)} %get-tuple-element.105.b_ref), custom_call_target="tpu_custom_call" | custom-call | tf_op jit(solution)/shard_map/pallas_call | solution.py:302
  296.8 8.7 %shard_map.372 = bf16[2048,1408]{1,0:T(8,128)(2,1)} custom-call(bf16[4,2,160,2048]{3,2,1,0:T(8,128)(2,1)} %get-tuple-element.101.x_ref.a_ref.refs_4_, bf16[2,640,1408]{2,1,0:T(8,128)(2,1)} %get-tuple-element.105.b_ref), custom_call_target="tpu_custom_call" | custom-call | tf_op jit(solution)/shard_map/pallas_call | solution.py:302
  305.6 8.7 %shard_map.373 = bf16[2048,1408]{1,0:T(8,128)(2,1)} custom-call(bf16[4,2,160,2048]{3,2,1,0:T(8,128)(2,1)} %get-tuple-element.101.x_ref.a_ref.refs_4_, bf16[2,640,1408]{2,1,0:T(8,128)(2,1)} %get-tuple-element.106.b_ref.refs_5_), custom_call_target="tpu_custom_call" | custom-call | tf_op jit(solution)/shard_map/pallas_call | solution.py:302
  314.9 0.7 reduce-scatter.7.cloned.1.call-update
  317.1 1.3 iota_compare_fusion.3
  320.5 0.9 pad_maximum_fusion.refs_6_
  321.4 81.8 %shard_map.374 = (bf16[1024,1408]{1,0:T(8,128)(2,1)}, bf16[1024,1408]{1,0:T(8,128)(2,1)}, bf16[1024,1408]{1,0:T(8,128)(2,1)}, bf16[1024,2048]{1,0:T(8,128)(2,1)}...) custom-call(bf16[1024,2048]{1,0:T(8,128)(2,1)} %bitcast.88, ...), custom_call_target="tpu_custom_call" | custom-call | tf_op jit(solution)/shard_map/pallas_call | solution.py:215
  403.2 86.9 %shard_map.375 = (f32[256,2048]{1,0:T(8,128)}, f32[4,2048]{1,0:T(4,128)}, bf16[4,256,2048]{2,1,0:T(8,128)(2,1)}, bf16[2048,1408]{1,0:T(8,128)(2,1)}, bf16[2048,1...) custom-call(bf16[4,256,2048]{2,1,0:T(8,128)(2,1)} %bitcast.107, ...), custom_call_target="tpu_custom_call" | custom-call | tf_op jit(solution)/shard_map/pallas_call | solution.py:1199
  490.3 38.5 %shard_map.376 = (bf16[1024,1536]{1,0:T(8,128)(2,1)}, bf16[1024,2048]{1,0:T(8,128)(2,1)}, f32[1,1536]{1,0:T(1,128)}) custom-call(bf16[1024,2048]{1,0:T(8,128)(2,1)} %bitcast.105, bf16[512,2048]{1,0:T(8,128)(2,1)} %w_out.3, bf16[1024,1536]{1,0:T(8,128)(2,1)} %get-tuple-element.141.three, bf16[2048,1536]{1,0:T(8,128)(2,1)} %copy-done, ...), custom_call_target="tpu_custom_call" | custom-call | tf_op jit(solution)/shard_map/pallas_call | solution.py:1590
  528.8 0.8 reduce.1
  530.7 3.1 fusion.5
  534.6 3.8 convolution_convert_fusion.1
  538.3 9.0 %convolution_convert_fusion = bf16[1536,2048]{1,0:T(8,128)(2,1)} fusion(bf16[1024,1536]{1,0:T(8,128)(2,1)S(1)} %copy-done.26, bf16[1024,2048]{1,0:T(8,128)(2,1)S(1)} %copy-done.25), kind=kOutput, calls=%fused_computation | convolution fusion | flops 6445596672 | bytes 13631488 | tf_op jit(solution)/shard_map/dot_general | solution.py:25
  547.3 241.6 %shard_map.377 = (f32[2,1408,256]{2,1,0:T(8,128)}, f32[256,1408]{1,0:T(8,128)}, f32[256,1408]{1,0:T(8,128)}, f32[1408,256]{1,0:T(8,128)}, f32[512,256]{1,0:T(8,1...) custom-call(bf16[4,2,256,1408]{3,2,1,0:T(8,128)(2,1)} %bitcast.95, ...), custom_call_target="tpu_custom_call" | custom-call | tf_op jit(solution)/shard_map/pallas_call | solution.py:905
  788.9 1.4 dynamic-slice_bitcast_fusion.5
  790.4 1.4 dynamic-slice_bitcast_fusion.4
  791.8 3.2 maximum_convert_fusion
  795.0 3.2 maximum_convert_fusion.1
  798.2 1.0 copy.99
  799.2 1.3 copy.100
  800.5 0.8 copy.101
  801.3 0.8 copy.102
  802.1 0.8 copy.103
  802.9 0.8 copy.104
  803.7 1.1 copy.105
  804.8 1.1 copy.106
  805.9 1.1 copy.107
  807.0 1.6 copy.108
  (107 shorter events, 10.4 us)
Async XLA Ops:
  7.2 482.9 %reduce-scatter.5.cloned.1.call-start = ((), (), s32[]{:S(2)}) async-start(), calls=%async_computation.4 | async-start | bytes 6488064 | tf_op jit(solution)/shard_map/reduce_scatter | solution.py:1676
  10.1 70.9 %copy-start.22 = (bf16[512]{0:T(512)(128)(2,1)S(1)}, bf16[512]{0:T(512)(128)(2,1)}, u32[]{:S(2)}) copy-start(bf16[512]{0:T(512)(128)(2,1)} %param.33) | copy-start | bytes 3076
  10.1 70.9 %copy-start.23 = (bf16[512]{0:T(512)(128)(2,1)S(1)}, bf16[512]{0:T(512)(128)(2,1)}, u32[]{:S(2)}) copy-start(bf16[512]{0:T(512)(128)(2,1)} %param.34) | copy-start | bytes 3076
  10.1 70.9 %copy-start.24 = (bf16[512]{0:T(512)(128)(2,1)S(1)}, bf16[512]{0:T(512)(128)(2,1)}, u32[]{:S(2)}) copy-start(bf16[512]{0:T(512)(128)(2,1)} %param.35) | copy-start | bytes 3076
  10.8 1.2 copy-start.1
  12.1 1.6 copy-start.3
  13.7 1.6 copy-start.4
  15.2 1.6 copy-start.5
  74.6 2.6 copy-start
  77.3 2.0 copy-start.2
  133.5 95.1 %collective-permute-start = (bf16[1024,2048]{1,0:T(8,128)(2,1)}, bf16[1024,2048]{1,0:T(8,128)(2,1)}, u32[]{:S(2)}, u32[]{:S(2)}) collective-permute-start(bf16[1024,2048]{1,0:T(8,128)(2,1)} %bitcast.91), channel_id=1, source_target_pairs={{0,8},{4,12},{24,16},{28,20},{1,9},{5,13},{25,17},{29,21},{2,10},{... | collective-permute-start | bytes 12582920 | tf_op jit(solution)/shard_map/ppermute | solution.py:1659
  211.3 103.6 %collective-permute-start.1 = (bf16[1024,2048]{1,0:T(8,128)(2,1)}, bf16[1024,2048]{1,0:T(8,128)(2,1)}, u32[]{:S(2)}, u32[]{:S(2)}) collective-permute-start(bf16[1024,2048]{1,0:T(8,128)(2,1)} %bitcast.86), channel_id=1, source_target_pairs={{0,8},{4,12},{24,16},{28,20},{1,9},{5,13},{25,17},{29,21},{2,10},{... | collective-permute-start | bytes 12582920 | tf_op jit(solution)/shard_map/ppermute | solution.py:1659
  314.9 476.9 %reduce-scatter.7.cloned.1.call-start = ((), (), s32[]{:S(2)}) async-start(), calls=%async_computation.5 | async-start | bytes 6488064 | tf_op jit(solution)/shard_map/reduce_scatter | solution.py:1676
  315.7 3.3 copy-start.14
  315.7 3.7 copy-start.20
  315.7 4.2 copy-start.8
  315.7 476.1 %reduce-scatter.9.cloned.1.call-start = ((), (), s32[]{:S(2)}) async-start(), calls=%async_computation.6 | async-start | bytes 6488064 | tf_op jit(solution)/shard_map/reduce_scatter | solution.py:1676
  316.4 478.5 %reduce-scatter.11.cloned.1.call-start = ((), (), s32[]{:S(2)}) async-start(), calls=%async_computation.7 | async-start | bytes 6488064 | tf_op jit(solution)/shard_map/reduce_scatter | solution.py:1676
  490.3 39.3 %copy-start.21 = (f32[4,2048]{1,0:T(4,128)S(1)}, f32[4,2048]{1,0:T(4,128)}, u32[]{:S(2)}) copy-start(f32[4,2048]{1,0:T(4,128)} %get-tuple-element.148) | copy-start | bytes 98308
  490.3 40.0 %copy-start.15 = (f32[1024,1]{1,0:T(8,128)S(1)}, f32[1024,1]{1,0:T(8,128)}, u32[]{:S(2)}) copy-start(f32[1024,1]{1,0:T(8,128)} %get-tuple-element.149) | copy-start | bytes 12292
  528.8 5.7 copy-start.27
  530.7 3.9 copy-start.6
  534.6 3.8 copy-start.25
  534.6 3.8 copy-start.26
  791.8 6.4 copy-start.13
  794.9 4.2 copy-start.9
  798.2 2.3 copy-start.19
  798.2 3.1 copy-start.18
  798.2 3.9 copy-start.17
  799.2 3.7 copy-start.16
  799.2 4.5 copy-start.12
  800.5 4.3 copy-start.11
  801.3 4.6 copy-start.10
  803.7 3.3 copy-start.7
Sparse Core Ops, SparseCore 0:
  315.0 66.9 reduce-scatter.4
  384.4 63.1 reduce-scatter.6
  449.9 63.2 reduce-scatter.8
  515.3 80.4 reduce-scatter.10

commit v6 on v5

--- a/solution.py
+++ b/solution.py
@@ -857,9 +857,9 @@
             vec_out[...] = vec_sib[...] + vec_line[1]
 
     def loop(t, carry):
+        c.turn(t)
         a.turn(t)
         b.turn(t - a.chunks)
-        c.turn(t)
         side_work(t)
         return carry
 

time: 827 us -> 820 us (level)
  no operation moved by 1% of the time
where the time goes in v6:
time: 820 us; the launch traced here: 809 us
  Pallas kernels  719 us (88%)
  local copies, waits for them, and re-layouts  31.2 us (4%)
  other arithmetic  17.8 us (2%)
  matrix products  16.6 us (2%)
  between operations  14.4 us (2%)
    pallas_call x1, Pallas kernels, line_call(): pl.pallas_call(functools.partial(line_kernel, m, s, parts, shift), out_sh...  235 us
    pallas_call x2, Pallas kernels, mid_call(): pl.pallas_call(functools.partial(mid_kernel, middle, chunks, gathers, len...  160 us
    pallas_call x1, Pallas kernels, shared_call(): pl.pallas_call(functools.partial(shared_kernel, blocks, bool(others)), gr...  81.8 us
    pallas_call x1, Pallas kernels, expert_call(): pl.pallas_call(expert_kernel, grid=(experts, steps), in_specs=[slot_spec(...  59.5 us
    pallas_call x1, Pallas kernels, start_call(): pl.pallas_call(start_kernel, out_shape=(jax.ShapeDtypeStruct((4,) + token...  57.8 us
    pallas_call x1, Pallas kernels, attend_call(): pl.pallas_call(attend_kernel, in_specs=in_specs, out_specs=out_specs, out...  48.1 us
    pallas_call x1, Pallas kernels, attend_back_call(): pl.pallas_call(attend_back_kernel, in_specs=[VMEM] * 8, out_specs=(VMEM,)...  38.5 us
    pallas_call x3, Pallas kernels, outer_call(): pl.pallas_call(outer_kernel, grid=(features // tile,), in_specs=[pl.Block...  26.2 us
  transfers between devices with their start and end apart: 6, of which 1 were waited for; matrix products, arithmetic and copies ran while one was open for 4% of the time, Pallas kernels for 76%

profile of v6, /device:TPU:0, one launch (start us, length us, event | category | flops | bytes accessed | tf_op | source)
XLA Modules:
  0.0 808.5 jit_solution(7454367279939610427)
XLA Ops:
  7.3 0.7 broadcast_in_dim.94
  9.3 0.7 pad_add_fusion.1
  10.1 0.7 fusion.19.small
  10.8 1.2 copy-done.1
  12.1 1.6 copy-done.3
  13.7 1.6 copy-done.4
  15.2 1.6 copy-done.5
  16.8 57.8 %shard_map.366 = (bf16[4,256,2048]{2,1,0:T(8,128)(2,1)S(1)}, bf16[4,16,512]{2,1,0:T(8,128)(2,1)S(1)}, s32[4,16,256]{2,1,0:T(8,128)S(1)}, bf16[2048,1536]{1,0:T(8,128)(2,1)S(1)}, bf16[2,3,64,512]{3,2,1,0:T(8,128)(2,1)}) custom-call(bf16[256,2048]{1,0:T(8,128)(2,1)S(1)} %copy-done.1, bf16[16,512]{1,0:T(8,128)(2,1)S(1)} %fusion.19.small, ...), custom_call_target="tpu_custom_call" | custom-call | tf_op jit(solution)/shard_map/pallas_call | solution.py:1373
  74.6 2.6 copy-done
  77.3 1.9 copy-done.2
  79.9 1.0 copy.72.mark_cols
  81.6 3.0 fusion.2
  85.3 48.1 %shard_map.367 = (bf16[1024,2048]{1,0:T(8,128)(2,1)}, bf16[1024,1536]{1,0:T(8,128)(2,1)}, bf16[1024,512]{1,0:T(8,128)(2,1)}, bf16[1024,2048]{1,0:T(8,128)(2,1)}, bf16[4,256,2048]{2,1,0:T(8,128)(2,1)}) custom-call(bf16[1024,2048]{1,0:T(8,128)(2,1)} %bitcast.85, f32[1,2048]{1,0:T(1,128)} %get-tuple-element.171.gain.refs_13_, bf16[2048,1536]{1,0:T(8,128)(2,1)} %copy-done, ...), custom_call_target="tpu_custom_call" | custom-call | tf_op jit(solution)/shard_map/pallas_call | solution.py:1524
  133.5 4.3 collective-permute-start
  137.7 73.6 %shard_map.368 = (f32[256,2048]{1,0:T(8,128)}, bf16[4,256,2048]{2,1,0:T(8,128)(2,1)}) custom-call(bf16[4,256,2048]{2,1,0:T(8,128)(2,1)} %bitcast.104, bf16[256,2048]{1,0:T(8,128)(2,1)} %refs_10_.3, f32[1,2048]{1,0:T(1,128)} %get-tuple-element.170.refs_2_), custom_call_target="tpu_custom_call" | custom-call | tf_op jit(solution)/shard_map/pallas_call | solution.py:1199
  211.3 3.3 collective-permute-start.1
  214.6 0.8 slice.109
  216.2 0.8 fusion.1.slot_ref
  217.0 11.5 %shard_map.369 = (bf16[4,2,160,2048]{3,2,1,0:T(8,128)(2,1)}, bf16[4,2,160,2048]{3,2,1,0:T(8,128)(2,1)}, f32[4,2,160,1]{3,2,1,0:T(8,128)}, bf16[4,320,256]{2,1,0:...) custom-call(bf16[1024,2048]{1,0:T(8,128)(2,1)} %bitcast.87, bf16[1024,2048]{1,0:T(8,128)(2,1)} %bitcast.92, ...), custom_call_target="tpu_custom_call" | custom-call | tf_op jit(solution)/shard_map/pallas_call | solution.py:265
  228.6 59.5 %shard_map.370 = (bf16[2,640,1408]{2,1,0:T(8,128)(2,1)}, bf16[2,640,1408]{2,1,0:T(8,128)(2,1)}, bf16[2,640,1408]{2,1,0:T(8,128)(2,1)}, bf16[4,2,160,2048]{3,2,1,...) custom-call(bf16[4,2,160,2048]{3,2,1,0:T(8,128)(2,1)} %get-tuple-ele, ...), custom_call_target="tpu_custom_call" | custom-call | tf_op jit(solution)/shard_map/pallas_call | solution.py:101
  288.1 8.8 %shard_map.371 = bf16[2048,1408]{1,0:T(8,128)(2,1)} custom-call(bf16[4,2,160,2048]{3,2,1,0:T(8,128)(2,1)} %get-tuple-element.101.x_ref.a_ref.refs_4_, bf16[2,640,1408]{2,1,0:T(8,128)(2,1)} %get-tuple-element.105.b_ref), custom_call_target="tpu_custom_call" | custom-call | tf_op jit(solution)/shard_map/pallas_call | solution.py:302
  296.8 8.7 %shard_map.372 = bf16[2048,1408]{1,0:T(8,128)(2,1)} custom-call(bf16[4,2,160,2048]{3,2,1,0:T(8,128)(2,1)} %get-tuple-element.101.x_ref.a_ref.refs_4_, bf16[2,640,1408]{2,1,0:T(8,128)(2,1)} %get-tuple-element.105.b_ref), custom_call_target="tpu_custom_call" | custom-call | tf_op jit(solution)/shard_map/pallas_call | solution.py:302
  305.6 8.7 %shard_map.373 = bf16[2048,1408]{1,0:T(8,128)(2,1)} custom-call(bf16[4,2,160,2048]{3,2,1,0:T(8,128)(2,1)} %get-tuple-element.101.x_ref.a_ref.refs_4_, bf16[2,640,1408]{2,1,0:T(8,128)(2,1)} %get-tuple-element.106.b_ref.refs_5_), custom_call_target="tpu_custom_call" | custom-call | tf_op jit(solution)/shard_map/pallas_call | solution.py:302
  314.9 0.7 reduce-scatter.7.cloned.1.call-update
  317.1 1.3 iota_compare_fusion.3
  320.5 0.9 pad_maximum_fusion.refs_6_
  321.4 81.8 %shard_map.374 = (bf16[1024,1408]{1,0:T(8,128)(2,1)}, bf16[1024,1408]{1,0:T(8,128)(2,1)}, bf16[1024,1408]{1,0:T(8,128)(2,1)}, bf16[1024,2048]{1,0:T(8,128)(2,1)}...) custom-call(bf16[1024,2048]{1,0:T(8,128)(2,1)} %bitcast.88, ...), custom_call_target="tpu_custom_call" | custom-call | tf_op jit(solution)/shard_map/pallas_call | solution.py:215
  403.2 86.9 %shard_map.375 = (f32[256,2048]{1,0:T(8,128)}, f32[4,2048]{1,0:T(4,128)}, bf16[4,256,2048]{2,1,0:T(8,128)(2,1)}, bf16[2048,1408]{1,0:T(8,128)(2,1)}, bf16[2048,1...) custom-call(bf16[4,256,2048]{2,1,0:T(8,128)(2,1)} %bitcast.107, ...), custom_call_target="tpu_custom_call" | custom-call | tf_op jit(solution)/shard_map/pallas_call | solution.py:1199
  490.3 38.5 %shard_map.376 = (bf16[1024,1536]{1,0:T(8,128)(2,1)}, bf16[1024,2048]{1,0:T(8,128)(2,1)}, f32[1,1536]{1,0:T(1,128)}) custom-call(bf16[1024,2048]{1,0:T(8,128)(2,1)} %bitcast.105, bf16[512,2048]{1,0:T(8,128)(2,1)} %w_out.3, bf16[1024,1536]{1,0:T(8,128)(2,1)} %get-tuple-element.141.three, bf16[2048,1536]{1,0:T(8,128)(2,1)} %copy-done, ...), custom_call_target="tpu_custom_call" | custom-call | tf_op jit(solution)/shard_map/pallas_call | solution.py:1590
  528.8 0.8 reduce.1
  530.7 3.1 fusion.5
  534.6 3.8 convolution_convert_fusion.1
  538.3 9.0 %convolution_convert_fusion = bf16[1536,2048]{1,0:T(8,128)(2,1)} fusion(bf16[1024,1536]{1,0:T(8,128)(2,1)S(1)} %copy-done.26, bf16[1024,2048]{1,0:T(8,128)(2,1)S(1)} %copy-done.25), kind=kOutput, calls=%fused_computation | convolution fusion | flops 6445596672 | bytes 13631488 | tf_op jit(solution)/shard_map/dot_general | solution.py:25
  547.3 234.8 %shard_map.377 = (f32[2,1408,256]{2,1,0:T(8,128)}, f32[256,1408]{1,0:T(8,128)}, f32[256,1408]{1,0:T(8,128)}, f32[1408,256]{1,0:T(8,128)}, f32[512,256]{1,0:T(8,1...) custom-call(bf16[4,2,256,1408]{3,2,1,0:T(8,128)(2,1)} %bitcast.95, ...), custom_call_target="tpu_custom_call" | custom-call | tf_op jit(solution)/shard_map/pallas_call | solution.py:905
  782.1 1.4 dynamic-slice_bitcast_fusion.5
  783.6 1.4 dynamic-slice_bitcast_fusion.4
  785.0 3.2 maximum_convert_fusion
  788.2 3.2 maximum_convert_fusion.1
  791.4 1.0 copy.99
  792.4 1.3 copy.100
  793.7 0.8 copy.101
  794.5 0.8 copy.102
  795.3 0.8 copy.103
  796.1 0.8 copy.104
  796.9 1.1 copy.105
  798.0 1.1 copy.106
  799.1 1.1 copy.107
  800.2 1.6 copy.108
  (107 shorter events, 10.4 us)
Async XLA Ops:
  7.2 482.9 %reduce-scatter.5.cloned.1.call-start = ((), (), s32[]{:S(2)}) async-start(), calls=%async_computation.4 | async-start | bytes 6488064 | tf_op jit(solution)/shard_map/reduce_scatter | solution.py:1676
  10.1 70.9 %copy-start.22 = (bf16[512]{0:T(512)(128)(2,1)S(1)}, bf16[512]{0:T(512)(128)(2,1)}, u32[]{:S(2)}) copy-start(bf16[512]{0:T(512)(128)(2,1)} %param.33) | copy-start | bytes 3076
  10.1 70.9 %copy-start.23 = (bf16[512]{0:T(512)(128)(2,1)S(1)}, bf16[512]{0:T(512)(128)(2,1)}, u32[]{:S(2)}) copy-start(bf16[512]{0:T(512)(128)(2,1)} %param.34) | copy-start | bytes 3076
  10.1 70.9 %copy-start.24 = (bf16[512]{0:T(512)(128)(2,1)S(1)}, bf16[512]{0:T(512)(128)(2,1)}, u32[]{:S(2)}) copy-start(bf16[512]{0:T(512)(128)(2,1)} %param.35) | copy-start | bytes 3076
  10.8 1.2 copy-start.1
  12.1 1.6 copy-start.3
  13.7 1.6 copy-start.4
  15.2 1.6 copy-start.5
  74.6 2.6 copy-start
  77.3 2.0 copy-start.2
  133.5 95.1 %collective-permute-start = (bf16[1024,2048]{1,0:T(8,128)(2,1)}, bf16[1024,2048]{1,0:T(8,128)(2,1)}, u32[]{:S(2)}, u32[]{:S(2)}) collective-permute-start(bf16[1024,2048]{1,0:T(8,128)(2,1)} %bitcast.91), channel_id=1, source_target_pairs={{0,8},{4,12},{24,16},{28,20},{1,9},{5,13},{25,17},{29,21},{2,10},{... | collective-permute-start | bytes 12582920 | tf_op jit(solution)/shard_map/ppermute | solution.py:1659
  211.3 103.6 %collective-permute-start.1 = (bf16[1024,2048]{1,0:T(8,128)(2,1)}, bf16[1024,2048]{1,0:T(8,128)(2,1)}, u32[]{:S(2)}, u32[]{:S(2)}) collective-permute-start(bf16[1024,2048]{1,0:T(8,128)(2,1)} %bitcast.86), channel_id=1, source_target_pairs={{0,8},{4,12},{24,16},{28,20},{1,9},{5,13},{25,17},{29,21},{2,10},{... | collective-permute-start | bytes 12582920 | tf_op jit(solution)/shard_map/ppermute | solution.py:1659
  314.9 470.1 %reduce-scatter.7.cloned.1.call-start = ((), (), s32[]{:S(2)}) async-start(), calls=%async_computation.5 | async-start | bytes 6488064 | tf_op jit(solution)/shard_map/reduce_scatter | solution.py:1676
  315.7 3.3 copy-start.14
  315.7 3.7 copy-start.20
  315.7 4.2 copy-start.8
  315.7 469.3 %reduce-scatter.9.cloned.1.call-start = ((), (), s32[]{:S(2)}) async-start(), calls=%async_computation.6 | async-start | bytes 6488064 | tf_op jit(solution)/shard_map/reduce_scatter | solution.py:1676
  316.4 471.7 %reduce-scatter.11.cloned.1.call-start = ((), (), s32[]{:S(2)}) async-start(), calls=%async_computation.7 | async-start | bytes 6488064 | tf_op jit(solution)/shard_map/reduce_scatter | solution.py:1676
  490.3 39.3 %copy-start.21 = (f32[4,2048]{1,0:T(4,128)S(1)}, f32[4,2048]{1,0:T(4,128)}, u32[]{:S(2)}) copy-start(f32[4,2048]{1,0:T(4,128)} %get-tuple-element.148) | copy-start | bytes 98308
  490.3 40.0 %copy-start.15 = (f32[1024,1]{1,0:T(8,128)S(1)}, f32[1024,1]{1,0:T(8,128)}, u32[]{:S(2)}) copy-start(f32[1024,1]{1,0:T(8,128)} %get-tuple-element.149) | copy-start | bytes 12292
  528.8 5.7 copy-start.27
  530.7 3.9 copy-start.6
  534.6 3.8 copy-start.25
  534.6 3.8 copy-start.26
  785.0 6.4 copy-start.13
  788.1 4.2 copy-start.9
  791.4 2.3 copy-start.19
  791.4 3.1 copy-start.18
  791.4 3.9 copy-start.17
  792.4 3.7 copy-start.16
  792.4 4.5 copy-start.12
  793.7 4.3 copy-start.11
  794.5 4.6 copy-start.10
  796.9 3.3 copy-start.7
Sparse Core Ops, SparseCore 0:
  315.0 66.9 reduce-scatter.4
  384.4 63.1 reduce-scatter.6
  449.9 63.2 reduce-scatter.8
  515.3 80.4 reduce-scatter.10
